TPU v7x, 32 devices: a whole 2x2x4 slice. The times are simulated.
32 devices in a mesh: space: 8 (over y, x, core), modes: 4 (over z).
Axes of the slice: x: 2, y: 2, z: 4, core: 2. Of those that a mesh axis runs over, the one named last changes fastest.
Arguments:
- voltage_expansion: float32 [220, 8, 2048], P('modes', 'space'), may hold values from -6 to 6
- current_injection: float32 [220, 8, 2048], P('modes', 'space'), may hold values from -48 to 48
- thermal_state: float32 [220, 8, 2048], P('modes', 'space'), may hold values from -6 to 6
- average_electric_transport: float32 [8, 2048], P('space'), may hold values from 0.5 to 4
- material_zone: int32 [8, 2048], P('space'), may hold values from 0 to 3
- zone_relative_response: float32 [4, 9], replicated, may hold values from 0.02 to 0.12
- polynomial_exponent_rows: int32 [220, 9], replicated, may hold values from 0 to 3, as said below
- quadrature_abscissa_choice: int32 [512, 9], replicated, may hold values from 0 to 4
- quadrature_integer_share: int32 [512], replicated, may hold values from 1 to 1024
Outputs:
- relaxed_voltage: float32 [220, 8, 2048], P('modes', 'space')
- advanced_thermal_state: float32 [220, 8, 2048], P('modes', 'space')
Inputs may be any that keep to these rules, and one draw needn't show every extreme that they name: `polynomial_exponent_rows`: the rows are the 220 multi-indices of total degree at most 3 over 9 parameters, each once.
All inputs are finite; a program needn't handle non-finite values.
Results may differ from a plain program's by a relative error of at most 0.0003.
Values sent between devices are 32-bit elements; how exact they have to be, the bound alone decides.
No kernel may reach another device: no remote copies, remote signals or barrier semaphores. Data moves between devices by JAX's collectives and lax.ppermute only.
A program may use at most 64 MiB of HBM per device.

v0:
```python
import jax
import jax.numpy as jnp
from jax import lax
from jax.sharding import PartitionSpec as P

NY = 256
NZ = 8


HERMITE_NODES = (
    0.0,
    1.355626179974266,
    -1.355626179974266,
    2.8569700138728056,
    -2.8569700138728056,
)


def padded_2(block, sides, width):
    for axis, dim in sides:
        count = lax.axis_size(axis)
        forward = [(i, i + 1) for i in range(count - 1)]
        backward = [(target, source) for source, target in forward]
        low = lax.ppermute(
            lax.slice_in_dim(block, block.shape[dim] - width, None, axis=dim), axis, forward
        )
        high = lax.ppermute(lax.slice_in_dim(block, 0, width, axis=dim), axis, backward)
        block = jnp.concatenate([low, block, high], axis=dim)
    return block


def from_behind(block, axis, distance):
    devices = range(lax.axis_size(axis))
    route = [(i - distance, i) for i in devices if i - distance in devices]
    return lax.ppermute(block, axis, route)


def neighbours(field):
    column_ids = jnp.arange(field.shape[-1])
    depth_pos = column_ids % NZ
    row_pos = column_ids // NZ
    z_next = jnp.where(depth_pos < NZ - 1, jnp.roll(field, -1, -1), 0.0)
    z_prev = jnp.where(depth_pos > 0, jnp.roll(field, 1, -1), 0.0)
    y_next = jnp.where(row_pos < NY - 1, jnp.roll(field, -NZ, -1), 0.0)
    y_prev = jnp.where(row_pos > 0, jnp.roll(field, NZ, -1), 0.0)
    return (z_next, z_prev, y_next, y_prev)


def diffusion_operator_weights(padded):
    center = padded[..., 1:-1, :]
    z_next, z_prev, y_next, y_prev = neighbours(center)
    return (
        6.0 * center - padded[..., 2:, :] - padded[..., :-2, :] - z_next - z_prev - y_next - y_prev
    )


def coupling(row_table, col_table):
    offsets = row_table[:, None, :] - col_table[None, :, :]
    differ_count = jnp.sum((offsets != 0).astype(jnp.int32), axis=2)
    layers = [jnp.where(differ_count == 0, 1.0, 0.0).astype(jnp.float32)]
    for which_param in range(row_table.shape[1]):
        larger = jnp.maximum(
            row_table[:, None, which_param], col_table[None, :, which_param]
        ).astype(jnp.float32)
        linked = (jnp.abs(offsets[:, :, which_param]) == 1) & (differ_count == 1)
        layers.append(jnp.where(linked, jnp.sqrt(larger), 0.0))
    return jnp.stack(layers)


def node_values(quadrature_abscissa_choice):
    node_vals = jnp.zeros(quadrature_abscissa_choice.shape, jnp.float32)
    for which_node in range(5):
        node_vals = node_vals + jnp.where(
            quadrature_abscissa_choice == which_node, HERMITE_NODES[which_node], 0.0
        )
    return node_vals


def basis_values(polynomial_exponent_rows, node_vals):
    poly_terms = [
        jnp.ones_like(node_vals),
        node_vals,
        (node_vals * node_vals - 1.0) / jnp.sqrt(2.0),
        (node_vals * node_vals * node_vals - 3.0 * node_vals) / jnp.sqrt(6.0),
    ]
    basis_vals = jnp.ones((node_vals.shape[0], polynomial_exponent_rows.shape[0]), jnp.float32)
    for which_param in range(polynomial_exponent_rows.shape[1]):
        degree = polynomial_exponent_rows[:, which_param]
        factor = jnp.zeros_like(basis_vals)
        for which_deg in range(4):
            factor = factor + jnp.where(
                degree[None, :] == which_deg, poly_terms[which_deg][:, which_param][:, None], 0.0
            )
        basis_vals = basis_vals * factor
    return basis_vals


def on_device(
    voltage_expansion,
    current_injection,
    thermal_state,
    average_electric_transport,
    material_zone,
    zone_relative_response,
    polynomial_exponent_rows,
    quadrature_abscissa_choice,
    quadrature_integer_share,
):
    hp = lax.Precision.HIGHEST
    modes_here = voltage_expansion.shape[0]
    planes = voltage_expansion.shape[1]
    columns = voltage_expansion.shape[2]
    cell_count = planes * columns
    nreg = zone_relative_response.shape[0]
    all_modes = polynomial_exponent_rows.shape[0]
    num_points = quadrature_integer_share.shape[0]
    first_mode = lax.axis_index("modes") * modes_here
    own_table = lax.dynamic_slice_in_dim(polynomial_exponent_rows, first_mode, modes_here, 0)
    bordered_quantities = padded_2(
        jnp.stack([voltage_expansion, thermal_state]), (("space", 2),), 1
    )
    pot_padded = bordered_quantities[0]
    thermal_state_bordered = bordered_quantities[1]
    sens_cell = jnp.zeros((zone_relative_response.shape[1],) + material_zone.shape, jnp.float32)
    for which_region in range(nreg):
        sens_cell = sens_cell + jnp.where(
            material_zone[None] == which_region,
            zone_relative_response[which_region][:, None, None],
            0.0,
        )
    coeff = (
        jnp.concatenate([jnp.ones((1,) + material_zone.shape, jnp.float32), sens_cell])
        * average_electric_transport
    )
    coeff_flat = coeff.reshape(coeff.shape[0], cell_count)
    flat_rough = diffusion_operator_weights(pot_padded).reshape(modes_here, cell_count)
    row_coup = coupling(own_table, polynomial_exponent_rows)
    mixed = jnp.einsum(
        "mij,jc->mic",
        row_coup,
        lax.all_gather(flat_rough, "modes", axis=0, tiled=True),
        precision=hp,
    )
    applied = jnp.sum(coeff_flat[:, None, :] * mixed, axis=0)
    applied = applied.reshape(modes_here, planes, columns)
    relaxed_voltage = voltage_expansion + 0.8 * (current_injection - applied) / (
        6.0 * average_electric_transport
    )
    node_vals = node_values(quadrature_abscissa_choice)
    basis_vals = basis_values(polynomial_exponent_rows, node_vals)
    field_quarter = lax.all_to_all(
        relaxed_voltage, "modes", split_axis=2, concat_axis=0, tiled=True
    )
    quarter_padded = padded_2(field_quarter, (("space", 1),), 1)
    rim_lower = from_behind(field_quarter[..., -NZ:], "modes", 1)
    rim_upper = from_behind(field_quarter[..., :NZ], "modes", -1)
    widened_field = jnp.concatenate([rim_lower, field_quarter, rim_upper], axis=2)
    along_x = (quarter_padded[:, 2:, :] - quarter_padded[:, :-2, :]) * 0.5
    along_y = (widened_field[..., 2 * NZ :] - widened_field[..., : -2 * NZ]) * 0.5
    depth_pos = jnp.arange(field_quarter.shape[-1]) % NZ
    z_next = jnp.where(depth_pos < NZ - 1, jnp.roll(field_quarter, -1, -1), 0.0)
    z_prev = jnp.where(depth_pos > 0, jnp.roll(field_quarter, 1, -1), 0.0)
    along_z = (z_next - z_prev) * 0.5
    quarter_grads = jnp.stack([along_x, along_y, along_z])
    point_grads = jnp.einsum("qi,kixn->kqxn", basis_vals, quarter_grads, precision=hp)
    quarter = columns // lax.axis_size("modes")
    offset = lax.axis_index("modes") * quarter
    cond_part = lax.dynamic_slice_in_dim(average_electric_transport, offset, quarter, 1)
    region_part = lax.dynamic_slice_in_dim(material_zone, offset, quarter, 1)
    cond_lift = 1.0 + jnp.dot(zone_relative_response, node_vals.T, precision=hp)
    spread = jnp.zeros((num_points, planes, quarter), jnp.float32)
    for which_region in range(nreg):
        spread = spread + jnp.where(
            region_part[None] == which_region, cond_lift[which_region][:, None, None], 0.0
        )
    joule_heat = cond_part * spread * jnp.sum(point_grads * point_grads, axis=0)
    weighted = (
        basis_vals.T
        * quadrature_integer_share[None, :].astype(jnp.float32)
        / (512.0 * num_points * all_modes)
    )
    heat_points = jnp.einsum("iq,qxn->ixn", weighted, joule_heat, precision=hp)
    thermal_expansion_terms = lax.all_to_all(
        heat_points, "modes", split_axis=0, concat_axis=2, tiled=True
    )
    advanced_thermal_state = thermal_state + 0.1 * (
        thermal_expansion_terms - 1.5 * diffusion_operator_weights(thermal_state_bordered)
    )
    return (relaxed_voltage, advanced_thermal_state)


def solution(mesh):
    in_specs = (
        P("modes", "space", None),
        P("modes", "space", None),
        P("modes", "space", None),
        P("space", None),
        P("space", None),
        P(),
        P(),
        P(),
        P(),
    )
    out_specs = (P("modes", "space", None), P("modes", "space", None))
    return jax.shard_map(
        on_device, mesh=mesh, in_specs=in_specs, out_specs=out_specs, check_vma=False
    )
```

profile of v0, /device:TPU:0, one launch (start us, length us, event | category | flops | bytes accessed | tf_op | source)
XLA Modules:
  0.0 187.2 jit_solution(11540672541500268416)
XLA Ops:
  7.2 1.4 copy_bitcast_fusion
  9.5 3.3 %collective-permute-start = (f32[2,55,1,2048]{3,0,2,1:T(2,128)S(1)}, f32[2,55,1,2048]{3,0,2,1:T(2,128)}, u32[]{:S(2)}, u32[]{:S(2)}) collective-permute-start(f32[2,55,1,2048]{3,0,2,1:T(2,128)S(1)} %copy.48), channel_id=1, source_target_pairs={{0,4},{4,8},{8,12},{12,16},{16,20},{20,24},{24,28},{1,5},{5,9},{9,... | collective-permute-start | bytes 2703368 | tf_op jit(solution)/shard_map/ppermute | solution.py:24
  24.2 1.7 copy.50
  25.9 1.7 copy.51
  32.3 49.1 %all-gather.3.cloned.1.call-done = f32[220,1,2048]{2,1,0:T(1,128)} async-done(((f32[55,1,2048]{2,1,0:T(1,128)}), f32[220,1,2048]{2,1,0:T(1,128)}) %all-gather.3.cloned.1.call-update) | async-done | bytes 1802256 | tf_op jit(solution)/shard_map/all_gather | solution.py:141
  81.4 6.0 %multiply_reduce_fusion = f32[55,2048]{1,0:T(8,128)S(1)} fusion(f32[10,55,220]{2,1,0:T(8,128)} %copy-done.9, f32[10,2048]{1,0:T(8,128)S(1)} %multiply_bitcast_fusion.1, f32[220,1,2048]{2,1,0:T(1,128)} %all-gather.3.cloned.1.call-done), kind=kOutput, calls=%fused_computation | convolution fusion | flops 2975836160 | bytes 2818720 | tf_op jit(solution)/shard_map/mij,jc->mic/dot_general | solution.py:138
  89.1 9.3 %reduce.20 = f32[2048,55]{1,0:T(8,128)S(1)} reduce(f32[2048,1,55]{2,1,0:T(1,128)S(1)} %bitcast.194, f32[]{:T(128)} %broadcast.1491), dimensions={1}, to_apply=%bitcast.190.reduce_sub_computation | reduce | bytes 901124
  98.5 2.1 %reshape.1981 = f32[4,1,28160]{2,1,0:T(1,128)} reshape(f32[2048,55]{1,0:T(8,128)S(1)} %reduce.20) | data formatting | bytes 901120
  100.5 3.5 %all-to-all-start = ((f32[4,1,28160]{2,1,0:T(1,128)}), f32[4,1,28160]{2,1,0:T(1,128)S(1)}, u32[]{:S(2)}, u32[]{:S(2)}) async-start(f32[4,1,28160]{2,1,0:T(1,128)} %reshape.1981), calls=%async_computation | async-start | bytes 901120 | tf_op jit(solution)/shard_map/all_to_all | solution.py:151
  104.3 12.9 %all-to-all-done = f32[4,1,28160]{2,1,0:T(1,128)S(1)} async-done(((f32[4,1,28160]{2,1,0:T(1,128)}), f32[4,1,28160]{2,1,0:T(1,128)S(1)}, u32[]{:S(2)}, u32[]{:S(2)}) %all-to-all-start) | async-done | bytes 450592 | tf_op jit(solution)/shard_map/all_to_all | solution.py:151
  117.2 2.7 %reduce.21 = f32[4,28160]{1,0:T(4,128)} reduce(f32[4,1,28160]{2,1,0:T(1,128)S(1)} %all-to-all-done, f32[]{:T(128)} %broadcast.1491), dimensions={1}, to_apply=%all_to_all.26.reduce_sub_computation | reduce | bytes 901124 | tf_op jit(solution)/shard_map/all_to_all | solution.py:151
  119.8 3.1 %reshape.1982 = f32[2048,1,55]{2,1,0:T(1,128)S(1)} reshape(f32[4,28160]{1,0:T(4,128)} %reduce.21) | data formatting | bytes 901120
  126.6 3.1 %collective-permute-start.3 = (f32[220,1,512]{2,0,1:T(8,128)S(1)}, f32[220,1,512]{2,0,1:T(8,128)S(1)}, u32[]{:S(2)}, u32[]{:S(2)}) collective-permute-start(f32[220,1,512]{2,0,1:T(8,128)S(1)} %all_to_all.29), channel_id=1, source_target_pairs={{0,4},{4,8},{8,12},{12,16},{16,20},{20,24},{24,28},{1,5},{5,9},{9,... | collective-permute-start | bytes 1351688 | tf_op jit(solution)/shard_map/ppermute | solution.py:24
  131.4 4.8 %collective-permute-start.5 = (f32[220,1,8]{2,0,1:T(8,128)S(1)}, f32[220,1,8]{2,0,1:T(8,128)S(1)}, u32[]{:S(2)}, u32[]{:S(2)}) collective-permute-start(f32[220,1,8]{2,0,1:T(8,128)S(1)} %get-tuple-element.41), channel_id=1, source_target_pairs={{0,1},{1,2},{2,3},{4,5},{5,6},{6,7},{8,9},{9,10},{10,11},{12,13},{... | collective-permute-start | bytes 21128 | tf_op jit(solution)/shard_map/ppermute | solution.py:35
  137.9 1.4 collective-permute-done.5
  140.1 5.6 %multiply_reduce_fusion.1 = f32[512,512]{1,0:T(8,128)S(1)} fusion(f32[1,220,1,512]{3,1,0,2:T(8,128)S(1)} %fusion.41, f32[1,220,1,512]{3,1,0,2:T(8,128)S(1)} %fusion.35, f32[1,220,1,512]{3,1,0,2:T(8,128)S(1)} %multiply_bitcast_fusion, f32[512]{0:T(512)S(1)} %bitcast.229, f32[512]{0:T(512)S(1)} %bitcast.277, f32[512]{0:T(512)S(1)} %bitcast.257, ...), kind=kOutput, calls=%fused_computation.1 | convolution fusion | flops 2085150720 | bytes 2469412 | tf_op jit(solution)/shard_map/qi,kixn->kqxn/dot_general | solution.py:165
  145.8 3.9 %convolution_bitcast_fusion = f32[220,1,512]{2,0,1:T(8,128)S(1)} fusion(f32[512,512]{1,0:T(8,128)S(1)} %multiply_reduce_fusion.1, f32[512]{0:T(512)S(1)} %bitcast.283, f32[512]{0:T(512)S(1)} %bitcast.284, f32[512]{0:T(512)S(1)} %bitcast.285, f32[512]{0:T(512)S(1)} %bitcast.282, f32[512]{0:T(512)S(1)} %bitcast.281, pred[512]{0:T(512)(128)(4,1)} %get-tuple-element.15, ...), kind=kOutput, calls=%fused_computation.12 | convolution fusion | flops 701628416 | bytes 1582628 | tf_op jit(solution)/shard_map/iq,qxn->ixn/dot_general | solution.py:182
  150.9 4.5 %all-to-all-start.1 = ((f32[220,1,512]{2,1,0:T(1,128)}), f32[220,1,512]{2,1,0:T(1,128)}, u32[]{:S(2)}, u32[]{:S(2)}) async-start(f32[220,1,512]{2,1,0:T(1,128)} %copy.59), calls=%async_computation.1 | async-start | bytes 901120 | tf_op jit(solution)/shard_map/all_to_all | solution.py:183
  157.7 10.8 %all-to-all-done.1 = f32[220,1,512]{2,1,0:T(1,128)} async-done(((f32[220,1,512]{2,1,0:T(1,128)}), f32[220,1,512]{2,1,0:T(1,128)}, u32[]{:S(2)}, u32[]{:S(2)}) %all-to-all-start.1) | async-done | bytes 450592 | tf_op jit(solution)/shard_map/all_to_all | solution.py:183
  168.5 2.9 %reduce.11 = f32[220,512]{1,0:T(8,128)} reduce(f32[220,1,512]{2,1,0:T(1,128)} %all-to-all-done.1, f32[]{:T(128)} %constant.141), dimensions={1}, to_apply=%all_to_all.30.reduce_sub_computation | reduce | bytes 901124 | tf_op jit(solution)/shard_map/all_to_all | solution.py:183
  171.3 1.9 %all_to_all.31 = f32[4,55,1,512]{3,1,0,2:T(8,128)} reshape(f32[220,512]{1,0:T(8,128)} %reduce.11) | data formatting | bytes 901120 | tf_op jit(solution)/shard_map/all_to_all | solution.py:183
  173.3 2.1 %copy.60 = f32[55,1,4,512]{3,2,0,1:T(4,128)} copy(f32[55,1,4,512]{3,0,2,1:T(8,128)} %bitcast.196) | data formatting | bytes 901120 | tf_op jit(solution)/shard_map/all_to_all | solution.py:183
  175.3 2.1 %all_to_all.33 = f32[55,1,2048]{2,0,1:T(8,128)} reshape(f32[55,1,4,512]{3,2,0,1:T(4,128)} %copy.60) | data formatting | bytes 901120 | tf_op jit(solution)/shard_map/all_to_all | solution.py:183
  177.4 1.7 fusion.32
  (187 shorter events, 30.7 us)
Async XLA Ops:
  7.2 74.3 %all-gather.3.cloned.1.call-start = ((), (), s32[]{:S(2)}) async-start(), calls=%async_computation.2 | async-start | bytes 2252800 | tf_op jit(solution)/shard_map/all_gather | solution.py:141
  8.7 6.1 %copy-start.5 = (s32[220,9]{0,1:T(8,128)S(1)}, s32[220,9]{0,1:T(8,128)}, u32[]{:S(2)}) copy-start(s32[220,9]{0,1:T(8,128)} %param.15) | copy-start | bytes 23764
  8.7 10.7 %copy-start.24 = (f32[4,9]{1,0:T(4,128)S(1)}, f32[4,9]{1,0:T(4,128)}, u32[]{:S(2)}) copy-start(f32[4,9]{1,0:T(4,128)} %param.14) | copy-start | bytes 436
  8.8 10.7 %copy-start.7 = (s32[512,9]{0,1:T(8,128)S(1)}, s32[512,9]{0,1:T(8,128)}, u32[]{:S(2)}) copy-start(s32[512,9]{0,1:T(8,128)} %param.16) | copy-start | bytes 55300
  8.8 11.1 %copy-start.8 = (s32[1,2048]{1,0:T(1,128)S(1)}, s32[1,2048]{1,0:T(1,128)}, u32[]{:S(2)}) copy-start(s32[1,2048]{1,0:T(1,128)} %param.13) | copy-start | bytes 24580
  8.8 11.9 %copy-start.6 = (f32[1,2048]{1,0:T(1,128)S(1)}, f32[1,2048]{1,0:T(1,128)}, u32[]{:S(2)}) copy-start(f32[1,2048]{1,0:T(1,128)} %param.12) | copy-start | bytes 24580
  8.8 13.1 %copy-start.25 = (s32[512]{0:T(512)S(1)}, s32[512]{0:T(512)}, u32[]{:S(2)}) copy-start(s32[512]{0:T(512)} %param.17) | copy-start | bytes 6148
  9.5 14.7 %collective-permute-start = (f32[2,55,1,2048]{3,0,2,1:T(2,128)S(1)}, f32[2,55,1,2048]{3,0,2,1:T(2,128)}, u32[]{:S(2)}, u32[]{:S(2)}) collective-permute-start(f32[2,55,1,2048]{3,0,2,1:T(2,128)S(1)} %copy.48), channel_id=1, source_target_pairs={{0,4},{4,8},{8,12},{12,16},{16,20},{20,24},{24,28},{1,5},{5,9},{9,... | collective-permute-start | bytes 2703368 | tf_op jit(solution)/shard_map/ppermute | solution.py:24
  12.8 13.1 %collective-permute-start.1 = (f32[2,55,1,2048]{3,0,2,1:T(2,128)S(1)}, f32[2,55,1,2048]{3,0,2,1:T(2,128)}, u32[]{:S(2)}, u32[]{:S(2)}) collective-permute-start(f32[2,55,1,2048]{3,0,2,1:T(2,128)S(1)} %copy.48), channel_id=1, source_target_pairs={{4,0},{8,4},{12,8},{16,12},{20,16},{24,20},{28,24},{5,1},{9,5},{13... | collective-permute-start | bytes 2703368 | tf_op jit(solution)/shard_map/ppermute | solution.py:27
  32.3 55.1 %copy-start.3 = (f32[55,1,2048]{2,1,0:T(1,128)S(1)}, f32[55,1,2048]{2,1,0:T(1,128)}, u32[]{:S(2)}) copy-start(f32[55,1,2048]{2,1,0:T(1,128)} %param.9) | copy-start | bytes 1351684
  32.3 55.1 %copy-start.4 = (f32[55,1,2048]{2,1,0:T(1,128)S(1)}, f32[55,1,2048]{2,1,0:T(1,128)}, u32[]{:S(2)}) copy-start(f32[55,1,2048]{2,1,0:T(1,128)} %param.10) | copy-start | bytes 1351684
  100.5 16.6 %all-to-all-start = ((f32[4,1,28160]{2,1,0:T(1,128)}), f32[4,1,28160]{2,1,0:T(1,128)S(1)}, u32[]{:S(2)}, u32[]{:S(2)}) async-start(f32[4,1,28160]{2,1,0:T(1,128)} %reshape.1981), calls=%async_computation | async-start | bytes 901120 | tf_op jit(solution)/shard_map/all_to_all | solution.py:151
  125.3 10.9 %copy-start.41 = (pred[512]{0:T(512)(128)(4,1)S(1)}, pred[512]{0:T(512)(128)(4,1)}, u32[]{:S(2)}) copy-start(pred[512]{0:T(512)(128)(4,1)} %get-tuple-element.145) | copy-start | bytes 1540
  125.3 10.9 %copy-start.42 = (pred[512]{0:T(512)(128)(4,1)S(1)}, pred[512]{0:T(512)(128)(4,1)}, u32[]{:S(2)}) copy-start(pred[512]{0:T(512)(128)(4,1)} %get-tuple-element.146) | copy-start | bytes 1540
  125.3 14.3 %collective-permute-start.2 = (f32[220,1,512]{2,0,1:T(8,128)S(1)}, f32[220,1,512]{2,0,1:T(8,128)S(1)}, u32[]{:S(2)}, u32[]{:S(2)}) collective-permute-start(f32[220,1,512]{2,0,1:T(8,128)S(1)} %all_to_all.29), channel_id=1, source_target_pairs={{4,0},{8,4},{12,8},{16,12},{20,16},{24,20},{28,24},{5,1},{9,5},{13... | collective-permute-start | bytes 1351688 | tf_op jit(solution)/shard_map/ppermute | solution.py:27
  126.6 13.0 %collective-permute-start.3 = (f32[220,1,512]{2,0,1:T(8,128)S(1)}, f32[220,1,512]{2,0,1:T(8,128)S(1)}, u32[]{:S(2)}, u32[]{:S(2)}) collective-permute-start(f32[220,1,512]{2,0,1:T(8,128)S(1)} %all_to_all.29), channel_id=1, source_target_pairs={{0,4},{4,8},{8,12},{12,16},{16,20},{20,24},{24,28},{1,5},{5,9},{9,... | collective-permute-start | bytes 1351688 | tf_op jit(solution)/shard_map/ppermute | solution.py:24
  130.1 7.8 %collective-permute-start.4 = (f32[220,1,8]{2,0,1:T(8,128)S(1)}, f32[220,1,8]{2,0,1:T(8,128)S(1)}, u32[]{:S(2)}, u32[]{:S(2)}) collective-permute-start(f32[220,1,8]{2,0,1:T(8,128)S(1)} %get-tuple-element.40), channel_id=1, source_target_pairs={{1,0},{2,1},{3,2},{5,4},{6,5},{7,6},{9,8},{10,9},{11,10},{13,12},{... | collective-permute-start | bytes 21128 | tf_op jit(solution)/shard_map/ppermute | solution.py:35
  131.4 7.9 %collective-permute-start.5 = (f32[220,1,8]{2,0,1:T(8,128)S(1)}, f32[220,1,8]{2,0,1:T(8,128)S(1)}, u32[]{:S(2)}, u32[]{:S(2)}) collective-permute-start(f32[220,1,8]{2,0,1:T(8,128)S(1)} %get-tuple-element.41), channel_id=1, source_target_pairs={{0,1},{1,2},{2,3},{4,5},{5,6},{6,7},{8,9},{9,10},{10,11},{12,13},{... | collective-permute-start | bytes 21128 | tf_op jit(solution)/shard_map/ppermute | solution.py:35
  140.0 5.7 %copy-start.26 = (f32[1,512]{1,0:T(1,128)S(1)}, f32[1,512]{1,0:T(1,128)}, u32[]{:S(2)}) copy-start(f32[1,512]{1,0:T(1,128)} %constant_dynamic-slice_fusion.2) | copy-start | bytes 6148
  140.0 5.7 %copy-start.27 = (f32[512]{0:T(512)S(1)}, f32[512]{0:T(512)}, u32[]{:S(2)}) copy-start(f32[512]{0:T(512)} %convert_element_type.107) | copy-start | bytes 6148
  140.1 5.7 %copy-start.28 = (f32[1,512]{1,0:T(1,128)S(1)}, f32[1,512]{1,0:T(1,128)}, u32[]{:S(2)}) copy-start(f32[1,512]{1,0:T(1,128)} %get-tuple-element.96) | copy-start | bytes 6148
  140.1 5.7 %copy-start.29 = (f32[1,512]{1,0:T(1,128)S(1)}, f32[1,512]{1,0:T(1,128)}, u32[]{:S(2)}) copy-start(f32[1,512]{1,0:T(1,128)} %get-tuple-element.97) | copy-start | bytes 6148
  150.9 17.6 %all-to-all-start.1 = ((f32[220,1,512]{2,1,0:T(1,128)}), f32[220,1,512]{2,1,0:T(1,128)}, u32[]{:S(2)}, u32[]{:S(2)}) async-start(f32[220,1,512]{2,1,0:T(1,128)} %copy.59), calls=%async_computation.1 | async-start | bytes 901120 | tf_op jit(solution)/shard_map/all_to_all | solution.py:183
  171.3 6.1 %copy-start.2 = (f32[55,1,2047]{2,0,1:T(8,128)S(1)}, f32[55,1,2047]{2,0,1:T(8,128)}, u32[]{:S(2)}) copy-start(f32[55,1,2047]{2,0,1:T(8,128)} %get-tuple-element.31) | copy-start | bytes 1351024
  (39 other events, 128.5 us)
Sparse Core Ops, SparseCore 0:
  30.5 50.9 all-gather.2
where the time goes:
time: 188 us; the launch traced here: 187 us
  waiting for transfers between devices  75.4 us (40%)
  local copies, waits for them, and re-layouts  30.8 us (16%)
  other arithmetic  27.3 us (15%)
  starting transfers between devices  23 us (12%)
  matrix products  15.6 us (8%)
  between operations  15.1 us (8%)
    all_gather x1, waiting for transfers between devices, on_device(): lax.all_gather(flat_rough, 'modes', axis=0, tiled=True)  49.1 us
    all_to_all x1, waiting for transfers between devices, on_device(): lax.all_to_all(relaxed_voltage, 'modes', split_axis=2, concat_axis=0, til...  12.9 us
    all_to_all x1, waiting for transfers between devices, on_device(): lax.all_to_all(heat_points, 'modes', split_axis=0, concat_axis=2, tiled=T...  10.8 us
    unnamed x114, local copies, waits for them, and re-layouts  10.5 us
    unnamed x10, other arithmetic  10.1 us
    ppermute x2, starting transfers between devices, padded_2(): lax.ppermute(lax.slice_in_dim(block, block.shape[dim] - width, None, axis...  6.35 us
    all_to_all x3, local copies, waits for them, and re-layouts, on_device(): lax.all_to_all(heat_points, 'modes', split_axis=0, concat_axis=2, tiled=T...  6.1 us
    ppermute x2, starting transfers between devices, from_behind(): return lax.ppermute(block, axis, route)  6.07 us
  transfers between devices with their start and end apart: 9, of which 5 were waited for; matrix products, arithmetic and copies ran while one was open for 9% of the time, Pallas kernels for 0%

commit v1 on v0

v1 whole, which is shorter than its diff:
```python
import functools

import jax
import jax.numpy as jnp
from jax import lax
from jax.experimental import pallas as pl
from jax.experimental.pallas import tpu as pltpu
from jax.sharding import PartitionSpec as P

NZ = 8
LANES = 128
SUB = 8
TILE16 = 16
VMEM_LIMIT = 40 * 1024 * 1024

HERMITE_NODES = (
    0.0,
    1.355626179974266,
    -1.355626179974266,
    2.8569700138728056,
    -2.8569700138728056,
)

F32 = jnp.float32
BF16 = jnp.bfloat16


def split2(x):
    high = x.astype(BF16)
    return high, (x - high.astype(F32)).astype(BF16)


def dot(a, b):
    return jnp.dot(a, b, preferred_element_type=F32)


def dot_nt(a, b):
    return lax.dot_general(a, b, (((1,), (1,)), ((), ())), preferred_element_type=F32)


def dot3(a_high, a_low, b_high, b_low):
    return dot(a_high, b_high) + (dot(a_high, b_low) + dot(a_low, b_high))


def lane_ids(shape):
    return lax.broadcasted_iota(jnp.int32, shape, len(shape) - 1)


def load_group(ref, group, modes, groups):
    return ref[pl.ds(group, modes, stride=groups), :]


def pad_rows(x, rows):
    if x.shape[0] == rows:
        return x
    return jnp.concatenate([x, jnp.zeros((rows - x.shape[0], x.shape[1]), x.dtype)], axis=0)


def emit_slots(me, parts, grouped, outs, padded):
    groups = grouped.shape[0] // padded
    per = groups // parts
    lane = lane_ids((padded, LANES))
    for k, out in enumerate(outs):
        q = lax.rem(me + k, parts)
        start = pl.multiple_of(q * (per * padded), SUB)
        out[: per * padded, :] = grouped[pl.ds(start, per * padded), :]
        before = pl.multiple_of(jnp.maximum(q * per - 1, 0) * padded, SUB)
        after = pl.multiple_of(jnp.minimum(q * per + per, groups - 1) * padded, SUB)
        low = pltpu.roll(grouped[pl.ds(before, padded), :], NZ, 1)
        high = pltpu.roll(grouped[pl.ds(after, padded), :], NZ, 1)
        rim = jnp.where((lane < NZ) & (q > 0), low, 0.0)
        rim = jnp.where((lane >= NZ) & (lane < 2 * NZ) & (q < parts - 1), high, rim)
        packed = rim[:SUB]
        for tile in range(1, padded // SUB):
            packed = packed + pltpu.roll(rim[tile * SUB : (tile + 1) * SUB], 2 * NZ * tile, 1)
        out[per * padded :, :] = packed


def source_kernel(parts, modes, padded, v_ref, j_ref, a_ref, *rest):
    outs, grouped = rest[:-1], rest[-1]
    me = lax.axis_index("modes")
    groups = a_ref.shape[0]
    factor = 0.8 / (6.0 * a_ref[...])
    for g in range(groups):
        w = load_group(v_ref, g, modes, groups)
        w = w + load_group(j_ref, g, modes, groups) * factor[g : g + 1]
        grouped[g * padded : (g + 1) * padded, :] = pad_rows(w, padded)
    emit_slots(me, parts, grouped, outs, padded)


def stencil_groups(x_ref, lo_ref, hi_ref, modes, groups, padded, emit):
    lane = lane_ids((padded, LANES))
    depth = lane % NZ
    fields = [pad_rows(load_group(x_ref, g, modes, groups), padded) for g in range(groups)]
    for g in range(groups):
        x = fields[g]
        total = 6.0 * x - pad_rows(load_group(lo_ref, g, modes, groups), padded)
        total = total - pad_rows(load_group(hi_ref, g, modes, groups), padded)
        total = total - jnp.where(depth < NZ - 1, pltpu.roll(x, LANES - 1, 1), 0.0)
        total = total - jnp.where(depth > 0, pltpu.roll(x, 1, 1), 0.0)
        right = fields[g + 1] if g + 1 < groups else jnp.zeros_like(x)
        left = fields[g - 1] if g > 0 else jnp.zeros_like(x)
        total = total - pltpu.roll(jnp.where(lane < NZ, right, x), LANES - NZ, 1)
        total = total - pltpu.roll(jnp.where(lane >= LANES - NZ, left, x), NZ, 1)
        emit(g, x, total)


def rough_kernel(parts, modes, padded, groups, v_ref, lo_ref, hi_ref, *rest):
    outs, grouped = rest[:-1], rest[-1]
    me = lax.axis_index("modes")

    def emit(g, _, total):
        grouped[g * padded : (g + 1) * padded, :] = total

    stencil_groups(v_ref, lo_ref, hi_ref, modes, groups, padded, emit)
    emit_slots(me, parts, grouped, outs, padded)


def thermal_kernel(modes, padded, groups, t_ref, lo_ref, hi_ref, out_ref):
    def emit(g, x, total):
        out_ref[g * padded : (g + 1) * padded, :] = x - 0.15 * total

    stencil_groups(t_ref, lo_ref, hi_ref, modes, groups, padded, emit)


def tables_kernel(
    parts, modes, padded, table_ref, nodes_ref, share_ref, z_ref, zone_ref,
    ah_ref, al_ref, bh_ref, bl_ref, wh_ref, wl_ref, lift_ref, zones_ref,
    cols, basis_t,
):
    nreg, npar = z_ref.shape
    all_modes = parts * modes
    rows = parts * padded
    points = nodes_ref.shape[1]
    me = lax.axis_index("modes")

    slot = lax.broadcasted_iota(jnp.int32, (rows, all_modes), 0)
    mode = lax.broadcasted_iota(jnp.int32, (rows, all_modes), 1)
    within = slot % padded
    pick = (within < modes) & (mode == slot // padded * modes + within)
    pick = jnp.where(pick, 1.0, 0.0).astype(BF16)
    table = table_ref[...].astype(F32).astype(BF16)
    along = dot_nt(table, pick)
    lane_pad = lane_ids(along.shape) % padded >= modes
    along = jnp.where(lane_pad, -50.0, along)
    down = dot_nt(pick, table)
    row_pad = lax.broadcasted_iota(jnp.int32, down.shape, 0) % padded >= modes
    cols[...] = jnp.where(row_pad, -50.0, down)

    nodes = nodes_ref[...]
    t = jnp.zeros(nodes.shape, F32)
    for which in range(1, len(HERMITE_NODES)):
        t = jnp.where(nodes == which, HERMITE_NODES[which], t)
    h2 = (t * t - 1.0) * (1.0 / 2.0**0.5)
    h3 = (t * t * t - 3.0 * t) * (1.0 / 6.0**0.5)
    share = share_ref[...].astype(F32) * (0.25 / (512.0 * points * all_modes))

    def block(b, carry):
        at = pl.multiple_of(b * TILE16, TILE16)
        mine = cols[pl.ds(at, TILE16), :]
        count = jnp.zeros((TILE16, rows), F32)
        larger = jnp.zeros((TILE16, rows), F32)
        weight = [jnp.zeros((TILE16, rows), F32) for _ in range(nreg)]
        basis = jnp.ones((TILE16, points), F32)
        for m in range(npar):
            own = mine[:, m : m + 1]
            other = along[m : m + 1, :]
            gap = jnp.abs(own - other)
            count = count + jnp.where(gap != 0.0, 1.0, 0.0)
            one = gap == 1.0
            larger = jnp.where(one, jnp.maximum(own, other), larger)
            weight = [jnp.where(one, z_ref[r, m], weight[r]) for r in range(nreg)]
            factor = jnp.where(own == 0.0, 1.0, 0.0) + jnp.where(own == 1.0, t[m : m + 1], 0.0)
            factor = factor + jnp.where(own == 2.0, h2[m : m + 1], 0.0)
            factor = factor + jnp.where(own == 3.0, h3[m : m + 1], 0.0)
            basis = basis * factor
        root = jnp.where(count == 1.0, jnp.sqrt(larger), 0.0)
        for r in range(nreg):
            high, low = split2(jnp.where(count == 0.0, 1.0, root * weight[r]))
            spot = pl.multiple_of(r * rows + at, TILE16)
            ah_ref[pl.ds(spot, TILE16), :] = high
            al_ref[pl.ds(spot, TILE16), :] = low
        basis_t[pl.ds(at, TILE16), :] = basis
        high, low = split2(basis * share)
        wh_ref[pl.ds(at, TILE16), :] = high
        wl_ref[pl.ds(at, TILE16), :] = low
        return carry

    lax.fori_loop(0, rows // TILE16, block, 0)
    high, low = split2(basis_t[...].T)
    bh_ref[...] = high
    bl_ref[...] = low

    terms = []
    for r in range(nreg):
        lift = jnp.ones((1, points), F32)
        for m in range(npar):
            lift = lift + z_ref[r, m] * t[m : m + 1]
        terms.append(lift)
    lift = jnp.concatenate(terms, axis=0)
    high = lift.astype(BF16).astype(F32)
    mid = (lift - high).astype(BF16).astype(F32)
    low = lift - high - mid
    stacked = jnp.concatenate(
        [high, mid, low, jnp.zeros((LANES - 3 * nreg, points), F32)], axis=0
    )
    lift_ref[...] = stacked.T.astype(BF16)

    groups = zone_ref.shape[0]
    per = groups // parts
    zone = zone_ref[...]
    row = lax.broadcasted_iota(jnp.int32, zone.shape, 0)

    def pick_row(g):
        return jnp.sum(jnp.where(row == g, zone, 0), axis=0, keepdims=True)

    for s in range(per):
        zones_ref[:, s * LANES : (s + 1) * LANES] = pick_row(me * per + s)
    low = pltpu.roll(pick_row(jnp.maximum(me * per - 1, 0)), NZ, 1)
    high = pltpu.roll(pick_row(jnp.minimum(me * per + per, groups - 1)), NZ, 1)
    zones_ref[:, per * LANES :] = jnp.where(lane_ids(low.shape) < NZ, low, high)


def couple_kernel(
    parts, padded, per, nreg, *refs
):
    w_refs = refs[:parts]
    r_refs = refs[parts : 2 * parts]
    ah_ref, al_ref, zones_ref = refs[2 * parts : 2 * parts + 3]
    rel_ref, rim_ref = refs[2 * parts + 3 : 2 * parts + 5]
    outs = refs[2 * parts + 5 : -2]
    w_all, r_all = refs[-2:]
    me = lax.axis_index("modes")
    rows = parts * padded
    width = per * LANES
    for k in range(parts):
        source = lax.rem(me + (parts - k), parts)
        at = pl.multiple_of(source * padded, SUB)
        for chunk, dest in ((w_refs[k], w_all), (r_refs[k], r_all)):
            for s in range(per):
                dest[pl.ds(at, padded), s * LANES : (s + 1) * LANES] = chunk[
                    s * padded : (s + 1) * padded, :
                ]
            packed = chunk[per * padded :, :]
            for tile in range(padded // SUB):
                spot = pl.multiple_of(at + tile * SUB, SUB)
                shift = (LANES - 2 * NZ * tile) % LANES
                part = pltpu.roll(packed, shift, 1) if shift else packed
                dest[pl.ds(spot, SUB), width:] = part
    r_high, r_low = split2(r_all[...])
    zones = zones_ref[...]
    applied = jnp.zeros(r_all.shape, F32)
    for r in range(nreg):
        a_high = ah_ref[r * rows : (r + 1) * rows, :]
        a_low = al_ref[r * rows : (r + 1) * rows, :]
        applied = jnp.where(zones == r, dot3(a_high, a_low, r_high, r_low), applied)
    w_all[...] = w_all[...] - (0.8 / 6.0) * applied
    rel_ref[...] = w_all[:, :width]
    rim_ref[...] = w_all[:, width:]
    for k, out in enumerate(outs):
        target = lax.rem(me + k, parts)
        at = pl.multiple_of(target * padded, SUB)
        for s in range(per):
            out[s * padded : (s + 1) * padded, :] = w_all[
                pl.ds(at, padded), s * LANES : (s + 1) * LANES
            ]


def joule_kernel(
    parts, padded, per, nreg, rel_ref, rim_ref, lo_ref, hi_ref, a_ref, zones_ref,
    bh_ref, bl_ref, wh_ref, wl_ref, lift_ref, *rest,
):
    outs, heat_ref = rest[:-1], rest[-1]
    me = lax.axis_index("modes")
    width = per * LANES
    rel = rel_ref[...]
    rim = rim_ref[...]
    lane = lane_ids(rel.shape)
    depth = lane % NZ
    wide = jnp.concatenate([rim] + [jnp.zeros_like(rim)] * (per - 1), axis=1)
    along_z = jnp.where(depth < NZ - 1, pltpu.roll(rel, width - 1, 1), 0.0)
    along_z = along_z - jnp.where(depth > 0, pltpu.roll(rel, 1, 1), 0.0)
    after = pltpu.roll(wide, width - 2 * NZ, 1)
    along_y = jnp.where(lane >= width - NZ, after, pltpu.roll(rel, width - NZ, 1))
    along_y = along_y - jnp.where(lane < NZ, wide, pltpu.roll(rel, NZ, 1))
    along_x = hi_ref[...] - lo_ref[...]
    b_high, b_low = bh_ref[...], bl_ref[...]
    total = None
    for grad in (along_y, along_z, along_x):
        g_high, g_low = split2(grad)
        at_point = dot3(b_high, b_low, g_high, g_low)
        total = at_point * at_point if total is None else total + at_point * at_point
    zones = zones_ref[:, :width]
    row = lax.broadcasted_iota(jnp.int32, (LANES, width), 0)
    hot = (row < 3 * nreg) & (row % nreg == zones)
    spread = dot(lift_ref[...], jnp.where(hot, 1.0, 0.0).astype(BF16))
    j_high, j_low = split2(spread * total)
    heat = dot3(wh_ref[...], wl_ref[...], j_high, j_low)
    for s in range(per):
        heat_ref[:, s * LANES : (s + 1) * LANES] = (
            heat[:, s * LANES : (s + 1) * LANES] * a_ref[pl.ds(me * per + s, 1), :]
        )
    for k, out in enumerate(outs):
        target = lax.rem(me + k, parts)
        at = pl.multiple_of(target * padded, SUB)
        for s in range(per):
            out[s * padded : (s + 1) * padded, :] = heat_ref[
                pl.ds(at, padded), s * LANES : (s + 1) * LANES
            ]


def gather_kernel(parts, modes, padded, per, *refs):
    chunks, out = refs[:parts], refs[parts]
    me = lax.axis_index("modes")
    for k in range(parts):
        q = lax.rem(me + (parts - k), parts)
        for s in range(per):
            rows = chunks[k][s * padded : s * padded + modes, :]
            out[pl.ds(q * per + s, modes, stride=parts * per), :] = rows


def final_kernel(parts, modes, padded, per, *refs):
    chunks, base, out = refs[:parts], refs[parts], refs[parts + 1]
    me = lax.axis_index("modes")
    for k in range(parts):
        q = lax.rem(me + (parts - k), parts)
        for s in range(per):
            at = pl.multiple_of((q * per + s) * padded, SUB)
            rows = base[pl.ds(at, padded), :] + 0.1 * chunks[k][s * padded : (s + 1) * padded, :]
            out[pl.ds(q * per + s, modes, stride=parts * per), :] = rows[:modes]


def call(kernel, out_shape, args, scratch=(), smem=(), flops=0):
    specs = [
        pl.BlockSpec(memory_space=pltpu.SMEM if i in smem else pltpu.VMEM)
        for i in range(len(args))
    ]
    many = isinstance(out_shape, (list, tuple))
    vmem = pl.BlockSpec(memory_space=pltpu.VMEM)
    nbytes = sum(x.size * x.dtype.itemsize for x in args)
    return pl.pallas_call(
        kernel,
        out_shape=out_shape,
        in_specs=specs,
        out_specs=[vmem] * len(out_shape) if many else vmem,
        scratch_shapes=list(scratch),
        compiler_params=pltpu.CompilerParams(vmem_limit_bytes=VMEM_LIMIT),
        cost_estimate=pl.CostEstimate(flops=flops, bytes_accessed=nbytes, transcendentals=0),
    )(*args)


def exchange(chunks):
    parts = lax.axis_size("modes")
    received = [chunks[0]]
    for k in range(1, parts):
        pairs = [(i, (i + k) % parts) for i in range(parts)]
        received.append(lax.ppermute(chunks[k], "modes", pairs))
    return received


def halo(x):
    count = lax.axis_size("space")
    forward = [(i, i + 1) for i in range(count - 1)]
    backward = [(i + 1, i) for i in range(count - 1)]
    return lax.ppermute(x, "space", forward), lax.ppermute(x, "space", backward)


def on_device(
    voltage_expansion,
    current_injection,
    thermal_state,
    average_electric_transport,
    material_zone,
    zone_relative_response,
    polynomial_exponent_rows,
    quadrature_abscissa_choice,
    quadrature_integer_share,
):
    parts = lax.axis_size("modes")
    modes, planes, columns = voltage_expansion.shape
    nreg = zone_relative_response.shape[0]
    points = quadrature_integer_share.shape[0]
    groups = columns // LANES
    per = groups // parts
    padded = -(-modes // SUB) * SUB
    rows = parts * padded
    assert planes == 1 and groups * LANES == columns and per * parts == groups
    assert rows % TILE16 == 0 and 2 * NZ * padded <= SUB * LANES and 3 * nreg <= LANES

    def flat(x):
        return x.reshape(modes * groups, LANES)

    def struct(*shape, dtype=F32):
        return jax.ShapeDtypeStruct(shape, dtype)

    v, cur, temp = flat(voltage_expansion), flat(current_injection), flat(thermal_state)
    avg = average_electric_transport.reshape(groups, LANES)
    zone = material_zone.reshape(groups, LANES)
    chunk = struct(per * padded, LANES)
    rimmed = struct(per * padded + SUB, LANES)
    grouped = pltpu.VMEM((groups * padded, LANES), F32)

    v_low, v_high = halo(v)
    source = call(
        functools.partial(source_kernel, parts, modes, padded),
        [rimmed] * parts, [v, cur, avg], [grouped],
    )
    source = exchange(source)
    rough = call(
        functools.partial(rough_kernel, parts, modes, padded, groups),
        [rimmed] * parts, [v, v_low, v_high], [grouped],
    )
    rough = exchange(rough)
    a_high, a_low, b_high, b_low, w_high, w_low, lift, zones = call(
        functools.partial(tables_kernel, parts, modes, padded),
        [
            struct(nreg * rows, rows, dtype=BF16),
            struct(nreg * rows, rows, dtype=BF16),
            struct(points, rows, dtype=BF16),
            struct(points, rows, dtype=BF16),
            struct(rows, points, dtype=BF16),
            struct(rows, points, dtype=BF16),
            struct(points, LANES, dtype=BF16),
            struct(1, (per + 1) * LANES, dtype=jnp.int32),
        ],
        [
            polynomial_exponent_rows.T,
            quadrature_abscissa_choice.T,
            quadrature_integer_share.reshape(1, points),
            zone_relative_response,
            zone,
        ],
        [pltpu.VMEM((rows, polynomial_exponent_rows.shape[1]), F32), pltpu.VMEM((rows, points), F32)],
        smem=(3,),
    )
    t_low, t_high = halo(temp)
    base = call(
        functools.partial(thermal_kernel, modes, padded, groups),
        struct(groups * padded, LANES), [temp, t_low, t_high],
    )
    wide = (per + 1) * LANES
    relaxed, rim, *back = call(
        functools.partial(couple_kernel, parts, padded, per, nreg),
        [struct(rows, per * LANES), struct(rows, LANES)] + [chunk] * parts,
        [*source, *rough, a_high, a_low, zones],
        [pltpu.VMEM((rows, wide), F32), pltpu.VMEM((rows, wide), F32)],
    )
    x_low, x_high = halo(relaxed)
    back = exchange(back)
    heat = call(
        functools.partial(joule_kernel, parts, padded, per, nreg),
        [chunk] * parts,
        [relaxed, rim, x_low, x_high, avg, zones, b_high, b_low, w_high, w_low, lift],
        [pltpu.VMEM((rows, per * LANES), F32)],
    )
    heat = exchange(heat)
    relaxed_voltage = call(
        functools.partial(gather_kernel, parts, modes, padded, per),
        struct(modes * groups, LANES), back,
    )
    advanced = call(
        functools.partial(final_kernel, parts, modes, padded, per),
        struct(modes * groups, LANES), [*heat, base],
    )
    shape = voltage_expansion.shape
    return relaxed_voltage.reshape(shape), advanced.reshape(shape)


def solution(mesh):
    in_specs = (
        P("modes", "space", None),
        P("modes", "space", None),
        P("modes", "space", None),
        P("space", None),
        P("space", None),
        P(),
        P(),
        P(),
        P(),
    )
    out_specs = (P("modes", "space", None), P("modes", "space", None))
    return jax.shard_map(
        on_device, mesh=mesh, in_specs=in_specs, out_specs=out_specs, check_vma=False
    )
```

time: 188 us -> 71.1 us (0.38)
  the two profiles are of different devices: /device:TPU:0 before, /device:TPU:11 now
where the time goes in v1:
time: 71.1 us; the launch traced here: 70.7 us
  starting transfers between devices  30 us (42%)
  waiting for transfers between devices  24 us (34%)
  Pallas kernels  12.5 us (18%)
  local copies, waits for them, and re-layouts  3.42 us (5%)
  between operations  0.82 us (1%)
    ppermute x12, waiting for transfers between devices, exchange(): received.append(lax.ppermute(chunks[k], 'modes', pairs))  14.6 us
    ppermute x12, starting transfers between devices, exchange(): received.append(lax.ppermute(chunks[k], 'modes', pairs))  12.5 us
    pallas_call x8, Pallas kernels, call(): pl.pallas_call(kernel, out_shape=out_shape, in_specs=specs, out_specs=[vm...  12.5 us
    ppermute x3, starting transfers between devices, halo(): lax.ppermute(x, 'space', forward)  11.7 us
    ppermute x3, waiting for transfers between devices, halo(): lax.ppermute(x, 'space', backward)  9.41 us
    ppermute x3, starting transfers between devices, halo(): lax.ppermute(x, 'space', backward)  5.76 us
    unnamed x20, local copies, waits for them, and re-layouts  3.42 us
  transfers between devices with their start and end apart: 18, of which 9 were waited for; matrix products, arithmetic and copies ran while one was open for 0% of the time, Pallas kernels for 14%

profile of v1, /device:TPU:11, one launch (start us, length us, event | category | flops | bytes accessed | tf_op | source)
XLA Modules:
  0.0 70.7 jit_solution(18145987018428812828)
XLA Ops:
  0.6 3.7 %collective-permute-start.3 = (f32[880,128]{1,0:T(8,128)}, f32[880,128]{1,0:T(8,128)S(1)}, u32[]{:S(2)}, u32[]{:S(2)}) collective-permute-start(f32[880,128]{1,0:T(8,128)} %bitcast.10), channel_id=1, source_target_pairs={{0,4},{4,8},{8,12},{12,16},{16,20},{20,24},{24,28},{1,5},{5,9},{9,... | collective-permute-start | bytes 1351688 | tf_op jit(solution)/shard_map/ppermute | solution.py:365
  4.3 1.9 %collective-permute-start.4 = (f32[880,128]{1,0:T(8,128)}, f32[880,128]{1,0:T(8,128)S(1)}, u32[]{:S(2)}, u32[]{:S(2)}) collective-permute-start(f32[880,128]{1,0:T(8,128)} %bitcast.11), channel_id=1, source_target_pairs={{4,0},{8,4},{12,8},{16,12},{20,16},{24,20},{28,24},{5,1},{9,5},{13... | collective-permute-start | bytes 1351688 | tf_op jit(solution)/shard_map/ppermute | solution.py:365
  9.5 1.3 %collective-permute-start = (f32[232,128]{1,0:T(8,128)S(1)}, f32[232,128]{1,0:T(8,128)S(1)}, u32[]{:S(2)}, u32[]{:S(2)}) collective-permute-start(f32[232,128]{1,0:T(8,128)S(1)} %get-tuple-element.29), channel_id=1, source_target_pairs={{0,1},{1,2},{2,3},{3,0},{4,5},{5,6},{6,7},{7,4},{8,9},{9,10},{10,1... | collective-permute-start | bytes 356360 | tf_op jit(solution)/shard_map/ppermute | solution.py:357
  11.9 1.4 %collective-permute-start.2 = (f32[232,128]{1,0:T(8,128)S(1)}, f32[232,128]{1,0:T(8,128)S(1)}, u32[]{:S(2)}, u32[]{:S(2)}) collective-permute-start(f32[232,128]{1,0:T(8,128)S(1)} %get-tuple-element.31), channel_id=1, source_target_pairs={{0,3},{1,0},{2,1},{3,2},{4,7},{5,4},{6,5},{7,6},{8,11},{9,8},{10,9... | collective-permute-start | bytes 356360 | tf_op jit(solution)/shard_map/ppermute | solution.py:357
  13.3 3.0 %collective-permute-done.4.hi_ref = f32[880,128]{1,0:T(8,128)S(1)} collective-permute-done((f32[880,128]{1,0:T(8,128)}, f32[880,128]{1,0:T(8,128)S(1)}, u32[]{:S(2)}, u32[]{:S(2)}) %collective-permute-start.4) | collective-permute-done | bytes 450592 | tf_op jit(solution)/shard_map/ppermute | solution.py:365
  17.2 1.6 %collective-permute-start.5 = (f32[232,128]{1,0:T(8,128)S(1)}, f32[232,128]{1,0:T(8,128)S(1)}, u32[]{:S(2)}, u32[]{:S(2)}) collective-permute-start(f32[232,128]{1,0:T(8,128)S(1)} %get-tuple-element.33), channel_id=1, source_target_pairs={{0,1},{1,2},{2,3},{3,0},{4,5},{5,6},{6,7},{7,4},{8,9},{9,10},{10,1... | collective-permute-start | bytes 356360 | tf_op jit(solution)/shard_map/ppermute | solution.py:357
  19.8 1.2 %collective-permute-start.7 = (f32[232,128]{1,0:T(8,128)S(1)}, f32[232,128]{1,0:T(8,128)S(1)}, u32[]{:S(2)}, u32[]{:S(2)}) collective-permute-start(f32[232,128]{1,0:T(8,128)S(1)} %get-tuple-element.35), channel_id=1, source_target_pairs={{0,3},{1,0},{2,1},{3,2},{4,7},{5,4},{6,5},{7,6},{8,11},{9,8},{10,9... | collective-permute-start | bytes 356360 | tf_op jit(solution)/shard_map/ppermute | solution.py:357
  21.8 4.6 %shard_map.106 = (bf16[896,224]{1,0:T(8,128)(2,1)S(1)}, bf16[896,224]{1,0:T(8,128)(2,1)S(1)}, bf16[512,224]{1,0:T(8,128)(2,1)S(1)}, bf16[512,224]{1,0:T(8,128)(2...) custom-call(s32[9,220]{1,0:T(8,128)S(1)} %bitcast.21, ...), custom_call_target="tpu_custom_call" | custom-call | bytes 36736 | tf_op jit(solution)/shard_map/pallas_call | solution.py:341
  26.4 1.9 %collective-permute-done.2.refs_3_ = f32[232,128]{1,0:T(8,128)S(1)} collective-permute-done((f32[232,128]{1,0:T(8,128)S(1)}, f32[232,128]{1,0:T(8,128)S(1)}, u32[]{:S(2)}, u32[]{:S(2)}) %collective-permute-start.2) | collective-permute-done | bytes 118816 | tf_op jit(solution)/shard_map/ppermute | solution.py:357
  28.3 2.3 %collective-permute-done.6.refs_6_ = f32[232,128]{1,0:T(8,128)S(1)} collective-permute-done((f32[232,128]{1,0:T(8,128)S(1)}, f32[232,128]{1,0:T(8,128)S(1)}, u32[]{:S(2)}, u32[]{:S(2)}) %collective-permute-start.6) | collective-permute-done | bytes 118816 | tf_op jit(solution)/shard_map/ppermute | solution.py:357
  30.6 2.8 %collective-permute-done.7.refs_7_ = f32[232,128]{1,0:T(8,128)S(1)} collective-permute-done((f32[232,128]{1,0:T(8,128)S(1)}, f32[232,128]{1,0:T(8,128)S(1)}, u32[]{:S(2)}, u32[]{:S(2)}) %collective-permute-start.7) | collective-permute-done | bytes 118816 | tf_op jit(solution)/shard_map/ppermute | solution.py:357
  33.4 1.4 %shard_map.107 = (f32[224,512]{1,0:T(8,128)S(1)}, f32[224,128]{1,0:T(8,128)S(1)}, f32[224,128]{1,0:T(8,128)S(1)}, f32[224,128]{1,0:T(8,128)S(1)}, f32[224,128]{1,0:T(8,128)S(1)}, /*index=5*/f32[224,128]{1,0:T(8,128)S(1)}) custom-call(f32[232,128]{1,0:T(8,128)S(1)} %get-tuple-element.28.refs_0_, f32[232,128]{1,0:T(8,128)S(1)} %collective-permute-done.refs_1_, ...), custom_call_target="tpu_custom_call" | custom-call | bytes 1755648 | tf_op jit(solution)/shard_map/pallas_call | solution.py:341
  34.8 3.5 %collective-permute-start.11 = (f32[224,512]{1,0:T(8,128)S(1)}, f32[224,512]{1,0:T(8,128)S(1)}, u32[]{:S(2)}, u32[]{:S(2)}) collective-permute-start(f32[224,512]{1,0:T(8,128)S(1)} %get-tuple-element.43.rel_ref), channel_id=1, source_target_pairs={{0,4},{4,8},{8,12},{12,16},{16,20},{20,24},{24,28},{1,5},{5,9},{9,... | collective-permute-start | bytes 1376264 | tf_op jit(solution)/shard_map/ppermute | solution.py:365
  38.3 1.9 %collective-permute-start.12 = (f32[224,512]{1,0:T(8,128)S(1)}, f32[224,512]{1,0:T(8,128)S(1)}, u32[]{:S(2)}, u32[]{:S(2)}) collective-permute-start(f32[224,512]{1,0:T(8,128)S(1)} %get-tuple-element.43.rel_ref), channel_id=1, source_target_pairs={{4,0},{8,4},{12,8},{16,12},{20,16},{24,20},{28,24},{5,1},{9,5},{13... | collective-permute-start | bytes 1376264 | tf_op jit(solution)/shard_map/ppermute | solution.py:365
  40.2 4.5 %collective-permute-start.16 = (f32[880,128]{1,0:T(8,128)S(1)}, f32[880,128]{1,0:T(8,128)S(1)}, u32[]{:S(2)}, u32[]{:S(2)}) collective-permute-start(f32[880,128]{1,0:T(8,128)S(1)} %bitcast.14), channel_id=1, source_target_pairs={{0,4},{4,8},{8,12},{12,16},{16,20},{20,24},{24,28},{1,5},{5,9},{9,... | collective-permute-start | bytes 1351688 | tf_op jit(solution)/shard_map/ppermute | solution.py:365
  44.8 1.9 %collective-permute-start.17 = (f32[880,128]{1,0:T(8,128)S(1)}, f32[880,128]{1,0:T(8,128)S(1)}, u32[]{:S(2)}, u32[]{:S(2)}) collective-permute-start(f32[880,128]{1,0:T(8,128)S(1)} %bitcast.15), channel_id=1, source_target_pairs={{4,0},{8,4},{12,8},{16,12},{20,16},{24,20},{28,24},{5,1},{9,5},{13... | collective-permute-start | bytes 1351688 | tf_op jit(solution)/shard_map/ppermute | solution.py:365
  46.8 1.4 %collective-permute-start.8 = (f32[224,128]{1,0:T(8,128)S(1)}, f32[224,128]{1,0:T(8,128)S(1)}, u32[]{:S(2)}, u32[]{:S(2)}) collective-permute-start(f32[224,128]{1,0:T(8,128)S(1)} %get-tuple-element.40), channel_id=1, source_target_pairs={{0,1},{1,2},{2,3},{3,0},{4,5},{5,6},{6,7},{7,4},{8,9},{9,10},{10,1... | collective-permute-start | bytes 344072 | tf_op jit(solution)/shard_map/ppermute | solution.py:357
  48.2 5.2 %collective-permute-done.12.hi_ref = f32[224,512]{1,0:T(8,128)S(1)} collective-permute-done((f32[224,512]{1,0:T(8,128)S(1)}, f32[224,512]{1,0:T(8,128)S(1)}, u32[]{:S(2)}, u32[]{:S(2)}) %collective-permute-start.12) | collective-permute-done | bytes 458784 | tf_op jit(solution)/shard_map/ppermute | solution.py:365
  53.4 1.6 %collective-permute-start.9 = (f32[224,128]{1,0:T(8,128)S(1)}, f32[224,128]{1,0:T(8,128)S(1)}, u32[]{:S(2)}, u32[]{:S(2)}) collective-permute-start(f32[224,128]{1,0:T(8,128)S(1)} %get-tuple-element.41), channel_id=1, source_target_pairs={{0,2},{1,3},{2,0},{3,1},{4,6},{5,7},{6,4},{7,5},{8,10},{9,11},{10,... | collective-permute-start | bytes 344072 | tf_op jit(solution)/shard_map/ppermute | solution.py:357
  55.1 2.5 %shard_map.109 = (f32[224,128]{1,0:T(8,128)S(1)}, f32[224,128]{1,0:T(8,128)S(1)}, f32[224,128]{1,0:T(8,128)S(1)}, f32[224,128]{1,0:T(8,128)S(1)}) custom-call(f32[224,512]{1,0:T(8,128)S(1)} %get-tuple-element.43.rel_ref, f32[224,128]{1,0:T(8,128)S(1)} %get-tuple-element.44.rim_ref, f32[224,512]{1,0:T(8,128)S(1)} %collective-permute-done.11.lo_ref, ...), custom_call_target="tpu_custom_call" | custom-call | bytes 2550272 | tf_op jit(solution)/shard_map/pallas_call | solution.py:341
  57.6 1.2 %collective-permute-done.17.hi_ref = f32[880,128]{1,0:T(8,128)S(1)} collective-permute-done((f32[880,128]{1,0:T(8,128)S(1)}, f32[880,128]{1,0:T(8,128)S(1)}, u32[]{:S(2)}, u32[]{:S(2)}) %collective-permute-start.17) | collective-permute-done | bytes 450592 | tf_op jit(solution)/shard_map/ppermute | solution.py:365
  58.8 1.6 %collective-permute-start.14 = (f32[224,128]{1,0:T(8,128)S(1)}, f32[224,128]{1,0:T(8,128)S(1)}, u32[]{:S(2)}, u32[]{:S(2)}) collective-permute-start(f32[224,128]{1,0:T(8,128)S(1)} %get-tuple-element.52), channel_id=1, source_target_pairs={{0,2},{1,3},{2,0},{3,1},{4,6},{5,7},{6,4},{7,5},{8,10},{9,11},{10,... | collective-permute-start | bytes 344072 | tf_op jit(solution)/shard_map/ppermute | solution.py:357
  62.2 4.8 %collective-permute-done.13.refs_1_ = f32[224,128]{1,0:T(8,128)S(1)} collective-permute-done((f32[224,128]{1,0:T(8,128)S(1)}, f32[224,128]{1,0:T(8,128)S(1)}, u32[]{:S(2)}, u32[]{:S(2)}) %collective-permute-start.13) | collective-permute-done | bytes 114720 | tf_op jit(solution)/shard_map/ppermute | solution.py:357
  66.9 1.9 %collective-permute-done.14.refs_2_ = f32[224,128]{1,0:T(8,128)S(1)} collective-permute-done((f32[224,128]{1,0:T(8,128)S(1)}, f32[224,128]{1,0:T(8,128)S(1)}, u32[]{:S(2)}, u32[]{:S(2)}) %collective-permute-start.14) | collective-permute-done | bytes 114720 | tf_op jit(solution)/shard_map/ppermute | solution.py:357
  (40 shorter events, 10.5 us)
Async XLA Ops:
  0.6 12.7 %collective-permute-start.3 = (f32[880,128]{1,0:T(8,128)}, f32[880,128]{1,0:T(8,128)S(1)}, u32[]{:S(2)}, u32[]{:S(2)}) collective-permute-start(f32[880,128]{1,0:T(8,128)} %bitcast.10), channel_id=1, source_target_pairs={{0,4},{4,8},{8,12},{12,16},{16,20},{20,24},{24,28},{1,5},{5,9},{9,... | collective-permute-start | bytes 1351688 | tf_op jit(solution)/shard_map/ppermute | solution.py:365
  4.3 12.0 %collective-permute-start.4 = (f32[880,128]{1,0:T(8,128)}, f32[880,128]{1,0:T(8,128)S(1)}, u32[]{:S(2)}, u32[]{:S(2)}) collective-permute-start(f32[880,128]{1,0:T(8,128)} %bitcast.11), channel_id=1, source_target_pairs={{4,0},{8,4},{12,8},{16,12},{20,16},{24,20},{28,24},{5,1},{9,5},{13... | collective-permute-start | bytes 1351688 | tf_op jit(solution)/shard_map/ppermute | solution.py:365
  6.2 1.0 %copy-start = (f32[55,1,2048]{2,1,0:T(1,128)S(1)}, f32[55,1,2048]{2,1,0:T(1,128)}, u32[]{:S(2)}) copy-start(f32[55,1,2048]{2,1,0:T(1,128)} %param.9) | copy-start | bytes 1351684
  9.5 10.4 %collective-permute-start = (f32[232,128]{1,0:T(8,128)S(1)}, f32[232,128]{1,0:T(8,128)S(1)}, u32[]{:S(2)}, u32[]{:S(2)}) collective-permute-start(f32[232,128]{1,0:T(8,128)S(1)} %get-tuple-element.29), channel_id=1, source_target_pairs={{0,1},{1,2},{2,3},{3,0},{4,5},{5,6},{6,7},{7,4},{8,9},{9,10},{10,1... | collective-permute-start | bytes 356360 | tf_op jit(solution)/shard_map/ppermute | solution.py:357
  10.8 15.5 %collective-permute-start.1 = (f32[232,128]{1,0:T(8,128)S(1)}, f32[232,128]{1,0:T(8,128)S(1)}, u32[]{:S(2)}, u32[]{:S(2)}) collective-permute-start(f32[232,128]{1,0:T(8,128)S(1)} %get-tuple-element.30), channel_id=1, source_target_pairs={{0,2},{1,3},{2,0},{3,1},{4,6},{5,7},{6,4},{7,5},{8,10},{9,11},{10,... | collective-permute-start | bytes 356360 | tf_op jit(solution)/shard_map/ppermute | solution.py:357
  11.9 16.4 %collective-permute-start.2 = (f32[232,128]{1,0:T(8,128)S(1)}, f32[232,128]{1,0:T(8,128)S(1)}, u32[]{:S(2)}, u32[]{:S(2)}) collective-permute-start(f32[232,128]{1,0:T(8,128)S(1)} %get-tuple-element.31), channel_id=1, source_target_pairs={{0,3},{1,0},{2,1},{3,2},{4,7},{5,4},{6,5},{7,6},{8,11},{9,8},{10,9... | collective-permute-start | bytes 356360 | tf_op jit(solution)/shard_map/ppermute | solution.py:357
  16.3 4.8 %copy-start.5 = (s32[512,9]{0,1:T(8,128)S(1)}, s32[512,9]{0,1:T(8,128)}, u32[]{:S(2)}) copy-start(s32[512,9]{0,1:T(8,128)} %param.16) | copy-start | bytes 55300
  16.3 4.8 %copy-start.6 = (s32[220,9]{0,1:T(8,128)S(1)}, s32[220,9]{0,1:T(8,128)}, u32[]{:S(2)}) copy-start(s32[220,9]{0,1:T(8,128)} %param.15) | copy-start | bytes 23764
  17.2 3.9 %copy-start.7 = (s32[1,2048]{1,0:T(1,128)S(1)}, s32[1,2048]{1,0:T(1,128)}, u32[]{:S(2)}) copy-start(s32[1,2048]{1,0:T(1,128)} %param.13) | copy-start | bytes 24580
  17.2 11.0 %collective-permute-start.5 = (f32[232,128]{1,0:T(8,128)S(1)}, f32[232,128]{1,0:T(8,128)S(1)}, u32[]{:S(2)}, u32[]{:S(2)}) collective-permute-start(f32[232,128]{1,0:T(8,128)S(1)} %get-tuple-element.33), channel_id=1, source_target_pairs={{0,1},{1,2},{2,3},{3,0},{4,5},{5,6},{6,7},{7,4},{8,9},{9,10},{10,1... | collective-permute-start | bytes 356360 | tf_op jit(solution)/shard_map/ppermute | solution.py:357
  18.9 11.7 %collective-permute-start.6 = (f32[232,128]{1,0:T(8,128)S(1)}, f32[232,128]{1,0:T(8,128)S(1)}, u32[]{:S(2)}, u32[]{:S(2)}) collective-permute-start(f32[232,128]{1,0:T(8,128)S(1)} %get-tuple-element.34), channel_id=1, source_target_pairs={{0,2},{1,3},{2,0},{3,1},{4,6},{5,7},{6,4},{7,5},{8,10},{9,11},{10,... | collective-permute-start | bytes 356360 | tf_op jit(solution)/shard_map/ppermute | solution.py:357
  19.8 13.5 %collective-permute-start.7 = (f32[232,128]{1,0:T(8,128)S(1)}, f32[232,128]{1,0:T(8,128)S(1)}, u32[]{:S(2)}, u32[]{:S(2)}) collective-permute-start(f32[232,128]{1,0:T(8,128)S(1)} %get-tuple-element.35), channel_id=1, source_target_pairs={{0,3},{1,0},{2,1},{3,2},{4,7},{5,4},{6,5},{7,6},{8,11},{9,8},{10,9... | collective-permute-start | bytes 356360 | tf_op jit(solution)/shard_map/ppermute | solution.py:357
  33.4 6.8 %copy-start.1 = (f32[55,1,2048]{2,1,0:T(1,128)S(1)}, f32[55,1,2048]{2,1,0:T(1,128)}, u32[]{:S(2)}) copy-start(f32[55,1,2048]{2,1,0:T(1,128)} %param.11) | copy-start | bytes 1351684
  34.8 12.0 %collective-permute-start.11 = (f32[224,512]{1,0:T(8,128)S(1)}, f32[224,512]{1,0:T(8,128)S(1)}, u32[]{:S(2)}, u32[]{:S(2)}) collective-permute-start(f32[224,512]{1,0:T(8,128)S(1)} %get-tuple-element.43.rel_ref), channel_id=1, source_target_pairs={{0,4},{4,8},{8,12},{12,16},{16,20},{20,24},{24,28},{1,5},{5,9},{9,... | collective-permute-start | bytes 1376264 | tf_op jit(solution)/shard_map/ppermute | solution.py:365
  38.3 15.2 %collective-permute-start.12 = (f32[224,512]{1,0:T(8,128)S(1)}, f32[224,512]{1,0:T(8,128)S(1)}, u32[]{:S(2)}, u32[]{:S(2)}) collective-permute-start(f32[224,512]{1,0:T(8,128)S(1)} %get-tuple-element.43.rel_ref), channel_id=1, source_target_pairs={{4,0},{8,4},{12,8},{16,12},{20,16},{24,20},{28,24},{5,1},{9,5},{13... | collective-permute-start | bytes 1376264 | tf_op jit(solution)/shard_map/ppermute | solution.py:365
  40.2 17.3 %collective-permute-start.16 = (f32[880,128]{1,0:T(8,128)S(1)}, f32[880,128]{1,0:T(8,128)S(1)}, u32[]{:S(2)}, u32[]{:S(2)}) collective-permute-start(f32[880,128]{1,0:T(8,128)S(1)} %bitcast.14), channel_id=1, source_target_pairs={{0,4},{4,8},{8,12},{12,16},{16,20},{20,24},{24,28},{1,5},{5,9},{9,... | collective-permute-start | bytes 1351688 | tf_op jit(solution)/shard_map/ppermute | solution.py:365
  44.8 14.1 %collective-permute-start.17 = (f32[880,128]{1,0:T(8,128)S(1)}, f32[880,128]{1,0:T(8,128)S(1)}, u32[]{:S(2)}, u32[]{:S(2)}) collective-permute-start(f32[880,128]{1,0:T(8,128)S(1)} %bitcast.15), channel_id=1, source_target_pairs={{4,0},{8,4},{12,8},{16,12},{20,16},{24,20},{28,24},{5,1},{9,5},{13... | collective-permute-start | bytes 1351688 | tf_op jit(solution)/shard_map/ppermute | solution.py:365
  46.7 8.4 %copy-start.4 = (f32[1,2048]{1,0:T(1,128)S(1)}, f32[1,2048]{1,0:T(1,128)}, u32[]{:S(2)}) copy-start(f32[1,2048]{1,0:T(1,128)} %param.12) | copy-start | bytes 24580
  46.7 13.8 %collective-permute-start.10 = (f32[224,128]{1,0:T(8,128)S(1)}, f32[224,128]{1,0:T(8,128)S(1)}, u32[]{:S(2)}, u32[]{:S(2)}) collective-permute-start(f32[224,128]{1,0:T(8,128)S(1)} %get-tuple-element.42), channel_id=1, source_target_pairs={{0,3},{1,0},{2,1},{3,2},{4,7},{5,4},{6,5},{7,6},{8,11},{9,8},{10,9... | collective-permute-start | bytes 344072 | tf_op jit(solution)/shard_map/ppermute | solution.py:357
  46.8 14.4 %collective-permute-start.8 = (f32[224,128]{1,0:T(8,128)S(1)}, f32[224,128]{1,0:T(8,128)S(1)}, u32[]{:S(2)}, u32[]{:S(2)}) collective-permute-start(f32[224,128]{1,0:T(8,128)S(1)} %get-tuple-element.40), channel_id=1, source_target_pairs={{0,1},{1,2},{2,3},{3,0},{4,5},{5,6},{6,7},{7,4},{8,9},{9,10},{10,1... | collective-permute-start | bytes 344072 | tf_op jit(solution)/shard_map/ppermute | solution.py:357
  53.4 7.8 %collective-permute-start.9 = (f32[224,128]{1,0:T(8,128)S(1)}, f32[224,128]{1,0:T(8,128)S(1)}, u32[]{:S(2)}, u32[]{:S(2)}) collective-permute-start(f32[224,128]{1,0:T(8,128)S(1)} %get-tuple-element.41), channel_id=1, source_target_pairs={{0,2},{1,3},{2,0},{3,1},{4,6},{5,7},{6,4},{7,5},{8,10},{9,11},{10,... | collective-permute-start | bytes 344072 | tf_op jit(solution)/shard_map/ppermute | solution.py:357
  57.6 9.4 %collective-permute-start.13 = (f32[224,128]{1,0:T(8,128)S(1)}, f32[224,128]{1,0:T(8,128)S(1)}, u32[]{:S(2)}, u32[]{:S(2)}) collective-permute-start(f32[224,128]{1,0:T(8,128)S(1)} %get-tuple-element.51), channel_id=1, source_target_pairs={{0,1},{1,2},{2,3},{3,0},{4,5},{5,6},{6,7},{7,4},{8,9},{9,10},{10,1... | collective-permute-start | bytes 344072 | tf_op jit(solution)/shard_map/ppermute | solution.py:357
  58.8 10.0 %collective-permute-start.14 = (f32[224,128]{1,0:T(8,128)S(1)}, f32[224,128]{1,0:T(8,128)S(1)}, u32[]{:S(2)}, u32[]{:S(2)}) collective-permute-start(f32[224,128]{1,0:T(8,128)S(1)} %get-tuple-element.52), channel_id=1, source_target_pairs={{0,2},{1,3},{2,0},{3,1},{4,6},{5,7},{6,4},{7,5},{8,10},{9,11},{10,... | collective-permute-start | bytes 344072 | tf_op jit(solution)/shard_map/ppermute | solution.py:357
  60.5 9.2 %collective-permute-start.15 = (f32[224,128]{1,0:T(8,128)S(1)}, f32[224,128]{1,0:T(8,128)S(1)}, u32[]{:S(2)}, u32[]{:S(2)}) collective-permute-start(f32[224,128]{1,0:T(8,128)S(1)} %get-tuple-element.53), channel_id=1, source_target_pairs={{0,3},{1,0},{2,1},{3,2},{4,7},{5,4},{6,5},{7,6},{8,11},{9,8},{10,9... | collective-permute-start | bytes 344072 | tf_op jit(solution)/shard_map/ppermute | solution.py:357
  (4 other events, 3.1 us)

commit v2 on v1

--- a/solution.py
+++ b/solution.py
@@ -76,8 +76,14 @@
         out[per * padded :, :] = packed
 
 
-def source_kernel(parts, modes, padded, v_ref, j_ref, a_ref, *rest):
-    outs, grouped = rest[:-1], rest[-1]
+def source_kernel(parts, modes, padded, v_hbm, j_hbm, a_hbm, *rest):
+    outs, (grouped, v_ref, j_ref, a_ref, sems) = rest[:-5], rest[-5:]
+    pairs = ((v_hbm, v_ref), (j_hbm, j_ref), (a_hbm, a_ref))
+    copies = [pltpu.make_async_copy(x, y, sems.at[i]) for i, (x, y) in enumerate(pairs)]
+    for copy in copies:
+        copy.start()
+    for copy in copies:
+        copy.wait()
     me = lax.axis_index("modes")
     groups = a_ref.shape[0]
     factor = 0.8 / (6.0 * a_ref[...])
@@ -88,14 +94,14 @@
     emit_slots(me, parts, grouped, outs, padded)
 
 
-def stencil_groups(x_ref, lo_ref, hi_ref, modes, groups, padded, emit):
+def stencil_groups(x_ref, near_ref, far_ref, modes, groups, padded, emit):
     lane = lane_ids((padded, LANES))
     depth = lane % NZ
     fields = [pad_rows(load_group(x_ref, g, modes, groups), padded) for g in range(groups)]
     for g in range(groups):
         x = fields[g]
-        total = 6.0 * x - pad_rows(load_group(lo_ref, g, modes, groups), padded)
-        total = total - pad_rows(load_group(hi_ref, g, modes, groups), padded)
+        total = 6.0 * x - pad_rows(load_group(near_ref, g, modes, groups), padded)
+        total = total - pad_rows(load_group(far_ref, g, modes, groups), padded)
         total = total - jnp.where(depth < NZ - 1, pltpu.roll(x, LANES - 1, 1), 0.0)
         total = total - jnp.where(depth > 0, pltpu.roll(x, 1, 1), 0.0)
         right = fields[g + 1] if g + 1 < groups else jnp.zeros_like(x)
@@ -105,22 +111,22 @@
         emit(g, x, total)
 
 
-def rough_kernel(parts, modes, padded, groups, v_ref, lo_ref, hi_ref, *rest):
+def rough_kernel(parts, modes, padded, groups, v_ref, near_ref, far_ref, *rest):
     outs, grouped = rest[:-1], rest[-1]
     me = lax.axis_index("modes")
 
     def emit(g, _, total):
         grouped[g * padded : (g + 1) * padded, :] = total
 
-    stencil_groups(v_ref, lo_ref, hi_ref, modes, groups, padded, emit)
+    stencil_groups(v_ref, near_ref, far_ref, modes, groups, padded, emit)
     emit_slots(me, parts, grouped, outs, padded)
 
 
-def thermal_kernel(modes, padded, groups, t_ref, lo_ref, hi_ref, out_ref):
+def thermal_kernel(modes, padded, groups, t_ref, near_ref, far_ref, out_ref):
     def emit(g, x, total):
         out_ref[g * padded : (g + 1) * padded, :] = x - 0.15 * total
 
-    stencil_groups(t_ref, lo_ref, hi_ref, modes, groups, padded, emit)
+    stencil_groups(t_ref, near_ref, far_ref, modes, groups, padded, emit)
 
 
 def tables_kernel(
@@ -267,7 +273,7 @@
 
 
 def joule_kernel(
-    parts, padded, per, nreg, rel_ref, rim_ref, lo_ref, hi_ref, a_ref, zones_ref,
+    parts, padded, per, nreg, rel_ref, rim_ref, near_ref, far_ref, a_ref, zones_ref,
     bh_ref, bl_ref, wh_ref, wl_ref, lift_ref, *rest,
 ):
     outs, heat_ref = rest[:-1], rest[-1]
@@ -283,7 +289,7 @@
     after = pltpu.roll(wide, width - 2 * NZ, 1)
     along_y = jnp.where(lane >= width - NZ, after, pltpu.roll(rel, width - NZ, 1))
     along_y = along_y - jnp.where(lane < NZ, wide, pltpu.roll(rel, NZ, 1))
-    along_x = hi_ref[...] - lo_ref[...]
+    along_x = far_ref[...] - near_ref[...]
     b_high, b_low = bh_ref[...], bl_ref[...]
     total = None
     for grad in (along_y, along_z, along_x):
@@ -330,9 +336,11 @@
             out[pl.ds(q * per + s, modes, stride=parts * per), :] = rows[:modes]
 
 
-def call(kernel, out_shape, args, scratch=(), smem=(), flops=0):
+def call(kernel, out_shape, args, scratch=(), smem=(), hbm=(), limit=VMEM_LIMIT):
     specs = [
-        pl.BlockSpec(memory_space=pltpu.SMEM if i in smem else pltpu.VMEM)
+        pl.BlockSpec(
+            memory_space=pltpu.SMEM if i in smem else pltpu.HBM if i in hbm else pltpu.VMEM
+        )
         for i in range(len(args))
     ]
     many = isinstance(out_shape, (list, tuple))
@@ -344,8 +352,8 @@
         in_specs=specs,
         out_specs=[vmem] * len(out_shape) if many else vmem,
         scratch_shapes=list(scratch),
-        compiler_params=pltpu.CompilerParams(vmem_limit_bytes=VMEM_LIMIT),
-        cost_estimate=pl.CostEstimate(flops=flops, bytes_accessed=nbytes, transcendentals=0),
+        compiler_params=pltpu.CompilerParams(vmem_limit_bytes=limit),
+        cost_estimate=pl.CostEstimate(flops=0, bytes_accessed=nbytes, transcendentals=0),
     )(*args)
 
 
@@ -360,9 +368,10 @@
 
 def halo(x):
     count = lax.axis_size("space")
-    forward = [(i, i + 1) for i in range(count - 1)]
-    backward = [(i + 1, i) for i in range(count - 1)]
-    return lax.ppermute(x, "space", forward), lax.ppermute(x, "space", backward)
+    near = [(i, i ^ 1) for i in range(count) if i ^ 1 < count]
+    far = [(i, ((i - 1) ^ 1) + 1) for i in range(1, count) if ((i - 1) ^ 1) + 1 < count]
+    far = lax.ppermute(x, "space", far)
+    return lax.ppermute(x, "space", near), far
 
 
 def on_device(
@@ -400,17 +409,17 @@
     rimmed = struct(per * padded + SUB, LANES)
     grouped = pltpu.VMEM((groups * padded, LANES), F32)
 
-    v_low, v_high = halo(v)
+    fields = pltpu.VMEM((modes * groups, LANES), F32)
+    v_near, v_far = halo(v)
     source = call(
         functools.partial(source_kernel, parts, modes, padded),
-        [rimmed] * parts, [v, cur, avg], [grouped],
+        [rimmed] * parts,
+        [v, cur, avg],
+        [grouped, fields, fields, pltpu.VMEM((groups, LANES), F32), pltpu.SemaphoreType.DMA((3,))],
+        hbm=(0, 1, 2),
+        limit=62 * 1024 * 1024,
     )
     source = exchange(source)
-    rough = call(
-        functools.partial(rough_kernel, parts, modes, padded, groups),
-        [rimmed] * parts, [v, v_low, v_high], [grouped],
-    )
-    rough = exchange(rough)
     a_high, a_low, b_high, b_low, w_high, w_low, lift, zones = call(
         functools.partial(tables_kernel, parts, modes, padded),
         [
@@ -433,10 +442,17 @@
         [pltpu.VMEM((rows, polynomial_exponent_rows.shape[1]), F32), pltpu.VMEM((rows, points), F32)],
         smem=(3,),
     )
-    t_low, t_high = halo(temp)
+    v, zones = lax.optimization_barrier((v, zones))
+    rough = call(
+        functools.partial(rough_kernel, parts, modes, padded, groups),
+        [rimmed] * parts, [v, v_near, v_far], [grouped],
+    )
+    temp_after, *rough = lax.optimization_barrier((temp, *rough))
+    rough = exchange(rough)
+    t_near, t_far = halo(temp_after)
     base = call(
         functools.partial(thermal_kernel, modes, padded, groups),
-        struct(groups * padded, LANES), [temp, t_low, t_high],
+        struct(groups * padded, LANES), [temp, t_near, t_far],
     )
     wide = (per + 1) * LANES
     relaxed, rim, *back = call(
@@ -445,12 +461,13 @@
         [*source, *rough, a_high, a_low, zones],
         [pltpu.VMEM((rows, wide), F32), pltpu.VMEM((rows, wide), F32)],
     )
-    x_low, x_high = halo(relaxed)
+    x_near, x_far = halo(relaxed)
+    base, *back = lax.optimization_barrier((base, *back))
     back = exchange(back)
     heat = call(
         functools.partial(joule_kernel, parts, padded, per, nreg),
         [chunk] * parts,
-        [relaxed, rim, x_low, x_high, avg, zones, b_high, b_low, w_high, w_low, lift],
+        [relaxed, rim, x_near, x_far, avg, zones, b_high, b_low, w_high, w_low, lift],
         [pltpu.VMEM((rows, per * LANES), F32)],
     )
     heat = exchange(heat)

time: 71.1 us -> 62.4 us (0.88)
  starting transfers between devices: 30 us -> 25 us
  local copies, waits for them, and re-layouts: 3.42 us -> 0.72 us
  waiting for transfers between devices: 24 us -> 21.3 us
  Pallas kernels: 12.5 us -> 14.4 us
    ppermute x6, starting transfers between devices: 17.5 us -> 10.9 us  [the longest x3 10.7 us: halo(): far = lax.ppermute(x, 'space', far)]
    unnamed x20 -> x18, local copies, waits for them, and re-layouts: 3.42 us -> 0.72 us
    ppermute x6, waiting for transfers between devices: 9.42 us -> 7.22 us  [the longest x3 7.21 us: halo(): far = lax.ppermute(x, 'space', far)]
    pallas_call x8, Pallas kernels: 12.5 us -> 14.4 us  [call(): pl.pallas_call(kernel, out_shape=out_shape, in_specs=specs, out_specs=[vm...]
    ppermute x12, starting transfers between devices: 12.5 us -> 14.1 us  [exchange(): received.append(lax.ppermute(chunks[k], 'modes', pairs))]
  transfers between devices with their start and end apart: 18 -> 18, of which waited for: 9 -> 8; matrix products, arithmetic and copies ran while one was open for 0% -> 0% of each run, Pallas kernels for 14% -> 22%
where the time goes in v2:
time: 62.4 us; the launch traced here: 62.2 us
  starting transfers between devices  25 us (40%)
  waiting for transfers between devices  21.3 us (34%)
  Pallas kernels  14.4 us (23%)
  between operations  0.81 us (1%)
  local copies, waits for them, and re-layouts  0.72 us (1%)
    pallas_call x8, Pallas kernels, call(): pl.pallas_call(kernel, out_shape=out_shape, in_specs=specs, out_specs=[vm...  14.4 us
    ppermute x12, starting transfers between devices, exchange(): received.append(lax.ppermute(chunks[k], 'modes', pairs))  14.1 us
    ppermute x12, waiting for transfers between devices, exchange(): received.append(lax.ppermute(chunks[k], 'modes', pairs))  14.1 us
    ppermute x3, starting transfers between devices, halo(): far = lax.ppermute(x, 'space', far)  10.7 us
    ppermute x3, waiting for transfers between devices, halo(): far = lax.ppermute(x, 'space', far)  7.21 us
  transfers between devices with their start and end apart: 18, of which 8 were waited for; matrix products, arithmetic and copies ran while one was open for 0% of the time, Pallas kernels for 22%

profile of v2, /device:TPU:11, one launch (start us, length us, event | category | flops | bytes accessed | tf_op | source)
XLA Modules:
  0.0 62.2 jit_solution(2696587662177059059)
XLA Ops:
  0.6 3.7 %collective-permute-start.1 = (f32[880,128]{1,0:T(8,128)}, f32[880,128]{1,0:T(8,128)S(1)}, u32[]{:S(2)}, u32[]{:S(2)}) collective-permute-start(f32[880,128]{1,0:T(8,128)} %bitcast.10), channel_id=1, source_target_pairs={{4,8},{8,4},{12,16},{16,12},{20,24},{24,20},{5,9},{9,5},{13,17},{1... | collective-permute-start | bytes 1351688 | tf_op jit(solution)/shard_map/ppermute | solution.py:373
  4.4 2.5 %shard_map.107 = (f32[232,128]{1,0:T(8,128)}, f32[232,128]{1,0:T(8,128)}, f32[232,128]{1,0:T(8,128)}, f32[232,128]{1,0:T(8,128)}) custom-call(f32[880,128]{1,0:T(8,128)} %bitcast.12, f32[880,128]{1,0:T(8,128)} %bitcast.23, f32[16,128]{1,0:T(8,128)} %bitcast.17), custom_call_target="tpu_custom_call" | custom-call | bytes 909312 | tf_op jit(solution)/shard_map/pallas_call | solution.py:349
  6.9 1.4 %collective-permute-start.4 = (f32[232,128]{1,0:T(8,128)}, f32[232,128]{1,0:T(8,128)S(1)}, u32[]{:S(2)}, u32[]{:S(2)}) collective-permute-start(f32[232,128]{1,0:T(8,128)} %get-tuple-element.48), channel_id=1, source_target_pairs={{0,1},{1,2},{2,3},{3,0},{4,5},{5,6},{6,7},{7,4},{8,9},{9,10},{10,1... | collective-permute-start | bytes 356360 | tf_op jit(solution)/shard_map/ppermute | solution.py:365
  8.3 1.1 %collective-permute-start.5 = (f32[232,128]{1,0:T(8,128)}, f32[232,128]{1,0:T(8,128)S(1)}, u32[]{:S(2)}, u32[]{:S(2)}) collective-permute-start(f32[232,128]{1,0:T(8,128)} %get-tuple-element.49), channel_id=1, source_target_pairs={{0,2},{1,3},{2,0},{3,1},{4,6},{5,7},{6,4},{7,5},{8,10},{9,11},{10,... | collective-permute-start | bytes 356360 | tf_op jit(solution)/shard_map/ppermute | solution.py:365
  9.4 1.4 %collective-permute-start.6 = (f32[232,128]{1,0:T(8,128)}, f32[232,128]{1,0:T(8,128)S(1)}, u32[]{:S(2)}, u32[]{:S(2)}) collective-permute-start(f32[232,128]{1,0:T(8,128)} %get-tuple-element.50), channel_id=1, source_target_pairs={{0,3},{1,0},{2,1},{3,2},{4,7},{5,4},{6,5},{7,6},{8,11},{9,8},{10,9... | collective-permute-start | bytes 356360 | tf_op jit(solution)/shard_map/ppermute | solution.py:365
  11.5 4.6 %shard_map.104 = (bf16[896,224]{1,0:T(8,128)(2,1)S(1)}, bf16[896,224]{1,0:T(8,128)(2,1)S(1)}, bf16[512,224]{1,0:T(8,128)(2,1)S(1)}, bf16[512,224]{1,0:T(8,128)(2...) custom-call(s32[9,220]{1,0:T(8,128)S(1)} %bitcast.20, ...), custom_call_target="tpu_custom_call" | custom-call | bytes 36736 | tf_op jit(solution)/shard_map/pallas_call | solution.py:349
  16.5 0.9 %shard_map.105 = (f32[232,128]{1,0:T(8,128)S(1)}, f32[232,128]{1,0:T(8,128)S(1)}, f32[232,128]{1,0:T(8,128)S(1)}, f32[232,128]{1,0:T(8,128)S(1)}) custom-call(f32[880,128]{1,0:T(8,128)S(1)} %bitcast.13, f32[880,128]{1,0:T(8,128)S(1)} %collective-permute-done.near_ref, f32[880,128]{1,0:T(8,128)S(1)} %collective-permute-done.1.far_ref), custom_call_target="tpu_custom_call" | custom-call | bytes 1351680 | tf_op jit(solution)/shard_map/pallas_call | solution.py:349
  17.4 1.1 %collective-permute-start.7 = (f32[232,128]{1,0:T(8,128)S(1)}, f32[232,128]{1,0:T(8,128)S(1)}, u32[]{:S(2)}, u32[]{:S(2)}) collective-permute-start(f32[232,128]{1,0:T(8,128)S(1)} %get-tuple-element.52), channel_id=1, source_target_pairs={{0,1},{1,2},{2,3},{3,0},{4,5},{5,6},{6,7},{7,4},{8,9},{9,10},{10,1... | collective-permute-start | bytes 356360 | tf_op jit(solution)/shard_map/ppermute | solution.py:365
  18.5 1.7 %collective-permute-start.8 = (f32[232,128]{1,0:T(8,128)S(1)}, f32[232,128]{1,0:T(8,128)S(1)}, u32[]{:S(2)}, u32[]{:S(2)}) collective-permute-start(f32[232,128]{1,0:T(8,128)S(1)} %get-tuple-element.53), channel_id=1, source_target_pairs={{0,2},{1,3},{2,0},{3,1},{4,6},{5,7},{6,4},{7,5},{8,10},{9,11},{10,... | collective-permute-start | bytes 356360 | tf_op jit(solution)/shard_map/ppermute | solution.py:365
  20.2 1.0 %collective-permute-start.9 = (f32[232,128]{1,0:T(8,128)S(1)}, f32[232,128]{1,0:T(8,128)S(1)}, u32[]{:S(2)}, u32[]{:S(2)}) collective-permute-start(f32[232,128]{1,0:T(8,128)S(1)} %get-tuple-element.54), channel_id=1, source_target_pairs={{0,3},{1,0},{2,1},{3,2},{4,7},{5,4},{6,5},{7,6},{8,11},{9,8},{10,9... | collective-permute-start | bytes 356360 | tf_op jit(solution)/shard_map/ppermute | solution.py:365
  21.3 3.8 %collective-permute-start.3 = (f32[880,128]{1,0:T(8,128)S(1)}, f32[880,128]{1,0:T(8,128)S(1)}, u32[]{:S(2)}, u32[]{:S(2)}) collective-permute-start(f32[880,128]{1,0:T(8,128)S(1)} %bitcast.14), channel_id=1, source_target_pairs={{4,8},{8,4},{12,16},{16,12},{20,24},{24,20},{5,9},{9,5},{13,17},{1... | collective-permute-start | bytes 1351688 | tf_op jit(solution)/shard_map/ppermute | solution.py:373
  25.2 4.0 %collective-permute-done.8.refs_6_ = f32[232,128]{1,0:T(8,128)S(1)} collective-permute-done((f32[232,128]{1,0:T(8,128)S(1)}, f32[232,128]{1,0:T(8,128)S(1)}, u32[]{:S(2)}, u32[]{:S(2)}) %collective-permute-start.8) | collective-permute-done | bytes 118816 | tf_op jit(solution)/shard_map/ppermute | solution.py:365
  29.3 2.2 %collective-permute-done.9.refs_7_ = f32[232,128]{1,0:T(8,128)S(1)} collective-permute-done((f32[232,128]{1,0:T(8,128)S(1)}, f32[232,128]{1,0:T(8,128)S(1)}, u32[]{:S(2)}, u32[]{:S(2)}) %collective-permute-start.9) | collective-permute-done | bytes 118816 | tf_op jit(solution)/shard_map/ppermute | solution.py:365
  31.4 1.4 %shard_map.108 = (f32[224,512]{1,0:T(8,128)S(1)}, f32[224,128]{1,0:T(8,128)S(1)}, f32[224,128]{1,0:T(8,128)S(1)}, f32[224,128]{1,0:T(8,128)S(1)}, f32[224,128]{1,0:T(8,128)S(1)}, /*index=5*/f32[224,128]{1,0:T(8,128)S(1)}) custom-call(f32[232,128]{1,0:T(8,128)S(1)} %copy-done.2, f32[232,128]{1,0:T(8,128)S(1)} %collective-permute-done.4.refs_1_, ...), custom_call_target="tpu_custom_call" | custom-call | bytes 1755648 | tf_op jit(solution)/shard_map/pallas_call | solution.py:349
  32.8 3.1 %collective-permute-start.14 = (f32[224,512]{1,0:T(8,128)S(1)}, f32[224,512]{1,0:T(8,128)S(1)}, u32[]{:S(2)}, u32[]{:S(2)}) collective-permute-start(f32[224,512]{1,0:T(8,128)S(1)} %get-tuple-element.66.rel_ref), channel_id=1, source_target_pairs={{4,8},{8,4},{12,16},{16,12},{20,24},{24,20},{5,9},{9,5},{13,17},{1... | collective-permute-start | bytes 1376264 | tf_op jit(solution)/shard_map/ppermute | solution.py:373
  37.2 1.3 %collective-permute-start.10 = (f32[224,128]{1,0:T(8,128)S(1)}, f32[224,128]{1,0:T(8,128)S(1)}, u32[]{:S(2)}, u32[]{:S(2)}) collective-permute-start(f32[224,128]{1,0:T(8,128)S(1)} %get-tuple-element.63), channel_id=1, source_target_pairs={{0,1},{1,2},{2,3},{3,0},{4,5},{5,6},{6,7},{7,4},{8,9},{9,10},{10,1... | collective-permute-start | bytes 344072 | tf_op jit(solution)/shard_map/ppermute | solution.py:365
  38.5 1.9 %collective-permute-start.11 = (f32[224,128]{1,0:T(8,128)S(1)}, f32[224,128]{1,0:T(8,128)S(1)}, u32[]{:S(2)}, u32[]{:S(2)}) collective-permute-start(f32[224,128]{1,0:T(8,128)S(1)} %get-tuple-element.64), channel_id=1, source_target_pairs={{0,2},{1,3},{2,0},{3,1},{4,6},{5,7},{6,4},{7,5},{8,10},{9,11},{10,... | collective-permute-start | bytes 344072 | tf_op jit(solution)/shard_map/ppermute | solution.py:365
  40.4 6.4 %collective-permute-done.14.far_ref = f32[224,512]{1,0:T(8,128)S(1)} collective-permute-done((f32[224,512]{1,0:T(8,128)S(1)}, f32[224,512]{1,0:T(8,128)S(1)}, u32[]{:S(2)}, u32[]{:S(2)}) %collective-permute-start.14) | collective-permute-done | bytes 458784 | tf_op jit(solution)/shard_map/ppermute | solution.py:373
  46.8 2.5 %shard_map.110 = (f32[224,128]{1,0:T(8,128)S(1)}, f32[224,128]{1,0:T(8,128)S(1)}, f32[224,128]{1,0:T(8,128)S(1)}, f32[224,128]{1,0:T(8,128)S(1)}) custom-call(f32[224,512]{1,0:T(8,128)S(1)} %get-tuple-element.66.rel_ref, f32[224,128]{1,0:T(8,128)S(1)} %get-tuple-element.67.rim_ref, f32[224,512]{1,0:T(8,128)S(1)} %collective-permute-done.13.near_ref, ...), custom_call_target="tpu_custom_call" | custom-call | bytes 2550272 | tf_op jit(solution)/shard_map/pallas_call | solution.py:349
  49.5 2.7 %collective-permute-start.16 = (f32[224,128]{1,0:T(8,128)S(1)}, f32[224,128]{1,0:T(8,128)S(1)}, u32[]{:S(2)}, u32[]{:S(2)}) collective-permute-start(f32[224,128]{1,0:T(8,128)S(1)} %get-tuple-element.75), channel_id=1, source_target_pairs={{0,2},{1,3},{2,0},{3,1},{4,6},{5,7},{6,4},{7,5},{8,10},{9,11},{10,... | collective-permute-start | bytes 344072 | tf_op jit(solution)/shard_map/ppermute | solution.py:365
  52.5 0.9 %shard_map.109 = f32[880,128]{1,0:T(8,128)} custom-call(f32[224,128]{1,0:T(8,128)S(1)} %get-tuple-element.62.refs_0_, f32[224,128]{1,0:T(8,128)S(1)} %collective-permute-done.10.refs_1_, f32[224,128]{1,0:T(8,128)S(1)} %collective-permute-done.11.refs_2_, f32[224,128]{1,0:T(8,128)S(1)} %collective-permute-done.12.refs_3_), custom_call_target="tpu_custom_call" | custom-call | bytes 458752 | tf_op jit(solution)/shard_map/pallas_call | solution.py:349
  54.3 4.6 %collective-permute-done.16.refs_2_ = f32[224,128]{1,0:T(8,128)S(1)} collective-permute-done((f32[224,128]{1,0:T(8,128)S(1)}, f32[224,128]{1,0:T(8,128)S(1)}, u32[]{:S(2)}, u32[]{:S(2)}) %collective-permute-start.16) | collective-permute-done | bytes 114720 | tf_op jit(solution)/shard_map/ppermute | solution.py:365
  58.9 2.4 %collective-permute-done.17.refs_3_ = f32[224,128]{1,0:T(8,128)S(1)} collective-permute-done((f32[224,128]{1,0:T(8,128)S(1)}, f32[224,128]{1,0:T(8,128)S(1)}, u32[]{:S(2)}, u32[]{:S(2)}) %collective-permute-start.17) | collective-permute-done | bytes 114720 | tf_op jit(solution)/shard_map/ppermute | solution.py:365
  61.3 0.9 %shard_map.111 = f32[880,128]{1,0:T(8,128)} custom-call(f32[224,128]{1,0:T(8,128)S(1)} %get-tuple-element.73.refs_0_, f32[224,128]{1,0:T(8,128)S(1)} %collective-permute-done.15.refs_1_, f32[224,128]{1,0:T(8,128)S(1)} %collective-permute-done.16.refs_2_, f32[224,128]{1,0:T(8,128)S(1)} %collective-permute-done.17.refs_3_, f32[896,128]{1,0:T(8,128)S(1)} %shard_map.106.refs_4_), custom_call_target="tpu_custom_call" | custom-call | bytes 917504 | tf_op jit(solution)/shard_map/pallas_call | solution.py:349
  (38 shorter events, 3.8 us)
Async XLA Ops:
  0.6 15.9 %collective-permute-start.1 = (f32[880,128]{1,0:T(8,128)}, f32[880,128]{1,0:T(8,128)S(1)}, u32[]{:S(2)}, u32[]{:S(2)}) collective-permute-start(f32[880,128]{1,0:T(8,128)} %bitcast.10), channel_id=1, source_target_pairs={{4,8},{8,4},{12,16},{16,12},{20,24},{24,20},{5,9},{9,5},{13,17},{1... | collective-permute-start | bytes 1351688 | tf_op jit(solution)/shard_map/ppermute | solution.py:373
  4.3 12.2 %collective-permute-start = (f32[880,128]{1,0:T(8,128)}, f32[880,128]{1,0:T(8,128)S(1)}, u32[]{:S(2)}, u32[]{:S(2)}) collective-permute-start(f32[880,128]{1,0:T(8,128)} %bitcast.11), channel_id=1, source_target_pairs={{0,4},{4,0},{8,12},{12,8},{16,20},{20,16},{24,28},{28,24},{1,5},{5... | collective-permute-start | bytes 1351688 | tf_op jit(solution)/shard_map/ppermute | solution.py:374
  4.4 6.4 %copy-start.4 = (s32[512,9]{0,1:T(8,128)S(1)}, s32[512,9]{0,1:T(8,128)}, u32[]{:S(2)}) copy-start(s32[512,9]{0,1:T(8,128)} %param.16) | copy-start | bytes 55300
  4.4 6.4 %copy-start.5 = (s32[220,9]{0,1:T(8,128)S(1)}, s32[220,9]{0,1:T(8,128)}, u32[]{:S(2)}) copy-start(s32[220,9]{0,1:T(8,128)} %param.15) | copy-start | bytes 23764
  4.4 12.1 %copy-start = (f32[55,1,2048]{2,1,0:T(1,128)S(1)}, f32[55,1,2048]{2,1,0:T(1,128)}, u32[]{:S(2)}) copy-start(f32[55,1,2048]{2,1,0:T(1,128)} %param.9) | copy-start | bytes 1351684
  6.9 13.3 %collective-permute-start.4 = (f32[232,128]{1,0:T(8,128)}, f32[232,128]{1,0:T(8,128)S(1)}, u32[]{:S(2)}, u32[]{:S(2)}) collective-permute-start(f32[232,128]{1,0:T(8,128)} %get-tuple-element.48), channel_id=1, source_target_pairs={{0,1},{1,2},{2,3},{3,0},{4,5},{5,6},{6,7},{7,4},{8,9},{9,10},{10,1... | collective-permute-start | bytes 356360 | tf_op jit(solution)/shard_map/ppermute | solution.py:365
  8.3 13.0 %collective-permute-start.5 = (f32[232,128]{1,0:T(8,128)}, f32[232,128]{1,0:T(8,128)S(1)}, u32[]{:S(2)}, u32[]{:S(2)}) collective-permute-start(f32[232,128]{1,0:T(8,128)} %get-tuple-element.49), channel_id=1, source_target_pairs={{0,2},{1,3},{2,0},{3,1},{4,6},{5,7},{6,4},{7,5},{8,10},{9,11},{10,... | collective-permute-start | bytes 356360 | tf_op jit(solution)/shard_map/ppermute | solution.py:365
  9.4 15.8 %collective-permute-start.6 = (f32[232,128]{1,0:T(8,128)}, f32[232,128]{1,0:T(8,128)S(1)}, u32[]{:S(2)}, u32[]{:S(2)}) collective-permute-start(f32[232,128]{1,0:T(8,128)} %get-tuple-element.50), channel_id=1, source_target_pairs={{0,3},{1,0},{2,1},{3,2},{4,7},{5,4},{6,5},{7,6},{8,11},{9,8},{10,9... | collective-permute-start | bytes 356360 | tf_op jit(solution)/shard_map/ppermute | solution.py:365
  16.1 5.2 %copy-start.1 = (f32[55,1,2048]{2,1,0:T(1,128)S(1)}, f32[55,1,2048]{2,1,0:T(1,128)}, u32[]{:S(2)}) copy-start(f32[55,1,2048]{2,1,0:T(1,128)} %param.11) | copy-start | bytes 1351684
  16.1 15.4 %copy-start.2 = (f32[232,128]{1,0:T(8,128)S(1)}, f32[232,128]{1,0:T(8,128)}, u32[]{:S(2)}) copy-start(f32[232,128]{1,0:T(8,128)} %get-tuple-element.47.refs_0_) | copy-start | bytes 356356
  17.4 7.8 %collective-permute-start.7 = (f32[232,128]{1,0:T(8,128)S(1)}, f32[232,128]{1,0:T(8,128)S(1)}, u32[]{:S(2)}, u32[]{:S(2)}) collective-permute-start(f32[232,128]{1,0:T(8,128)S(1)} %get-tuple-element.52), channel_id=1, source_target_pairs={{0,1},{1,2},{2,3},{3,0},{4,5},{5,6},{6,7},{7,4},{8,9},{9,10},{10,1... | collective-permute-start | bytes 356360 | tf_op jit(solution)/shard_map/ppermute | solution.py:365
  18.5 10.8 %collective-permute-start.8 = (f32[232,128]{1,0:T(8,128)S(1)}, f32[232,128]{1,0:T(8,128)S(1)}, u32[]{:S(2)}, u32[]{:S(2)}) collective-permute-start(f32[232,128]{1,0:T(8,128)S(1)} %get-tuple-element.53), channel_id=1, source_target_pairs={{0,2},{1,3},{2,0},{3,1},{4,6},{5,7},{6,4},{7,5},{8,10},{9,11},{10,... | collective-permute-start | bytes 356360 | tf_op jit(solution)/shard_map/ppermute | solution.py:365
  20.2 11.2 %collective-permute-start.9 = (f32[232,128]{1,0:T(8,128)S(1)}, f32[232,128]{1,0:T(8,128)S(1)}, u32[]{:S(2)}, u32[]{:S(2)}) collective-permute-start(f32[232,128]{1,0:T(8,128)S(1)} %get-tuple-element.54), channel_id=1, source_target_pairs={{0,3},{1,0},{2,1},{3,2},{4,7},{5,4},{6,5},{7,6},{8,11},{9,8},{10,9... | collective-permute-start | bytes 356360 | tf_op jit(solution)/shard_map/ppermute | solution.py:365
  21.3 15.1 %collective-permute-start.3 = (f32[880,128]{1,0:T(8,128)S(1)}, f32[880,128]{1,0:T(8,128)S(1)}, u32[]{:S(2)}, u32[]{:S(2)}) collective-permute-start(f32[880,128]{1,0:T(8,128)S(1)} %bitcast.14), channel_id=1, source_target_pairs={{4,8},{8,4},{12,16},{16,12},{20,24},{24,20},{5,9},{9,5},{13,17},{1... | collective-permute-start | bytes 1351688 | tf_op jit(solution)/shard_map/ppermute | solution.py:373
  25.2 11.3 %collective-permute-start.2 = (f32[880,128]{1,0:T(8,128)S(1)}, f32[880,128]{1,0:T(8,128)S(1)}, u32[]{:S(2)}, u32[]{:S(2)}) collective-permute-start(f32[880,128]{1,0:T(8,128)S(1)} %bitcast.15), channel_id=1, source_target_pairs={{0,4},{4,0},{8,12},{12,8},{16,20},{20,16},{24,28},{28,24},{1,5},{5... | collective-permute-start | bytes 1351688 | tf_op jit(solution)/shard_map/ppermute | solution.py:374
  32.8 14.0 %collective-permute-start.14 = (f32[224,512]{1,0:T(8,128)S(1)}, f32[224,512]{1,0:T(8,128)S(1)}, u32[]{:S(2)}, u32[]{:S(2)}) collective-permute-start(f32[224,512]{1,0:T(8,128)S(1)} %get-tuple-element.66.rel_ref), channel_id=1, source_target_pairs={{4,8},{8,4},{12,16},{16,12},{20,24},{24,20},{5,9},{9,5},{13,17},{1... | collective-permute-start | bytes 1376264 | tf_op jit(solution)/shard_map/ppermute | solution.py:373
  36.0 10.8 %collective-permute-start.13 = (f32[224,512]{1,0:T(8,128)S(1)}, f32[224,512]{1,0:T(8,128)S(1)}, u32[]{:S(2)}, u32[]{:S(2)}) collective-permute-start(f32[224,512]{1,0:T(8,128)S(1)} %get-tuple-element.66.rel_ref), channel_id=1, source_target_pairs={{0,4},{4,0},{8,12},{12,8},{16,20},{20,16},{24,28},{28,24},{1,5},{5... | collective-permute-start | bytes 1376264 | tf_op jit(solution)/shard_map/ppermute | solution.py:374
  37.2 9.7 %copy-start.3 = (f32[1,2048]{1,0:T(1,128)S(1)}, f32[1,2048]{1,0:T(1,128)}, u32[]{:S(2)}) copy-start(f32[1,2048]{1,0:T(1,128)} %param.12) | copy-start | bytes 24580
  37.2 15.0 %collective-permute-start.10 = (f32[224,128]{1,0:T(8,128)S(1)}, f32[224,128]{1,0:T(8,128)S(1)}, u32[]{:S(2)}, u32[]{:S(2)}) collective-permute-start(f32[224,128]{1,0:T(8,128)S(1)} %get-tuple-element.63), channel_id=1, source_target_pairs={{0,1},{1,2},{2,3},{3,0},{4,5},{5,6},{6,7},{7,4},{8,9},{9,10},{10,1... | collective-permute-start | bytes 344072 | tf_op jit(solution)/shard_map/ppermute | solution.py:365
  38.5 14.0 %collective-permute-start.11 = (f32[224,128]{1,0:T(8,128)S(1)}, f32[224,128]{1,0:T(8,128)S(1)}, u32[]{:S(2)}, u32[]{:S(2)}) collective-permute-start(f32[224,128]{1,0:T(8,128)S(1)} %get-tuple-element.64), channel_id=1, source_target_pairs={{0,2},{1,3},{2,0},{3,1},{4,6},{5,7},{6,4},{7,5},{8,10},{9,11},{10,... | collective-permute-start | bytes 344072 | tf_op jit(solution)/shard_map/ppermute | solution.py:365
  40.4 12.1 %collective-permute-start.12 = (f32[224,128]{1,0:T(8,128)S(1)}, f32[224,128]{1,0:T(8,128)S(1)}, u32[]{:S(2)}, u32[]{:S(2)}) collective-permute-start(f32[224,128]{1,0:T(8,128)S(1)} %get-tuple-element.65), channel_id=1, source_target_pairs={{0,3},{1,0},{2,1},{3,2},{4,7},{5,4},{6,5},{7,6},{8,11},{9,8},{10,9... | collective-permute-start | bytes 344072 | tf_op jit(solution)/shard_map/ppermute | solution.py:365
  49.3 5.0 %collective-permute-start.15 = (f32[224,128]{1,0:T(8,128)S(1)}, f32[224,128]{1,0:T(8,128)S(1)}, u32[]{:S(2)}, u32[]{:S(2)}) collective-permute-start(f32[224,128]{1,0:T(8,128)S(1)} %get-tuple-element.74), channel_id=1, source_target_pairs={{0,1},{1,2},{2,3},{3,0},{4,5},{5,6},{6,7},{7,4},{8,9},{9,10},{10,1... | collective-permute-start | bytes 344072 | tf_op jit(solution)/shard_map/ppermute | solution.py:365
  49.5 9.5 %collective-permute-start.16 = (f32[224,128]{1,0:T(8,128)S(1)}, f32[224,128]{1,0:T(8,128)S(1)}, u32[]{:S(2)}, u32[]{:S(2)}) collective-permute-start(f32[224,128]{1,0:T(8,128)S(1)} %get-tuple-element.75), channel_id=1, source_target_pairs={{0,2},{1,3},{2,0},{3,1},{4,6},{5,7},{6,4},{7,5},{8,10},{9,11},{10,... | collective-permute-start | bytes 344072 | tf_op jit(solution)/shard_map/ppermute | solution.py:365
  52.2 9.1 %collective-permute-start.17 = (f32[224,128]{1,0:T(8,128)S(1)}, f32[224,128]{1,0:T(8,128)S(1)}, u32[]{:S(2)}, u32[]{:S(2)}) collective-permute-start(f32[224,128]{1,0:T(8,128)S(1)} %get-tuple-element.76), channel_id=1, source_target_pairs={{0,3},{1,0},{2,1},{3,2},{4,7},{5,4},{6,5},{7,6},{8,11},{9,8},{10,9... | collective-permute-start | bytes 344072 | tf_op jit(solution)/shard_map/ppermute | solution.py:365
  (3 other events, 5.2 us)

commit v3 on v2

--- a/solution.py
+++ b/solution.py
@@ -78,19 +78,26 @@
 
 def source_kernel(parts, modes, padded, v_hbm, j_hbm, a_hbm, *rest):
     outs, (grouped, v_ref, j_ref, a_ref, sems) = rest[:-5], rest[-5:]
-    pairs = ((v_hbm, v_ref), (j_hbm, j_ref), (a_hbm, a_ref))
+    groups = a_ref.shape[0]
+    starts = range(0, modes, SUB)
+    pairs = [(a_hbm, a_ref)]
+    for start in starts:
+        rows = pl.ds(start * groups, min(SUB, modes - start) * groups)
+        pairs += [(v_hbm.at[rows], v_ref.at[rows]), (j_hbm.at[rows], j_ref.at[rows])]
     copies = [pltpu.make_async_copy(x, y, sems.at[i]) for i, (x, y) in enumerate(pairs)]
     for copy in copies:
         copy.start()
-    for copy in copies:
-        copy.wait()
-    me = lax.axis_index("modes")
-    groups = a_ref.shape[0]
+    me = lax.axis_index("modes")
+    copies[0].wait()
     factor = 0.8 / (6.0 * a_ref[...])
-    for g in range(groups):
-        w = load_group(v_ref, g, modes, groups)
-        w = w + load_group(j_ref, g, modes, groups) * factor[g : g + 1]
-        grouped[g * padded : (g + 1) * padded, :] = pad_rows(w, padded)
+    for tile, start in enumerate(starts):
+        copies[2 * tile + 1].wait()
+        copies[2 * tile + 2].wait()
+        count = min(SUB, modes - start)
+        for g in range(groups):
+            rows = pl.ds(start * groups + g, count, stride=groups)
+            w = v_ref[rows, :] + j_ref[rows, :] * factor[g : g + 1]
+            grouped[g * padded + start : g * padded + start + SUB, :] = pad_rows(w, SUB)
     emit_slots(me, parts, grouped, outs, padded)
 
 
@@ -139,6 +146,7 @@
     rows = parts * padded
     points = nodes_ref.shape[1]
     me = lax.axis_index("modes")
+    kinds = 4 * TILE16
 
     slot = lax.broadcasted_iota(jnp.int32, (rows, all_modes), 0)
     mode = lax.broadcasted_iota(jnp.int32, (rows, all_modes), 1)
@@ -146,12 +154,44 @@
     pick = (within < modes) & (mode == slot // padded * modes + within)
     pick = jnp.where(pick, 1.0, 0.0).astype(BF16)
     table = table_ref[...].astype(F32).astype(BF16)
+    spread = lax.broadcasted_iota(jnp.int32, (kinds, npar), 0) % TILE16
+    spread = spread == lax.broadcasted_iota(jnp.int32, (kinds, npar), 1)
+    table = dot(jnp.where(spread, 1.0, 0.0).astype(BF16), table).astype(BF16)
     along = dot_nt(table, pick)
-    lane_pad = lane_ids(along.shape) % padded >= modes
-    along = jnp.where(lane_pad, -50.0, along)
     down = dot_nt(pick, table)
-    row_pad = lax.broadcasted_iota(jnp.int32, down.shape, 0) % padded >= modes
-    cols[...] = jnp.where(row_pad, -50.0, down)
+    cols[...] = down
+
+    def one_hot(values, axis):
+        kind = lax.broadcasted_iota(jnp.int32, values.shape, axis)
+        row = lax.broadcasted_iota(jnp.int32, values.shape, 1 - axis)
+        hit = (values == (kind // TILE16).astype(F32)) & (kind % TILE16 < npar)
+        return jnp.where(hit & (row % padded < modes), 1.0, 0.0).astype(BF16)
+
+    hot_down, hot_along = one_hot(down, 1), one_hot(along, 0)
+    agree = dot(hot_down, hot_along)
+    degree_down = jnp.sum(down[:, :TILE16], axis=1, keepdims=True)
+    degree_along = jnp.sum(along[:TILE16], axis=0, keepdims=True)
+    linked = (agree == npar - 1.0) & (jnp.abs(degree_down - degree_along) == 1.0)
+    same = agree == float(npar)
+    left = lax.broadcasted_iota(jnp.int32, (kinds, kinds), 0)
+    right = lax.broadcasted_iota(jnp.int32, (kinds, kinds), 1)
+    step = (left % TILE16 == right % TILE16) & (jnp.abs(left // TILE16 - right // TILE16) == 1)
+    root = jnp.where(step, jnp.sqrt((jnp.maximum(left, right) // TILE16).astype(F32)), 0.0)
+    param = lax.broadcasted_iota(jnp.int32, (1, kinds), 1) % TILE16
+    hot3 = jnp.concatenate([hot_along] * 3, axis=0)
+    for r in range(nreg):
+        weight = jnp.zeros((1, kinds), F32)
+        for m in range(npar):
+            weight = jnp.where(param == m, z_ref[r, m], weight)
+        link = root * weight
+        high = link.astype(BF16)
+        mid = (link - high.astype(F32)).astype(BF16)
+        low = (link - high.astype(F32) - mid.astype(F32)).astype(BF16)
+        part = dot(hot_down, jnp.concatenate([high, mid, low], axis=1)).astype(BF16)
+        matrix = jnp.where(linked, dot(part, hot3), jnp.where(same, 1.0, 0.0))
+        high, low = split2(matrix)
+        ah_ref[r * rows : (r + 1) * rows, :] = high
+        al_ref[r * rows : (r + 1) * rows, :] = low
 
     nodes = nodes_ref[...]
     t = jnp.zeros(nodes.shape, F32)
@@ -160,36 +200,27 @@
     h2 = (t * t - 1.0) * (1.0 / 2.0**0.5)
     h3 = (t * t * t - 3.0 * t) * (1.0 / 6.0**0.5)
     share = share_ref[...].astype(F32) * (0.25 / (512.0 * points * all_modes))
+    tiles = points // LANES
 
     def block(b, carry):
         at = pl.multiple_of(b * TILE16, TILE16)
         mine = cols[pl.ds(at, TILE16), :]
-        count = jnp.zeros((TILE16, rows), F32)
-        larger = jnp.zeros((TILE16, rows), F32)
-        weight = [jnp.zeros((TILE16, rows), F32) for _ in range(nreg)]
-        basis = jnp.ones((TILE16, points), F32)
+        row = lax.broadcasted_iota(jnp.int32, (TILE16, LANES), 0) + at
+        basis = [jnp.where(row % padded < modes, 1.0, 0.0)] * tiles
         for m in range(npar):
-            own = mine[:, m : m + 1]
-            other = along[m : m + 1, :]
-            gap = jnp.abs(own - other)
-            count = count + jnp.where(gap != 0.0, 1.0, 0.0)
-            one = gap == 1.0
-            larger = jnp.where(one, jnp.maximum(own, other), larger)
-            weight = [jnp.where(one, z_ref[r, m], weight[r]) for r in range(nreg)]
-            factor = jnp.where(own == 0.0, 1.0, 0.0) + jnp.where(own == 1.0, t[m : m + 1], 0.0)
-            factor = factor + jnp.where(own == 2.0, h2[m : m + 1], 0.0)
-            factor = factor + jnp.where(own == 3.0, h3[m : m + 1], 0.0)
-            basis = basis * factor
-        root = jnp.where(count == 1.0, jnp.sqrt(larger), 0.0)
-        for r in range(nreg):
-            high, low = split2(jnp.where(count == 0.0, 1.0, root * weight[r]))
-            spot = pl.multiple_of(r * rows + at, TILE16)
-            ah_ref[pl.ds(spot, TILE16), :] = high
-            al_ref[pl.ds(spot, TILE16), :] = low
-        basis_t[pl.ds(at, TILE16), :] = basis
-        high, low = split2(basis * share)
-        wh_ref[pl.ds(at, TILE16), :] = high
-        wl_ref[pl.ds(at, TILE16), :] = low
+            own = jnp.broadcast_to(mine[:, m : m + 1], (TILE16, LANES))
+            is0, is1, is2 = own == 0.0, own == 1.0, own == 2.0
+            for i in range(tiles):
+                lanes = slice(i * LANES, (i + 1) * LANES)
+                factor = jnp.where(is2, h2[m : m + 1, lanes], h3[m : m + 1, lanes])
+                factor = jnp.where(is1, t[m : m + 1, lanes], factor)
+                basis[i] = basis[i] * jnp.where(is0, 1.0, factor)
+        for i in range(tiles):
+            lanes = slice(i * LANES, (i + 1) * LANES)
+            basis_t[pl.ds(at, TILE16), lanes] = basis[i]
+            high, low = split2(basis[i] * share[:, lanes])
+            wh_ref[pl.ds(at, TILE16), lanes] = high
+            wl_ref[pl.ds(at, TILE16), lanes] = low
         return carry
 
     lax.fori_loop(0, rows // TILE16, block, 0)
@@ -227,14 +258,12 @@
     zones_ref[:, per * LANES :] = jnp.where(lane_ids(low.shape) < NZ, low, high)
 
 
-def couple_kernel(
-    parts, padded, per, nreg, *refs
-):
+def couple_kernel(parts, padded, per, nreg, halves, *refs):
     w_refs = refs[:parts]
     r_refs = refs[parts : 2 * parts]
     ah_ref, al_ref, zones_ref = refs[2 * parts : 2 * parts + 3]
-    rel_ref, rim_ref = refs[2 * parts + 3 : 2 * parts + 5]
-    outs = refs[2 * parts + 5 : -2]
+    rel_refs = refs[2 * parts + 3 : 2 * parts + 3 + halves]
+    rim_ref, *outs = refs[2 * parts + 3 + halves : -2]
     w_all, r_all = refs[-2:]
     me = lax.axis_index("modes")
     rows = parts * padded
@@ -261,7 +290,8 @@
         a_low = al_ref[r * rows : (r + 1) * rows, :]
         applied = jnp.where(zones == r, dot3(a_high, a_low, r_high, r_low), applied)
     w_all[...] = w_all[...] - (0.8 / 6.0) * applied
-    rel_ref[...] = w_all[:, :width]
+    for h, rel_ref in enumerate(rel_refs):
+        rel_ref[...] = w_all[:, h * width // halves : (h + 1) * width // halves]
     rim_ref[...] = w_all[:, width:]
     for k, out in enumerate(outs):
         target = lax.rem(me + k, parts)
@@ -272,44 +302,55 @@
             ]
 
 
-def joule_kernel(
-    parts, padded, per, nreg, rel_ref, rim_ref, near_ref, far_ref, a_ref, zones_ref,
-    bh_ref, bl_ref, wh_ref, wl_ref, lift_ref, *rest,
-):
-    outs, heat_ref = rest[:-1], rest[-1]
-    me = lax.axis_index("modes")
-    width = per * LANES
-    rel = rel_ref[...]
+def plane_kernel(nreg, halves, *refs):
+    rel_refs, (rim_ref, zones_ref, bh_ref, bl_ref, lift_ref, part_ref, spread_ref) = (
+        refs[:halves], refs[halves:],
+    )
+    width = sum(ref.shape[1] for ref in rel_refs)
+    rel = jnp.concatenate([ref[...] for ref in rel_refs], axis=1)
     rim = rim_ref[...]
     lane = lane_ids(rel.shape)
     depth = lane % NZ
-    wide = jnp.concatenate([rim] + [jnp.zeros_like(rim)] * (per - 1), axis=1)
+    wide = jnp.concatenate([rim, jnp.zeros((rim.shape[0], width - LANES), F32)], axis=1)
     along_z = jnp.where(depth < NZ - 1, pltpu.roll(rel, width - 1, 1), 0.0)
     along_z = along_z - jnp.where(depth > 0, pltpu.roll(rel, 1, 1), 0.0)
     after = pltpu.roll(wide, width - 2 * NZ, 1)
     along_y = jnp.where(lane >= width - NZ, after, pltpu.roll(rel, width - NZ, 1))
     along_y = along_y - jnp.where(lane < NZ, wide, pltpu.roll(rel, NZ, 1))
-    along_x = far_ref[...] - near_ref[...]
     b_high, b_low = bh_ref[...], bl_ref[...]
     total = None
-    for grad in (along_y, along_z, along_x):
+    for grad in (along_y, along_z):
         g_high, g_low = split2(grad)
         at_point = dot3(b_high, b_low, g_high, g_low)
         total = at_point * at_point if total is None else total + at_point * at_point
-    zones = zones_ref[:, :width]
     row = lax.broadcasted_iota(jnp.int32, (LANES, width), 0)
-    hot = (row < 3 * nreg) & (row % nreg == zones)
+    hot = (row < 3 * nreg) & (row % nreg == zones_ref[:, :width])
     spread = dot(lift_ref[...], jnp.where(hot, 1.0, 0.0).astype(BF16))
-    j_high, j_low = split2(spread * total)
+    spread_ref[...] = spread
+    part_ref[...] = spread * total
+
+
+def joule_kernel(
+    parts, padded, per, halves, half, near_ref, far_ref, part_ref, spread_ref, a_ref,
+    bh_ref, bl_ref, wh_ref, wl_ref, *rest,
+):
+    outs, heat_ref = rest[:-1], rest[-1]
+    me = lax.axis_index("modes")
+    own = per // halves
+    lanes = slice(half * own * LANES, (half + 1) * own * LANES)
+    g_high, g_low = split2(far_ref[...] - near_ref[...])
+    at_point = dot3(bh_ref[...], bl_ref[...], g_high, g_low)
+    joule = part_ref[:, lanes] + spread_ref[:, lanes] * (at_point * at_point)
+    j_high, j_low = split2(joule)
     heat = dot3(wh_ref[...], wl_ref[...], j_high, j_low)
-    for s in range(per):
+    for s in range(own):
         heat_ref[:, s * LANES : (s + 1) * LANES] = (
-            heat[:, s * LANES : (s + 1) * LANES] * a_ref[pl.ds(me * per + s, 1), :]
+            heat[:, s * LANES : (s + 1) * LANES] * a_ref[pl.ds(me * per + half * own + s, 1), :]
         )
     for k, out in enumerate(outs):
         target = lax.rem(me + k, parts)
         at = pl.multiple_of(target * padded, SUB)
-        for s in range(per):
+        for s in range(own):
             out[s * padded : (s + 1) * padded, :] = heat_ref[
                 pl.ds(at, padded), s * LANES : (s + 1) * LANES
             ]
@@ -325,14 +366,17 @@
             out[pl.ds(q * per + s, modes, stride=parts * per), :] = rows
 
 
-def final_kernel(parts, modes, padded, per, *refs):
-    chunks, base, out = refs[:parts], refs[parts], refs[parts + 1]
-    me = lax.axis_index("modes")
+def final_kernel(parts, modes, padded, per, halves, *refs):
+    chunks, base, out = refs[: parts * halves], refs[-2], refs[-1]
+    me = lax.axis_index("modes")
+    own = per // halves
     for k in range(parts):
         q = lax.rem(me + (parts - k), parts)
         for s in range(per):
+            chunk = chunks[s // own * parts + k]
             at = pl.multiple_of((q * per + s) * padded, SUB)
-            rows = base[pl.ds(at, padded), :] + 0.1 * chunks[k][s * padded : (s + 1) * padded, :]
+            within = s % own * padded
+            rows = base[pl.ds(at, padded), :] + 0.1 * chunk[within : within + padded, :]
             out[pl.ds(q * per + s, modes, stride=parts * per), :] = rows[:modes]
 
 
@@ -392,8 +436,10 @@
     groups = columns // LANES
     per = groups // parts
     padded = -(-modes // SUB) * SUB
+    halves = 1
     rows = parts * padded
     assert planes == 1 and groups * LANES == columns and per * parts == groups
+    assert polynomial_exponent_rows.shape[1] <= TILE16 and points % LANES == 0
     assert rows % TILE16 == 0 and 2 * NZ * padded <= SUB * LANES and 3 * nreg <= LANES
 
     def flat(x):
@@ -415,11 +461,12 @@
         functools.partial(source_kernel, parts, modes, padded),
         [rimmed] * parts,
         [v, cur, avg],
-        [grouped, fields, fields, pltpu.VMEM((groups, LANES), F32), pltpu.SemaphoreType.DMA((3,))],
+        [grouped, fields, fields, pltpu.VMEM((groups, LANES), F32), pltpu.SemaphoreType.DMA((1 + 2 * (padded // SUB),))],
         hbm=(0, 1, 2),
         limit=62 * 1024 * 1024,
     )
     source = exchange(source)
+    temp, source[1] = lax.optimization_barrier((temp, source[1]))
     a_high, a_low, b_high, b_low, w_high, w_low, lift, zones = call(
         functools.partial(tables_kernel, parts, modes, padded),
         [
@@ -439,7 +486,7 @@
             zone_relative_response,
             zone,
         ],
-        [pltpu.VMEM((rows, polynomial_exponent_rows.shape[1]), F32), pltpu.VMEM((rows, points), F32)],
+        [pltpu.VMEM((rows, 4 * TILE16), F32), pltpu.VMEM((rows, points), F32)],
         smem=(3,),
     )
     v, zones = lax.optimization_barrier((v, zones))
@@ -447,36 +494,44 @@
         functools.partial(rough_kernel, parts, modes, padded, groups),
         [rimmed] * parts, [v, v_near, v_far], [grouped],
     )
-    temp_after, *rough = lax.optimization_barrier((temp, *rough))
     rough = exchange(rough)
-    t_near, t_far = halo(temp_after)
+    t_near, t_far = halo(temp)
     base = call(
         functools.partial(thermal_kernel, modes, padded, groups),
         struct(groups * padded, LANES), [temp, t_near, t_far],
     )
     wide = (per + 1) * LANES
-    relaxed, rim, *back = call(
-        functools.partial(couple_kernel, parts, padded, per, nreg),
-        [struct(rows, per * LANES), struct(rows, LANES)] + [chunk] * parts,
+    half_width = per * LANES // halves
+    results = call(
+        functools.partial(couple_kernel, parts, padded, per, nreg, halves),
+        [struct(rows, half_width)] * halves + [struct(rows, LANES)] + [chunk] * parts,
         [*source, *rough, a_high, a_low, zones],
         [pltpu.VMEM((rows, wide), F32), pltpu.VMEM((rows, wide), F32)],
     )
-    x_near, x_far = halo(relaxed)
+    relaxed, rim, back = results[:halves], results[halves], results[halves + 1 :]
+    beside = [halo(x) for x in relaxed]
     base, *back = lax.optimization_barrier((base, *back))
     back = exchange(back)
-    heat = call(
-        functools.partial(joule_kernel, parts, padded, per, nreg),
-        [chunk] * parts,
-        [relaxed, rim, x_near, x_far, avg, zones, b_high, b_low, w_high, w_low, lift],
-        [pltpu.VMEM((rows, per * LANES), F32)],
-    )
-    heat = exchange(heat)
+    part, spread = call(
+        functools.partial(plane_kernel, nreg, halves),
+        [struct(points, per * LANES)] * 2,
+        [*relaxed, rim, zones, b_high, b_low, lift],
+    )
+    heat = []
+    for half in range(halves):
+        pieces = call(
+            functools.partial(joule_kernel, parts, padded, per, halves, half),
+            [struct(per // halves * padded, LANES)] * parts,
+            [*beside[half], part, spread, avg, b_high, b_low, w_high, w_low],
+            [pltpu.VMEM((rows, half_width), F32)],
+        )
+        heat += exchange(pieces)
     relaxed_voltage = call(
         functools.partial(gather_kernel, parts, modes, padded, per),
         struct(modes * groups, LANES), back,
     )
     advanced = call(
-        functools.partial(final_kernel, parts, modes, padded, per),
+        functools.partial(final_kernel, parts, modes, padded, per, halves),
         struct(modes * groups, LANES), [*heat, base],
     )
     shape = voltage_expansion.shape

time: 62.4 us -> 60.6 us (0.971)
  waiting for transfers between devices: 21.3 us -> 20.1 us
  Pallas kernels: 14.4 us -> 13.5 us
    ppermute x12, waiting for transfers between devices: 14.1 us -> 10.5 us  [exchange(): received.append(lax.ppermute(chunks[k], 'modes', pairs))]
    ppermute x12, starting transfers between devices: 14.1 us -> 11.5 us  [exchange(): received.append(lax.ppermute(chunks[k], 'modes', pairs))]
    ppermute x3, waiting for transfers between devices: 7.21 us -> 9.62 us  [halo(): far = lax.ppermute(x, 'space', far)]
    ppermute x3, starting transfers between devices: 10.7 us -> 12.9 us  [halo(): far = lax.ppermute(x, 'space', far)]
    pallas_call x8 -> x9, Pallas kernels: 14.4 us -> 13.5 us  [call(): pl.pallas_call(kernel, out_shape=out_shape, in_specs=specs, out_specs=[vm...]
    ppermute x3, starting transfers between devices: 0.21 us -> 0.89 us  [halo(): return (lax.ppermute(x, 'space', near), far)]
  transfers between devices with their start and end apart: 18 -> 18, of which waited for: 8 -> 8; matrix products, arithmetic and copies ran while one was open for 0% -> 0% of each run, Pallas kernels for 22% -> 21%
where the time goes in v3:
time: 60.6 us; the launch traced here: 60.4 us
  starting transfers between devices  25.2 us (42%)
  waiting for transfers between devices  20.1 us (33%)
  Pallas kernels  13.5 us (22%)
  between operations  0.83 us (1%)
  local copies, waits for them, and re-layouts  0.71 us (1%)
    pallas_call x9, Pallas kernels, call(): pl.pallas_call(kernel, out_shape=out_shape, in_specs=specs, out_specs=[vm...  13.5 us
    ppermute x3, starting transfers between devices, halo(): far = lax.ppermute(x, 'space', far)  12.9 us
    ppermute x12, starting transfers between devices, exchange(): received.append(lax.ppermute(chunks[k], 'modes', pairs))  11.5 us
    ppermute x12, waiting for transfers between devices, exchange(): received.append(lax.ppermute(chunks[k], 'modes', pairs))  10.5 us
    ppermute x3, waiting for transfers between devices, halo(): far = lax.ppermute(x, 'space', far)  9.62 us
  transfers between devices with their start and end apart: 18, of which 8 were waited for; matrix products, arithmetic and copies ran while one was open for 0% of the time, Pallas kernels for 21%

profile of v3, /device:TPU:11, one launch (start us, length us, event | category | flops | bytes accessed | tf_op | source)
XLA Modules:
  0.0 60.4 jit_solution(4847396735384895936)
XLA Ops:
  1.4 3.0 %collective-permute-start.6 = (f32[880,128]{1,0:T(8,128)}, f32[880,128]{1,0:T(8,128)S(1)}, u32[]{:S(2)}, u32[]{:S(2)}) collective-permute-start(f32[880,128]{1,0:T(8,128)} %bitcast.11), channel_id=1, source_target_pairs={{4,8},{8,4},{12,16},{16,12},{20,24},{24,20},{5,9},{9,5},{13,17},{1... | collective-permute-start | bytes 1351688 | tf_op jit(solution)/shard_map/ppermute | solution.py:417
  4.4 2.4 %shard_map.104 = (f32[232,128]{1,0:T(8,128)}, f32[232,128]{1,0:T(8,128)}, f32[232,128]{1,0:T(8,128)}, f32[232,128]{1,0:T(8,128)}) custom-call(f32[880,128]{1,0:T(8,128)} %bitcast.12, f32[880,128]{1,0:T(8,128)} %bitcast.23, f32[16,128]{1,0:T(8,128)} %bitcast.17), custom_call_target="tpu_custom_call" | custom-call | bytes 909312 | tf_op jit(solution)/shard_map/pallas_call | solution.py:393
  6.9 1.3 %collective-permute-start = (f32[232,128]{1,0:T(8,128)}, f32[232,128]{1,0:T(8,128)S(1)}, u32[]{:S(2)}, u32[]{:S(2)}) collective-permute-start(f32[232,128]{1,0:T(8,128)} %get-tuple-element.39), channel_id=1, source_target_pairs={{0,1},{1,2},{2,3},{3,0},{4,5},{5,6},{6,7},{7,4},{8,9},{9,10},{10,1... | collective-permute-start | bytes 356360 | tf_op jit(solution)/shard_map/ppermute | solution.py:409
  8.2 1.1 %collective-permute-start.3 = (f32[232,128]{1,0:T(8,128)}, f32[232,128]{1,0:T(8,128)S(1)}, u32[]{:S(2)}, u32[]{:S(2)}) collective-permute-start(f32[232,128]{1,0:T(8,128)} %get-tuple-element.43), channel_id=1, source_target_pairs={{0,2},{1,3},{2,0},{3,1},{4,6},{5,7},{6,4},{7,5},{8,10},{9,11},{10,... | collective-permute-start | bytes 356360 | tf_op jit(solution)/shard_map/ppermute | solution.py:409
  9.3 1.4 %collective-permute-start.4 = (f32[232,128]{1,0:T(8,128)}, f32[232,128]{1,0:T(8,128)S(1)}, u32[]{:S(2)}, u32[]{:S(2)}) collective-permute-start(f32[232,128]{1,0:T(8,128)} %get-tuple-element.44), channel_id=1, source_target_pairs={{0,3},{1,0},{2,1},{3,2},{4,7},{5,4},{6,5},{7,6},{8,11},{9,8},{10,9... | collective-permute-start | bytes 356360 | tf_op jit(solution)/shard_map/ppermute | solution.py:409
  11.4 3.6 %shard_map.106 = (bf16[896,224]{1,0:T(8,128)(2,1)S(1)}, bf16[896,224]{1,0:T(8,128)(2,1)S(1)}, bf16[512,224]{1,0:T(8,128)(2,1)S(1)}, bf16[512,224]{1,0:T(8,128)(2...) custom-call(s32[9,220]{1,0:T(8,128)S(1)} %bitcast.20, ...), custom_call_target="tpu_custom_call" | custom-call | bytes 36736 | tf_op jit(solution)/shard_map/pallas_call | solution.py:393
  15.0 1.4 %collective-permute-done.6.far_ref = f32[880,128]{1,0:T(8,128)S(1)} collective-permute-done((f32[880,128]{1,0:T(8,128)}, f32[880,128]{1,0:T(8,128)S(1)}, u32[]{:S(2)}, u32[]{:S(2)}) %collective-permute-start.6) | collective-permute-done | bytes 450592 | tf_op jit(solution)/shard_map/ppermute | solution.py:417
  17.3 1.4 %collective-permute-start.7 = (f32[232,128]{1,0:T(8,128)S(1)}, f32[232,128]{1,0:T(8,128)S(1)}, u32[]{:S(2)}, u32[]{:S(2)}) collective-permute-start(f32[232,128]{1,0:T(8,128)S(1)} %get-tuple-element.48), channel_id=1, source_target_pairs={{0,1},{1,2},{2,3},{3,0},{4,5},{5,6},{6,7},{7,4},{8,9},{9,10},{10,1... | collective-permute-start | bytes 356360 | tf_op jit(solution)/shard_map/ppermute | solution.py:409
  18.7 1.4 %collective-permute-start.8 = (f32[232,128]{1,0:T(8,128)S(1)}, f32[232,128]{1,0:T(8,128)S(1)}, u32[]{:S(2)}, u32[]{:S(2)}) collective-permute-start(f32[232,128]{1,0:T(8,128)S(1)} %get-tuple-element.49), channel_id=1, source_target_pairs={{0,2},{1,3},{2,0},{3,1},{4,6},{5,7},{6,4},{7,5},{8,10},{9,11},{10,... | collective-permute-start | bytes 356360 | tf_op jit(solution)/shard_map/ppermute | solution.py:409
  20.1 1.4 %collective-permute-start.9 = (f32[232,128]{1,0:T(8,128)S(1)}, f32[232,128]{1,0:T(8,128)S(1)}, u32[]{:S(2)}, u32[]{:S(2)}) collective-permute-start(f32[232,128]{1,0:T(8,128)S(1)} %get-tuple-element.50), channel_id=1, source_target_pairs={{0,3},{1,0},{2,1},{3,2},{4,7},{5,4},{6,5},{7,6},{8,11},{9,8},{10,9... | collective-permute-start | bytes 356360 | tf_op jit(solution)/shard_map/ppermute | solution.py:409
  21.5 6.7 %collective-permute-start.2 = (f32[880,128]{1,0:T(8,128)S(1)}, f32[880,128]{1,0:T(8,128)S(1)}, u32[]{:S(2)}, u32[]{:S(2)}) collective-permute-start(f32[880,128]{1,0:T(8,128)S(1)} %bitcast.15), channel_id=1, source_target_pairs={{4,8},{8,4},{12,16},{16,12},{20,24},{24,20},{5,9},{9,5},{13,17},{1... | collective-permute-start | bytes 1351688 | tf_op jit(solution)/shard_map/ppermute | solution.py:417
  28.2 1.1 %collective-permute-done.8.refs_6_ = f32[232,128]{1,0:T(8,128)S(1)} collective-permute-done((f32[232,128]{1,0:T(8,128)S(1)}, f32[232,128]{1,0:T(8,128)S(1)}, u32[]{:S(2)}, u32[]{:S(2)}) %collective-permute-start.8) | collective-permute-done | bytes 118816 | tf_op jit(solution)/shard_map/ppermute | solution.py:409
  29.3 1.9 %collective-permute-done.9.refs_7_ = f32[232,128]{1,0:T(8,128)S(1)} collective-permute-done((f32[232,128]{1,0:T(8,128)S(1)}, f32[232,128]{1,0:T(8,128)S(1)}, u32[]{:S(2)}, u32[]{:S(2)}) %collective-permute-start.9) | collective-permute-done | bytes 118816 | tf_op jit(solution)/shard_map/ppermute | solution.py:409
  31.2 1.4 %shard_map.108 = (f32[224,512]{1,0:T(8,128)S(1)}, f32[224,128]{1,0:T(8,128)S(1)}, f32[224,128]{1,0:T(8,128)S(1)}, f32[224,128]{1,0:T(8,128)S(1)}, f32[224,128]{1,0:T(8,128)S(1)}, /*index=5*/f32[224,128]{1,0:T(8,128)S(1)}) custom-call(f32[232,128]{1,0:T(8,128)S(1)} %copy-done.2, f32[232,128]{1,0:T(8,128)S(1)} %collective-permute-done.refs_1_, ...), custom_call_target="tpu_custom_call" | custom-call | bytes 1755648 | tf_op jit(solution)/shard_map/pallas_call | solution.py:393
  32.8 3.1 %collective-permute-start.14 = (f32[224,512]{1,0:T(8,128)S(1)}, f32[224,512]{1,0:T(8,128)S(1)}, u32[]{:S(2)}, u32[]{:S(2)}) collective-permute-start(f32[224,512]{1,0:T(8,128)S(1)} %get-tuple-element.62.refs_0_), channel_id=1, source_target_pairs={{4,8},{8,4},{12,16},{16,12},{20,24},{24,20},{5,9},{9,5},{13,17},{1... | collective-permute-start | bytes 1376264 | tf_op jit(solution)/shard_map/ppermute | solution.py:417
  36.0 3.1 %collective-permute-done.2.far_ref = f32[880,128]{1,0:T(8,128)S(1)} collective-permute-done((f32[880,128]{1,0:T(8,128)S(1)}, f32[880,128]{1,0:T(8,128)S(1)}, u32[]{:S(2)}, u32[]{:S(2)}) %collective-permute-start.2) | collective-permute-done | bytes 450592 | tf_op jit(solution)/shard_map/ppermute | solution.py:417
  41.3 1.5 %shard_map.110 = (f32[512,512]{1,0:T(8,128)S(1)}, f32[512,512]{1,0:T(8,128)S(1)}) custom-call(f32[224,512]{1,0:T(8,128)S(1)} %get-tuple-element.62.refs_0_, f32[224,128]{1,0:T(8,128)S(1)} %get-tuple-element.63.refs_1_, s32[1,640]{1,0:T(1,128)S(1)} %get-tuple-element.53.refs_10_.refs_2_, bf16[512,224]{1,0:T(8,128)(2,1)S(1)} %get-tuple-element.64.refs_3_.bh_ref, ...), custom_call_target="tpu_custom_call" | custom-call | bytes 1165824 | tf_op jit(solution)/shard_map/pallas_call | solution.py:393
  42.8 5.1 %collective-permute-done.14.far_ref = f32[224,512]{1,0:T(8,128)S(1)} collective-permute-done((f32[224,512]{1,0:T(8,128)S(1)}, f32[224,512]{1,0:T(8,128)S(1)}, u32[]{:S(2)}, u32[]{:S(2)}) %collective-permute-start.14) | collective-permute-done | bytes 458784 | tf_op jit(solution)/shard_map/ppermute | solution.py:417
  48.0 1.1 %shard_map.111 = (f32[224,128]{1,0:T(8,128)S(1)}, f32[224,128]{1,0:T(8,128)S(1)}, f32[224,128]{1,0:T(8,128)S(1)}, f32[224,128]{1,0:T(8,128)S(1)}) custom-call(f32[224,512]{1,0:T(8,128)S(1)} %collective-permute-done.13.near_ref, f32[224,512]{1,0:T(8,128)S(1)} %collective-permute-done.14.far_ref, f32[512,512]{1,0:T(8,128)S(1)} %get-tuple-element.67.part_ref, ...), custom_call_target="tpu_custom_call" | custom-call | bytes 3940352 | tf_op jit(solution)/shard_map/pallas_call | solution.py:393
  49.2 1.1 %collective-permute-start.16 = (f32[224,128]{1,0:T(8,128)S(1)}, f32[224,128]{1,0:T(8,128)S(1)}, u32[]{:S(2)}, u32[]{:S(2)}) collective-permute-start(f32[224,128]{1,0:T(8,128)S(1)} %get-tuple-element.73), channel_id=1, source_target_pairs={{0,2},{1,3},{2,0},{3,1},{4,6},{5,7},{6,4},{7,5},{8,10},{9,11},{10,... | collective-permute-start | bytes 344072 | tf_op jit(solution)/shard_map/ppermute | solution.py:409
  52.0 4.6 %collective-permute-done.15.refs_1_ = f32[224,128]{1,0:T(8,128)S(1)} collective-permute-done((f32[224,128]{1,0:T(8,128)S(1)}, f32[224,128]{1,0:T(8,128)S(1)}, u32[]{:S(2)}, u32[]{:S(2)}) %collective-permute-start.15) | collective-permute-done | bytes 114720 | tf_op jit(solution)/shard_map/ppermute | solution.py:409
  56.6 1.2 %collective-permute-done.16.refs_2_ = f32[224,128]{1,0:T(8,128)S(1)} collective-permute-done((f32[224,128]{1,0:T(8,128)S(1)}, f32[224,128]{1,0:T(8,128)S(1)}, u32[]{:S(2)}, u32[]{:S(2)}) %collective-permute-start.16) | collective-permute-done | bytes 114720 | tf_op jit(solution)/shard_map/ppermute | solution.py:409
  57.9 1.6 %collective-permute-done.17.refs_3_ = f32[224,128]{1,0:T(8,128)S(1)} collective-permute-done((f32[224,128]{1,0:T(8,128)S(1)}, f32[224,128]{1,0:T(8,128)S(1)}, u32[]{:S(2)}, u32[]{:S(2)}) %collective-permute-start.17) | collective-permute-done | bytes 114720 | tf_op jit(solution)/shard_map/ppermute | solution.py:409
  59.5 0.9 %shard_map.112 = f32[880,128]{1,0:T(8,128)} custom-call(f32[224,128]{1,0:T(8,128)S(1)} %get-tuple-element.71.refs_0_, f32[224,128]{1,0:T(8,128)S(1)} %collective-permute-done.15.refs_1_, f32[224,128]{1,0:T(8,128)S(1)} %collective-permute-done.16.refs_2_, f32[224,128]{1,0:T(8,128)S(1)} %collective-permute-done.17.refs_3_, f32[896,128]{1,0:T(8,128)S(1)} %shard_map.105.refs_4_), custom_call_target="tpu_custom_call" | custom-call | bytes 917504 | tf_op jit(solution)/shard_map/pallas_call | solution.py:393
  (39 shorter events, 6.6 us)
Async XLA Ops:
  0.6 14.4 %collective-permute-start.5 = (f32[880,128]{1,0:T(8,128)}, f32[880,128]{1,0:T(8,128)S(1)}, u32[]{:S(2)}, u32[]{:S(2)}) collective-permute-start(f32[880,128]{1,0:T(8,128)} %bitcast.10), channel_id=1, source_target_pairs={{0,4},{4,0},{8,12},{12,8},{16,20},{20,16},{24,28},{28,24},{1,5},{5... | collective-permute-start | bytes 1351688 | tf_op jit(solution)/shard_map/ppermute | solution.py:418
  1.4 15.0 %collective-permute-start.6 = (f32[880,128]{1,0:T(8,128)}, f32[880,128]{1,0:T(8,128)S(1)}, u32[]{:S(2)}, u32[]{:S(2)}) collective-permute-start(f32[880,128]{1,0:T(8,128)} %bitcast.11), channel_id=1, source_target_pairs={{4,8},{8,4},{12,16},{16,12},{20,24},{24,20},{5,9},{9,5},{13,17},{1... | collective-permute-start | bytes 1351688 | tf_op jit(solution)/shard_map/ppermute | solution.py:417
  4.4 6.3 %copy-start.4 = (s32[512,9]{0,1:T(8,128)S(1)}, s32[512,9]{0,1:T(8,128)}, u32[]{:S(2)}) copy-start(s32[512,9]{0,1:T(8,128)} %param.16) | copy-start | bytes 55300
  4.4 6.3 %copy-start.5 = (s32[220,9]{0,1:T(8,128)S(1)}, s32[220,9]{0,1:T(8,128)}, u32[]{:S(2)}) copy-start(s32[220,9]{0,1:T(8,128)} %param.15) | copy-start | bytes 23764
  4.4 12.0 %copy-start = (f32[55,1,2048]{2,1,0:T(1,128)S(1)}, f32[55,1,2048]{2,1,0:T(1,128)}, u32[]{:S(2)}) copy-start(f32[55,1,2048]{2,1,0:T(1,128)} %param.9) | copy-start | bytes 1351684
  6.9 13.2 %collective-permute-start = (f32[232,128]{1,0:T(8,128)}, f32[232,128]{1,0:T(8,128)S(1)}, u32[]{:S(2)}, u32[]{:S(2)}) collective-permute-start(f32[232,128]{1,0:T(8,128)} %get-tuple-element.39), channel_id=1, source_target_pairs={{0,1},{1,2},{2,3},{3,0},{4,5},{5,6},{6,7},{7,4},{8,9},{9,10},{10,1... | collective-permute-start | bytes 356360 | tf_op jit(solution)/shard_map/ppermute | solution.py:409
  8.2 13.2 %collective-permute-start.3 = (f32[232,128]{1,0:T(8,128)}, f32[232,128]{1,0:T(8,128)S(1)}, u32[]{:S(2)}, u32[]{:S(2)}) collective-permute-start(f32[232,128]{1,0:T(8,128)} %get-tuple-element.43), channel_id=1, source_target_pairs={{0,2},{1,3},{2,0},{3,1},{4,6},{5,7},{6,4},{7,5},{8,10},{9,11},{10,... | collective-permute-start | bytes 356360 | tf_op jit(solution)/shard_map/ppermute | solution.py:409
  9.3 12.2 %collective-permute-start.4 = (f32[232,128]{1,0:T(8,128)}, f32[232,128]{1,0:T(8,128)S(1)}, u32[]{:S(2)}, u32[]{:S(2)}) collective-permute-start(f32[232,128]{1,0:T(8,128)} %get-tuple-element.44), channel_id=1, source_target_pairs={{0,3},{1,0},{2,1},{3,2},{4,7},{5,4},{6,5},{7,6},{8,11},{9,8},{10,9... | collective-permute-start | bytes 356360 | tf_op jit(solution)/shard_map/ppermute | solution.py:409
  15.0 6.4 %copy-start.1 = (f32[55,1,2048]{2,1,0:T(1,128)S(1)}, f32[55,1,2048]{2,1,0:T(1,128)}, u32[]{:S(2)}) copy-start(f32[55,1,2048]{2,1,0:T(1,128)} %param.11) | copy-start | bytes 1351684
  15.0 16.2 %copy-start.2 = (f32[232,128]{1,0:T(8,128)S(1)}, f32[232,128]{1,0:T(8,128)}, u32[]{:S(2)}) copy-start(f32[232,128]{1,0:T(8,128)} %get-tuple-element.41.refs_0_) | copy-start | bytes 356356
  17.3 10.9 %collective-permute-start.7 = (f32[232,128]{1,0:T(8,128)S(1)}, f32[232,128]{1,0:T(8,128)S(1)}, u32[]{:S(2)}, u32[]{:S(2)}) collective-permute-start(f32[232,128]{1,0:T(8,128)S(1)} %get-tuple-element.48), channel_id=1, source_target_pairs={{0,1},{1,2},{2,3},{3,0},{4,5},{5,6},{6,7},{7,4},{8,9},{9,10},{10,1... | collective-permute-start | bytes 356360 | tf_op jit(solution)/shard_map/ppermute | solution.py:409
  18.7 10.6 %collective-permute-start.8 = (f32[232,128]{1,0:T(8,128)S(1)}, f32[232,128]{1,0:T(8,128)S(1)}, u32[]{:S(2)}, u32[]{:S(2)}) collective-permute-start(f32[232,128]{1,0:T(8,128)S(1)} %get-tuple-element.49), channel_id=1, source_target_pairs={{0,2},{1,3},{2,0},{3,1},{4,6},{5,7},{6,4},{7,5},{8,10},{9,11},{10,... | collective-permute-start | bytes 356360 | tf_op jit(solution)/shard_map/ppermute | solution.py:409
  20.1 11.2 %collective-permute-start.9 = (f32[232,128]{1,0:T(8,128)S(1)}, f32[232,128]{1,0:T(8,128)S(1)}, u32[]{:S(2)}, u32[]{:S(2)}) collective-permute-start(f32[232,128]{1,0:T(8,128)S(1)} %get-tuple-element.50), channel_id=1, source_target_pairs={{0,3},{1,0},{2,1},{3,2},{4,7},{5,4},{6,5},{7,6},{8,11},{9,8},{10,9... | collective-permute-start | bytes 356360 | tf_op jit(solution)/shard_map/ppermute | solution.py:409
  21.5 14.5 %collective-permute-start.1 = (f32[880,128]{1,0:T(8,128)S(1)}, f32[880,128]{1,0:T(8,128)S(1)}, u32[]{:S(2)}, u32[]{:S(2)}) collective-permute-start(f32[880,128]{1,0:T(8,128)S(1)} %bitcast.14), channel_id=1, source_target_pairs={{0,4},{4,0},{8,12},{12,8},{16,20},{20,16},{24,28},{28,24},{1,5},{5... | collective-permute-start | bytes 1351688 | tf_op jit(solution)/shard_map/ppermute | solution.py:418
  21.5 17.6 %collective-permute-start.2 = (f32[880,128]{1,0:T(8,128)S(1)}, f32[880,128]{1,0:T(8,128)S(1)}, u32[]{:S(2)}, u32[]{:S(2)}) collective-permute-start(f32[880,128]{1,0:T(8,128)S(1)} %bitcast.15), channel_id=1, source_target_pairs={{4,8},{8,4},{12,16},{16,12},{20,24},{24,20},{5,9},{9,5},{13,17},{1... | collective-permute-start | bytes 1351688 | tf_op jit(solution)/shard_map/ppermute | solution.py:417
  32.6 10.2 %collective-permute-start.13 = (f32[224,512]{1,0:T(8,128)S(1)}, f32[224,512]{1,0:T(8,128)S(1)}, u32[]{:S(2)}, u32[]{:S(2)}) collective-permute-start(f32[224,512]{1,0:T(8,128)S(1)} %get-tuple-element.62.refs_0_), channel_id=1, source_target_pairs={{0,4},{4,0},{8,12},{12,8},{16,20},{20,16},{24,28},{28,24},{1,5},{5... | collective-permute-start | bytes 1376264 | tf_op jit(solution)/shard_map/ppermute | solution.py:418
  32.8 15.2 %collective-permute-start.14 = (f32[224,512]{1,0:T(8,128)S(1)}, f32[224,512]{1,0:T(8,128)S(1)}, u32[]{:S(2)}, u32[]{:S(2)}) collective-permute-start(f32[224,512]{1,0:T(8,128)S(1)} %get-tuple-element.62.refs_0_), channel_id=1, source_target_pairs={{4,8},{8,4},{12,16},{16,12},{20,24},{24,20},{5,9},{9,5},{13,17},{1... | collective-permute-start | bytes 1376264 | tf_op jit(solution)/shard_map/ppermute | solution.py:417
  39.8 10.5 %collective-permute-start.10 = (f32[224,128]{1,0:T(8,128)S(1)}, f32[224,128]{1,0:T(8,128)S(1)}, u32[]{:S(2)}, u32[]{:S(2)}) collective-permute-start(f32[224,128]{1,0:T(8,128)S(1)} %get-tuple-element.59), channel_id=1, source_target_pairs={{0,1},{1,2},{2,3},{3,0},{4,5},{5,6},{6,7},{7,4},{8,9},{9,10},{10,1... | collective-permute-start | bytes 344072 | tf_op jit(solution)/shard_map/ppermute | solution.py:409
  39.8 11.3 %collective-permute-start.11 = (f32[224,128]{1,0:T(8,128)S(1)}, f32[224,128]{1,0:T(8,128)S(1)}, u32[]{:S(2)}, u32[]{:S(2)}) collective-permute-start(f32[224,128]{1,0:T(8,128)S(1)} %get-tuple-element.60), channel_id=1, source_target_pairs={{0,2},{1,3},{2,0},{3,1},{4,6},{5,7},{6,4},{7,5},{8,10},{9,11},{10,... | collective-permute-start | bytes 344072 | tf_op jit(solution)/shard_map/ppermute | solution.py:409
  40.4 10.7 %collective-permute-start.12 = (f32[224,128]{1,0:T(8,128)S(1)}, f32[224,128]{1,0:T(8,128)S(1)}, u32[]{:S(2)}, u32[]{:S(2)}) collective-permute-start(f32[224,128]{1,0:T(8,128)S(1)} %get-tuple-element.61), channel_id=1, source_target_pairs={{0,3},{1,0},{2,1},{3,2},{4,7},{5,4},{6,5},{7,6},{8,11},{9,8},{10,9... | collective-permute-start | bytes 344072 | tf_op jit(solution)/shard_map/ppermute | solution.py:409
  41.3 6.7 %copy-start.3 = (f32[1,2048]{1,0:T(1,128)S(1)}, f32[1,2048]{1,0:T(1,128)}, u32[]{:S(2)}) copy-start(f32[1,2048]{1,0:T(1,128)} %param.12) | copy-start | bytes 24580
  49.1 7.5 %collective-permute-start.15 = (f32[224,128]{1,0:T(8,128)S(1)}, f32[224,128]{1,0:T(8,128)S(1)}, u32[]{:S(2)}, u32[]{:S(2)}) collective-permute-start(f32[224,128]{1,0:T(8,128)S(1)} %get-tuple-element.72), channel_id=1, source_target_pairs={{0,1},{1,2},{2,3},{3,0},{4,5},{5,6},{6,7},{7,4},{8,9},{9,10},{10,1... | collective-permute-start | bytes 344072 | tf_op jit(solution)/shard_map/ppermute | solution.py:409
  49.2 8.7 %collective-permute-start.16 = (f32[224,128]{1,0:T(8,128)S(1)}, f32[224,128]{1,0:T(8,128)S(1)}, u32[]{:S(2)}, u32[]{:S(2)}) collective-permute-start(f32[224,128]{1,0:T(8,128)S(1)} %get-tuple-element.73), channel_id=1, source_target_pairs={{0,2},{1,3},{2,0},{3,1},{4,6},{5,7},{6,4},{7,5},{8,10},{9,11},{10,... | collective-permute-start | bytes 344072 | tf_op jit(solution)/shard_map/ppermute | solution.py:409
  50.2 9.3 %collective-permute-start.17 = (f32[224,128]{1,0:T(8,128)S(1)}, f32[224,128]{1,0:T(8,128)S(1)}, u32[]{:S(2)}, u32[]{:S(2)}) collective-permute-start(f32[224,128]{1,0:T(8,128)S(1)} %get-tuple-element.74), channel_id=1, source_target_pairs={{0,3},{1,0},{2,1},{3,2},{4,7},{5,4},{6,5},{7,6},{8,11},{9,8},{10,9... | collective-permute-start | bytes 344072 | tf_op jit(solution)/shard_map/ppermute | solution.py:409
  (3 other events, 5.2 us)

commit v4 on v3

--- a/solution.py
+++ b/solution.py
@@ -508,9 +508,9 @@
         [*source, *rough, a_high, a_low, zones],
         [pltpu.VMEM((rows, wide), F32), pltpu.VMEM((rows, wide), F32)],
     )
-    relaxed, rim, back = results[:halves], results[halves], results[halves + 1 :]
+    relaxed, rim, back = results[:halves], results[halves], list(results[halves + 1 :])
     beside = [halo(x) for x in relaxed]
-    base, *back = lax.optimization_barrier((base, *back))
+    base, rim, back[2] = lax.optimization_barrier((base, rim, back[2]))
     back = exchange(back)
     part, spread = call(
         functools.partial(plane_kernel, nreg, halves),

time: 60.6 us -> 60.1 us (level)
  waiting for transfers between devices: 20.1 us -> 18.8 us
  starting transfers between devices: 25.2 us -> 26 us
    ppermute x12, starting transfers between devices: 11.5 us -> 14.7 us  [exchange(): received.append(lax.ppermute(chunks[k], 'modes', pairs))]
    ppermute x3, waiting for transfers between devices: 9.62 us -> 6.39 us  [halo(): far = lax.ppermute(x, 'space', far)]
    ppermute x3, starting transfers between devices: 12.9 us -> 10 us  [halo(): far = lax.ppermute(x, 'space', far)]
    ppermute x12, waiting for transfers between devices: 10.5 us -> 12.5 us  [exchange(): received.append(lax.ppermute(chunks[k], 'modes', pairs))]
where the time goes in v4:
time: 60.1 us; the launch traced here: 59.9 us
  starting transfers between devices  26 us (43%)
  waiting for transfers between devices  18.8 us (31%)
  Pallas kernels  13.5 us (22%)
  between operations  0.81 us (1%)
  local copies, waits for them, and re-layouts  0.71 us (1%)
    ppermute x12, starting transfers between devices, exchange(): received.append(lax.ppermute(chunks[k], 'modes', pairs))  14.7 us
    pallas_call x9, Pallas kernels, call(): pl.pallas_call(kernel, out_shape=out_shape, in_specs=specs, out_specs=[vm...  13.5 us
    ppermute x12, waiting for transfers between devices, exchange(): received.append(lax.ppermute(chunks[k], 'modes', pairs))  12.5 us
    ppermute x3, starting transfers between devices, halo(): far = lax.ppermute(x, 'space', far)  10 us
    ppermute x3, waiting for transfers between devices, halo(): far = lax.ppermute(x, 'space', far)  6.39 us
    ppermute x3, starting transfers between devices, halo(): return (lax.ppermute(x, 'space', near), far)  1.25 us
  transfers between devices with their start and end apart: 18, of which 8 were waited for; matrix products, arithmetic and copies ran while one was open for 0% of the time, Pallas kernels for 21%

profile of v4, /device:TPU:11, one launch (start us, length us, event | category | flops | bytes accessed | tf_op | source)
XLA Modules:
  0.0 59.9 jit_solution(11891144203815800492)
XLA Ops:
  1.4 3.0 %collective-permute-start.4 = (f32[880,128]{1,0:T(8,128)}, f32[880,128]{1,0:T(8,128)S(1)}, u32[]{:S(2)}, u32[]{:S(2)}) collective-permute-start(f32[880,128]{1,0:T(8,128)} %bitcast.11), channel_id=1, source_target_pairs={{4,8},{8,4},{12,16},{16,12},{20,24},{24,20},{5,9},{9,5},{13,17},{1... | collective-permute-start | bytes 1351688 | tf_op jit(solution)/shard_map/ppermute | solution.py:417
  4.4 2.4 %shard_map.104 = (f32[232,128]{1,0:T(8,128)}, f32[232,128]{1,0:T(8,128)}, f32[232,128]{1,0:T(8,128)}, f32[232,128]{1,0:T(8,128)}) custom-call(f32[880,128]{1,0:T(8,128)} %bitcast.12, f32[880,128]{1,0:T(8,128)} %bitcast.23, f32[16,128]{1,0:T(8,128)} %bitcast.17), custom_call_target="tpu_custom_call" | custom-call | bytes 909312 | tf_op jit(solution)/shard_map/pallas_call | solution.py:393
  6.9 1.3 %collective-permute-start = (f32[232,128]{1,0:T(8,128)}, f32[232,128]{1,0:T(8,128)S(1)}, u32[]{:S(2)}, u32[]{:S(2)}) collective-permute-start(f32[232,128]{1,0:T(8,128)} %get-tuple-element.38), channel_id=1, source_target_pairs={{0,1},{1,2},{2,3},{3,0},{4,5},{5,6},{6,7},{7,4},{8,9},{9,10},{10,1... | collective-permute-start | bytes 356360 | tf_op jit(solution)/shard_map/ppermute | solution.py:409
  8.2 1.1 %collective-permute-start.1 = (f32[232,128]{1,0:T(8,128)}, f32[232,128]{1,0:T(8,128)S(1)}, u32[]{:S(2)}, u32[]{:S(2)}) collective-permute-start(f32[232,128]{1,0:T(8,128)} %get-tuple-element.40), channel_id=1, source_target_pairs={{0,2},{1,3},{2,0},{3,1},{4,6},{5,7},{6,4},{7,5},{8,10},{9,11},{10,... | collective-permute-start | bytes 356360 | tf_op jit(solution)/shard_map/ppermute | solution.py:409
  9.3 1.4 %collective-permute-start.2 = (f32[232,128]{1,0:T(8,128)}, f32[232,128]{1,0:T(8,128)S(1)}, u32[]{:S(2)}, u32[]{:S(2)}) collective-permute-start(f32[232,128]{1,0:T(8,128)} %get-tuple-element.41), channel_id=1, source_target_pairs={{0,3},{1,0},{2,1},{3,2},{4,7},{5,4},{6,5},{7,6},{8,11},{9,8},{10,9... | collective-permute-start | bytes 356360 | tf_op jit(solution)/shard_map/ppermute | solution.py:409
  11.4 3.6 %shard_map.105 = (bf16[896,224]{1,0:T(8,128)(2,1)S(1)}, bf16[896,224]{1,0:T(8,128)(2,1)S(1)}, bf16[512,224]{1,0:T(8,128)(2,1)S(1)}, bf16[512,224]{1,0:T(8,128)(2...) custom-call(s32[9,220]{1,0:T(8,128)S(1)} %bitcast.20, ...), custom_call_target="tpu_custom_call" | custom-call | bytes 36736 | tf_op jit(solution)/shard_map/pallas_call | solution.py:393
  15.0 1.4 %collective-permute-done.4.far_ref = f32[880,128]{1,0:T(8,128)S(1)} collective-permute-done((f32[880,128]{1,0:T(8,128)}, f32[880,128]{1,0:T(8,128)S(1)}, u32[]{:S(2)}, u32[]{:S(2)}) %collective-permute-start.4) | collective-permute-done | bytes 450592 | tf_op jit(solution)/shard_map/ppermute | solution.py:417
  17.3 1.4 %collective-permute-start.5 = (f32[232,128]{1,0:T(8,128)S(1)}, f32[232,128]{1,0:T(8,128)S(1)}, u32[]{:S(2)}, u32[]{:S(2)}) collective-permute-start(f32[232,128]{1,0:T(8,128)S(1)} %get-tuple-element.45), channel_id=1, source_target_pairs={{0,1},{1,2},{2,3},{3,0},{4,5},{5,6},{6,7},{7,4},{8,9},{9,10},{10,1... | collective-permute-start | bytes 356360 | tf_op jit(solution)/shard_map/ppermute | solution.py:409
  18.7 1.4 %collective-permute-start.6 = (f32[232,128]{1,0:T(8,128)S(1)}, f32[232,128]{1,0:T(8,128)S(1)}, u32[]{:S(2)}, u32[]{:S(2)}) collective-permute-start(f32[232,128]{1,0:T(8,128)S(1)} %get-tuple-element.46), channel_id=1, source_target_pairs={{0,2},{1,3},{2,0},{3,1},{4,6},{5,7},{6,4},{7,5},{8,10},{9,11},{10,... | collective-permute-start | bytes 356360 | tf_op jit(solution)/shard_map/ppermute | solution.py:409
  20.1 1.4 %collective-permute-start.7 = (f32[232,128]{1,0:T(8,128)S(1)}, f32[232,128]{1,0:T(8,128)S(1)}, u32[]{:S(2)}, u32[]{:S(2)}) collective-permute-start(f32[232,128]{1,0:T(8,128)S(1)} %get-tuple-element.47), channel_id=1, source_target_pairs={{0,3},{1,0},{2,1},{3,2},{4,7},{5,4},{6,5},{7,6},{8,11},{9,8},{10,9... | collective-permute-start | bytes 356360 | tf_op jit(solution)/shard_map/ppermute | solution.py:409
  21.5 3.9 %collective-permute-start.10 = (f32[880,128]{1,0:T(8,128)S(1)}, f32[880,128]{1,0:T(8,128)S(1)}, u32[]{:S(2)}, u32[]{:S(2)}) collective-permute-start(f32[880,128]{1,0:T(8,128)S(1)} %bitcast.14), channel_id=1, source_target_pairs={{4,8},{8,4},{12,16},{16,12},{20,24},{24,20},{5,9},{9,5},{13,17},{1... | collective-permute-start | bytes 1351688 | tf_op jit(solution)/shard_map/ppermute | solution.py:417
  25.4 1.3 %collective-permute-done.5.refs_5_ = f32[232,128]{1,0:T(8,128)S(1)} collective-permute-done((f32[232,128]{1,0:T(8,128)S(1)}, f32[232,128]{1,0:T(8,128)S(1)}, u32[]{:S(2)}, u32[]{:S(2)}) %collective-permute-start.5) | collective-permute-done | bytes 118816 | tf_op jit(solution)/shard_map/ppermute | solution.py:409
  26.8 2.5 %collective-permute-done.6.refs_6_ = f32[232,128]{1,0:T(8,128)S(1)} collective-permute-done((f32[232,128]{1,0:T(8,128)S(1)}, f32[232,128]{1,0:T(8,128)S(1)}, u32[]{:S(2)}, u32[]{:S(2)}) %collective-permute-start.6) | collective-permute-done | bytes 118816 | tf_op jit(solution)/shard_map/ppermute | solution.py:409
  29.3 1.6 %collective-permute-done.7.refs_7_ = f32[232,128]{1,0:T(8,128)S(1)} collective-permute-done((f32[232,128]{1,0:T(8,128)S(1)}, f32[232,128]{1,0:T(8,128)S(1)}, u32[]{:S(2)}, u32[]{:S(2)}) %collective-permute-start.7) | collective-permute-done | bytes 118816 | tf_op jit(solution)/shard_map/ppermute | solution.py:409
  30.9 1.4 %shard_map.107 = (f32[224,512]{1,0:T(8,128)S(1)}, f32[224,128]{1,0:T(8,128)S(1)}, f32[224,128]{1,0:T(8,128)S(1)}, f32[224,128]{1,0:T(8,128)S(1)}, f32[224,128]{1,0:T(8,128)S(1)}, /*index=5*/f32[224,128]{1,0:T(8,128)S(1)}) custom-call(f32[232,128]{1,0:T(8,128)S(1)} %copy-done.2, f32[232,128]{1,0:T(8,128)S(1)} %collective-permute-done.refs_1_, ...), custom_call_target="tpu_custom_call" | custom-call | bytes 1755648 | tf_op jit(solution)/shard_map/pallas_call | solution.py:393
  32.8 3.1 %collective-permute-start.14 = (f32[224,512]{1,0:T(8,128)S(1)}, f32[224,512]{1,0:T(8,128)S(1)}, u32[]{:S(2)}, u32[]{:S(2)}) collective-permute-start(f32[224,512]{1,0:T(8,128)S(1)} %get-tuple-element.58.refs_0_), channel_id=1, source_target_pairs={{4,8},{8,4},{12,16},{16,12},{20,24},{24,20},{5,9},{9,5},{13,17},{1... | collective-permute-start | bytes 1376264 | tf_op jit(solution)/shard_map/ppermute | solution.py:417
  36.7 2.1 %collective-permute-start.11 = (f32[224,128]{1,0:T(8,128)S(1)}, f32[224,128]{1,0:T(8,128)S(1)}, u32[]{:S(2)}, u32[]{:S(2)}) collective-permute-start(f32[224,128]{1,0:T(8,128)S(1)} %get-tuple-element.56), channel_id=1, source_target_pairs={{0,2},{1,3},{2,0},{3,1},{4,6},{5,7},{6,4},{7,5},{8,10},{9,11},{10,... | collective-permute-start | bytes 344072 | tf_op jit(solution)/shard_map/ppermute | solution.py:409
  38.9 1.4 %collective-permute-start.8 = (f32[224,128]{1,0:T(8,128)S(1)}, f32[224,128]{1,0:T(8,128)S(1)}, u32[]{:S(2)}, u32[]{:S(2)}) collective-permute-start(f32[224,128]{1,0:T(8,128)S(1)} %get-tuple-element.52), channel_id=1, source_target_pairs={{0,1},{1,2},{2,3},{3,0},{4,5},{5,6},{6,7},{7,4},{8,9},{9,10},{10,1... | collective-permute-start | bytes 344072 | tf_op jit(solution)/shard_map/ppermute | solution.py:409
  40.3 1.5 %shard_map.110 = (f32[512,512]{1,0:T(8,128)S(1)}, f32[512,512]{1,0:T(8,128)S(1)}) custom-call(f32[224,512]{1,0:T(8,128)S(1)} %get-tuple-element.58.refs_0_, f32[224,128]{1,0:T(8,128)S(1)} %get-tuple-element.59.refs_1_, s32[1,640]{1,0:T(1,128)S(1)} %get-tuple-element.50.refs_10_.refs_2_, bf16[512,224]{1,0:T(8,128)(2,1)S(1)} %get-tuple-element.60.refs_3_.bh_ref, ...), custom_call_target="tpu_custom_call" | custom-call | bytes 1165824 | tf_op jit(solution)/shard_map/pallas_call | solution.py:393
  41.8 5.0 %collective-permute-done.14.far_ref = f32[224,512]{1,0:T(8,128)S(1)} collective-permute-done((f32[224,512]{1,0:T(8,128)S(1)}, f32[224,512]{1,0:T(8,128)S(1)}, u32[]{:S(2)}, u32[]{:S(2)}) %collective-permute-start.14) | collective-permute-done | bytes 458784 | tf_op jit(solution)/shard_map/ppermute | solution.py:417
  46.8 1.1 %shard_map.111 = (f32[224,128]{1,0:T(8,128)S(1)}, f32[224,128]{1,0:T(8,128)S(1)}, f32[224,128]{1,0:T(8,128)S(1)}, f32[224,128]{1,0:T(8,128)S(1)}) custom-call(f32[224,512]{1,0:T(8,128)S(1)} %collective-permute-done.13.near_ref, f32[224,512]{1,0:T(8,128)S(1)} %collective-permute-done.14.far_ref, f32[512,512]{1,0:T(8,128)S(1)} %get-tuple-element.63.part_ref, ...), custom_call_target="tpu_custom_call" | custom-call | bytes 3940352 | tf_op jit(solution)/shard_map/pallas_call | solution.py:393
  48.0 2.4 %collective-permute-start.16 = (f32[224,128]{1,0:T(8,128)S(1)}, f32[224,128]{1,0:T(8,128)S(1)}, u32[]{:S(2)}, u32[]{:S(2)}) collective-permute-start(f32[224,128]{1,0:T(8,128)S(1)} %get-tuple-element.69), channel_id=1, source_target_pairs={{0,2},{1,3},{2,0},{3,1},{4,6},{5,7},{6,4},{7,5},{8,10},{9,11},{10,... | collective-permute-start | bytes 344072 | tf_op jit(solution)/shard_map/ppermute | solution.py:409
  52.9 4.3 %collective-permute-done.16.refs_2_ = f32[224,128]{1,0:T(8,128)S(1)} collective-permute-done((f32[224,128]{1,0:T(8,128)S(1)}, f32[224,128]{1,0:T(8,128)S(1)}, u32[]{:S(2)}, u32[]{:S(2)}) %collective-permute-start.16) | collective-permute-done | bytes 114720 | tf_op jit(solution)/shard_map/ppermute | solution.py:409
  57.1 1.8 %collective-permute-done.17.refs_3_ = f32[224,128]{1,0:T(8,128)S(1)} collective-permute-done((f32[224,128]{1,0:T(8,128)S(1)}, f32[224,128]{1,0:T(8,128)S(1)}, u32[]{:S(2)}, u32[]{:S(2)}) %collective-permute-start.17) | collective-permute-done | bytes 114720 | tf_op jit(solution)/shard_map/ppermute | solution.py:409
  (39 shorter events, 7.1 us)
Async XLA Ops:
  0.6 14.4 %collective-permute-start.3 = (f32[880,128]{1,0:T(8,128)}, f32[880,128]{1,0:T(8,128)S(1)}, u32[]{:S(2)}, u32[]{:S(2)}) collective-permute-start(f32[880,128]{1,0:T(8,128)} %bitcast.10), channel_id=1, source_target_pairs={{0,4},{4,0},{8,12},{12,8},{16,20},{20,16},{24,28},{28,24},{1,5},{5... | collective-permute-start | bytes 1351688 | tf_op jit(solution)/shard_map/ppermute | solution.py:418
  1.4 15.0 %collective-permute-start.4 = (f32[880,128]{1,0:T(8,128)}, f32[880,128]{1,0:T(8,128)S(1)}, u32[]{:S(2)}, u32[]{:S(2)}) collective-permute-start(f32[880,128]{1,0:T(8,128)} %bitcast.11), channel_id=1, source_target_pairs={{4,8},{8,4},{12,16},{16,12},{20,24},{24,20},{5,9},{9,5},{13,17},{1... | collective-permute-start | bytes 1351688 | tf_op jit(solution)/shard_map/ppermute | solution.py:417
  4.4 6.3 %copy-start.4 = (s32[512,9]{0,1:T(8,128)S(1)}, s32[512,9]{0,1:T(8,128)}, u32[]{:S(2)}) copy-start(s32[512,9]{0,1:T(8,128)} %param.16) | copy-start | bytes 55300
  4.4 6.3 %copy-start.5 = (s32[220,9]{0,1:T(8,128)S(1)}, s32[220,9]{0,1:T(8,128)}, u32[]{:S(2)}) copy-start(s32[220,9]{0,1:T(8,128)} %param.15) | copy-start | bytes 23764
  4.4 12.0 %copy-start = (f32[55,1,2048]{2,1,0:T(1,128)S(1)}, f32[55,1,2048]{2,1,0:T(1,128)}, u32[]{:S(2)}) copy-start(f32[55,1,2048]{2,1,0:T(1,128)} %param.9) | copy-start | bytes 1351684
  6.9 13.2 %collective-permute-start = (f32[232,128]{1,0:T(8,128)}, f32[232,128]{1,0:T(8,128)S(1)}, u32[]{:S(2)}, u32[]{:S(2)}) collective-permute-start(f32[232,128]{1,0:T(8,128)} %get-tuple-element.38), channel_id=1, source_target_pairs={{0,1},{1,2},{2,3},{3,0},{4,5},{5,6},{6,7},{7,4},{8,9},{9,10},{10,1... | collective-permute-start | bytes 356360 | tf_op jit(solution)/shard_map/ppermute | solution.py:409
  8.2 13.2 %collective-permute-start.1 = (f32[232,128]{1,0:T(8,128)}, f32[232,128]{1,0:T(8,128)S(1)}, u32[]{:S(2)}, u32[]{:S(2)}) collective-permute-start(f32[232,128]{1,0:T(8,128)} %get-tuple-element.40), channel_id=1, source_target_pairs={{0,2},{1,3},{2,0},{3,1},{4,6},{5,7},{6,4},{7,5},{8,10},{9,11},{10,... | collective-permute-start | bytes 356360 | tf_op jit(solution)/shard_map/ppermute | solution.py:409
  9.3 16.0 %collective-permute-start.2 = (f32[232,128]{1,0:T(8,128)}, f32[232,128]{1,0:T(8,128)S(1)}, u32[]{:S(2)}, u32[]{:S(2)}) collective-permute-start(f32[232,128]{1,0:T(8,128)} %get-tuple-element.41), channel_id=1, source_target_pairs={{0,3},{1,0},{2,1},{3,2},{4,7},{5,4},{6,5},{7,6},{8,11},{9,8},{10,9... | collective-permute-start | bytes 356360 | tf_op jit(solution)/shard_map/ppermute | solution.py:409
  15.0 6.4 %copy-start.1 = (f32[55,1,2048]{2,1,0:T(1,128)S(1)}, f32[55,1,2048]{2,1,0:T(1,128)}, u32[]{:S(2)}) copy-start(f32[55,1,2048]{2,1,0:T(1,128)} %param.11) | copy-start | bytes 1351684
  15.0 15.9 %copy-start.2 = (f32[232,128]{1,0:T(8,128)S(1)}, f32[232,128]{1,0:T(8,128)}, u32[]{:S(2)}) copy-start(f32[232,128]{1,0:T(8,128)} %get-tuple-element.37.refs_0_) | copy-start | bytes 356356
  17.3 9.5 %collective-permute-start.5 = (f32[232,128]{1,0:T(8,128)S(1)}, f32[232,128]{1,0:T(8,128)S(1)}, u32[]{:S(2)}, u32[]{:S(2)}) collective-permute-start(f32[232,128]{1,0:T(8,128)S(1)} %get-tuple-element.45), channel_id=1, source_target_pairs={{0,1},{1,2},{2,3},{3,0},{4,5},{5,6},{6,7},{7,4},{8,9},{9,10},{10,1... | collective-permute-start | bytes 356360 | tf_op jit(solution)/shard_map/ppermute | solution.py:409
  18.7 10.6 %collective-permute-start.6 = (f32[232,128]{1,0:T(8,128)S(1)}, f32[232,128]{1,0:T(8,128)S(1)}, u32[]{:S(2)}, u32[]{:S(2)}) collective-permute-start(f32[232,128]{1,0:T(8,128)S(1)} %get-tuple-element.46), channel_id=1, source_target_pairs={{0,2},{1,3},{2,0},{3,1},{4,6},{5,7},{6,4},{7,5},{8,10},{9,11},{10,... | collective-permute-start | bytes 356360 | tf_op jit(solution)/shard_map/ppermute | solution.py:409
  20.1 10.9 %collective-permute-start.7 = (f32[232,128]{1,0:T(8,128)S(1)}, f32[232,128]{1,0:T(8,128)S(1)}, u32[]{:S(2)}, u32[]{:S(2)}) collective-permute-start(f32[232,128]{1,0:T(8,128)S(1)} %get-tuple-element.47), channel_id=1, source_target_pairs={{0,3},{1,0},{2,1},{3,2},{4,7},{5,4},{6,5},{7,6},{8,11},{9,8},{10,9... | collective-permute-start | bytes 356360 | tf_op jit(solution)/shard_map/ppermute | solution.py:409
  21.5 14.5 %collective-permute-start.10 = (f32[880,128]{1,0:T(8,128)S(1)}, f32[880,128]{1,0:T(8,128)S(1)}, u32[]{:S(2)}, u32[]{:S(2)}) collective-permute-start(f32[880,128]{1,0:T(8,128)S(1)} %bitcast.14), channel_id=1, source_target_pairs={{4,8},{8,4},{12,16},{16,12},{20,24},{24,20},{5,9},{9,5},{13,17},{1... | collective-permute-start | bytes 1351688 | tf_op jit(solution)/shard_map/ppermute | solution.py:417
  25.4 10.6 %collective-permute-start.9 = (f32[880,128]{1,0:T(8,128)S(1)}, f32[880,128]{1,0:T(8,128)S(1)}, u32[]{:S(2)}, u32[]{:S(2)}) collective-permute-start(f32[880,128]{1,0:T(8,128)S(1)} %bitcast.15), channel_id=1, source_target_pairs={{0,4},{4,0},{8,12},{12,8},{16,20},{20,16},{24,28},{28,24},{1,5},{5... | collective-permute-start | bytes 1351688 | tf_op jit(solution)/shard_map/ppermute | solution.py:418
  32.4 9.4 %collective-permute-start.13 = (f32[224,512]{1,0:T(8,128)S(1)}, f32[224,512]{1,0:T(8,128)S(1)}, u32[]{:S(2)}, u32[]{:S(2)}) collective-permute-start(f32[224,512]{1,0:T(8,128)S(1)} %get-tuple-element.58.refs_0_), channel_id=1, source_target_pairs={{0,4},{4,0},{8,12},{12,8},{16,20},{20,16},{24,28},{28,24},{1,5},{5... | collective-permute-start | bytes 1376264 | tf_op jit(solution)/shard_map/ppermute | solution.py:418
  32.8 14.0 %collective-permute-start.14 = (f32[224,512]{1,0:T(8,128)S(1)}, f32[224,512]{1,0:T(8,128)S(1)}, u32[]{:S(2)}, u32[]{:S(2)}) collective-permute-start(f32[224,512]{1,0:T(8,128)S(1)} %get-tuple-element.58.refs_0_), channel_id=1, source_target_pairs={{4,8},{8,4},{12,16},{16,12},{20,24},{24,20},{5,9},{9,5},{13,17},{1... | collective-permute-start | bytes 1376264 | tf_op jit(solution)/shard_map/ppermute | solution.py:417
  36.7 13.8 %collective-permute-start.11 = (f32[224,128]{1,0:T(8,128)S(1)}, f32[224,128]{1,0:T(8,128)S(1)}, u32[]{:S(2)}, u32[]{:S(2)}) collective-permute-start(f32[224,128]{1,0:T(8,128)S(1)} %get-tuple-element.56), channel_id=1, source_target_pairs={{0,2},{1,3},{2,0},{3,1},{4,6},{5,7},{6,4},{7,5},{8,10},{9,11},{10,... | collective-permute-start | bytes 344072 | tf_op jit(solution)/shard_map/ppermute | solution.py:409
  38.8 12.3 %collective-permute-start.12 = (f32[224,128]{1,0:T(8,128)S(1)}, f32[224,128]{1,0:T(8,128)S(1)}, u32[]{:S(2)}, u32[]{:S(2)}) collective-permute-start(f32[224,128]{1,0:T(8,128)S(1)} %get-tuple-element.57), channel_id=1, source_target_pairs={{0,3},{1,0},{2,1},{3,2},{4,7},{5,4},{6,5},{7,6},{8,11},{9,8},{10,9... | collective-permute-start | bytes 344072 | tf_op jit(solution)/shard_map/ppermute | solution.py:409
  38.9 12.2 %collective-permute-start.8 = (f32[224,128]{1,0:T(8,128)S(1)}, f32[224,128]{1,0:T(8,128)S(1)}, u32[]{:S(2)}, u32[]{:S(2)}) collective-permute-start(f32[224,128]{1,0:T(8,128)S(1)} %get-tuple-element.52), channel_id=1, source_target_pairs={{0,1},{1,2},{2,3},{3,0},{4,5},{5,6},{6,7},{7,4},{8,9},{9,10},{10,1... | collective-permute-start | bytes 344072 | tf_op jit(solution)/shard_map/ppermute | solution.py:409
  40.3 6.5 %copy-start.3 = (f32[1,2048]{1,0:T(1,128)S(1)}, f32[1,2048]{1,0:T(1,128)}, u32[]{:S(2)}) copy-start(f32[1,2048]{1,0:T(1,128)} %param.12) | copy-start | bytes 24580
  48.0 4.9 %collective-permute-start.15 = (f32[224,128]{1,0:T(8,128)S(1)}, f32[224,128]{1,0:T(8,128)S(1)}, u32[]{:S(2)}, u32[]{:S(2)}) collective-permute-start(f32[224,128]{1,0:T(8,128)S(1)} %get-tuple-element.68), channel_id=1, source_target_pairs={{0,1},{1,2},{2,3},{3,0},{4,5},{5,6},{6,7},{7,4},{8,9},{9,10},{10,1... | collective-permute-start | bytes 344072 | tf_op jit(solution)/shard_map/ppermute | solution.py:409
  48.0 9.1 %collective-permute-start.16 = (f32[224,128]{1,0:T(8,128)S(1)}, f32[224,128]{1,0:T(8,128)S(1)}, u32[]{:S(2)}, u32[]{:S(2)}) collective-permute-start(f32[224,128]{1,0:T(8,128)S(1)} %get-tuple-element.69), channel_id=1, source_target_pairs={{0,2},{1,3},{2,0},{3,1},{4,6},{5,7},{6,4},{7,5},{8,10},{9,11},{10,... | collective-permute-start | bytes 344072 | tf_op jit(solution)/shard_map/ppermute | solution.py:409
  50.5 8.5 %collective-permute-start.17 = (f32[224,128]{1,0:T(8,128)S(1)}, f32[224,128]{1,0:T(8,128)S(1)}, u32[]{:S(2)}, u32[]{:S(2)}) collective-permute-start(f32[224,128]{1,0:T(8,128)S(1)} %get-tuple-element.70), channel_id=1, source_target_pairs={{0,3},{1,0},{2,1},{3,2},{4,7},{5,4},{6,5},{7,6},{8,11},{9,8},{10,9... | collective-permute-start | bytes 344072 | tf_op jit(solution)/shard_map/ppermute | solution.py:409
  (3 other events, 5.2 us)

commit v5 on v4

--- a/solution.py
+++ b/solution.py
@@ -46,6 +46,29 @@
     return lax.broadcasted_iota(jnp.int32, shape, len(shape) - 1)
 
 
+def target_of(swap, me, k, parts):
+    if swap and parts & (parts - 1) == 0:
+        return me ^ (swap(k, parts) if k else 0)
+    return (me + k) % parts if isinstance(me, int) else lax.rem(me + k, parts)
+
+
+def origin_of(swap, me, k, parts):
+    if swap and parts & (parts - 1) == 0:
+        return me ^ (swap(k, parts) if k else 0)
+    return lax.rem(me + (parts - k), parts)
+
+
+def upward(k, parts):
+    return k
+
+
+def downward(k, parts):
+    return parts - k
+
+
+W_SWAP, R_SWAP, B_SWAP, H_SWAP = None, upward, None, None
+
+
 def load_group(ref, group, modes, groups):
     return ref[pl.ds(group, modes, stride=groups), :]
 
@@ -56,12 +79,12 @@
     return jnp.concatenate([x, jnp.zeros((rows - x.shape[0], x.shape[1]), x.dtype)], axis=0)
 
 
-def emit_slots(me, parts, grouped, outs, padded):
+def emit_slots(swap, me, parts, grouped, outs, padded):
     groups = grouped.shape[0] // padded
     per = groups // parts
     lane = lane_ids((padded, LANES))
     for k, out in enumerate(outs):
-        q = lax.rem(me + k, parts)
+        q = target_of(swap, me, k, parts)
         start = pl.multiple_of(q * (per * padded), SUB)
         out[: per * padded, :] = grouped[pl.ds(start, per * padded), :]
         before = pl.multiple_of(jnp.maximum(q * per - 1, 0) * padded, SUB)
@@ -98,7 +121,7 @@
             rows = pl.ds(start * groups + g, count, stride=groups)
             w = v_ref[rows, :] + j_ref[rows, :] * factor[g : g + 1]
             grouped[g * padded + start : g * padded + start + SUB, :] = pad_rows(w, SUB)
-    emit_slots(me, parts, grouped, outs, padded)
+    emit_slots(W_SWAP, me, parts, grouped, outs, padded)
 
 
 def stencil_groups(x_ref, near_ref, far_ref, modes, groups, padded, emit):
@@ -126,7 +149,7 @@
         grouped[g * padded : (g + 1) * padded, :] = total
 
     stencil_groups(v_ref, near_ref, far_ref, modes, groups, padded, emit)
-    emit_slots(me, parts, grouped, outs, padded)
+    emit_slots(R_SWAP, me, parts, grouped, outs, padded)
 
 
 def thermal_kernel(modes, padded, groups, t_ref, near_ref, far_ref, out_ref):
@@ -179,6 +202,7 @@
     root = jnp.where(step, jnp.sqrt((jnp.maximum(left, right) // TILE16).astype(F32)), 0.0)
     param = lax.broadcasted_iota(jnp.int32, (1, kinds), 1) % TILE16
     hot3 = jnp.concatenate([hot_along] * 3, axis=0)
+    matrices = []
     for r in range(nreg):
         weight = jnp.zeros((1, kinds), F32)
         for m in range(npar):
@@ -188,10 +212,12 @@
         mid = (link - high.astype(F32)).astype(BF16)
         low = (link - high.astype(F32) - mid.astype(F32)).astype(BF16)
         part = dot(hot_down, jnp.concatenate([high, mid, low], axis=1)).astype(BF16)
-        matrix = jnp.where(linked, dot(part, hot3), jnp.where(same, 1.0, 0.0))
-        high, low = split2(matrix)
-        ah_ref[r * rows : (r + 1) * rows, :] = high
-        al_ref[r * rows : (r + 1) * rows, :] = low
+        matrices.append(jnp.where(linked, dot(part, hot3), jnp.where(same, 1.0, 0.0)))
+    for source in range(parts):
+        columns = slice(source * padded, (source + 1) * padded)
+        high, low = split2(jnp.concatenate([x[:, columns] for x in matrices], axis=1))
+        ah_ref[source] = high
+        al_ref[source] = low
 
     nodes = nodes_ref[...]
     t = jnp.zeros(nodes.shape, F32)
@@ -258,46 +284,57 @@
     zones_ref[:, per * LANES :] = jnp.where(lane_ids(low.shape) < NZ, low, high)
 
 
-def couple_kernel(parts, padded, per, nreg, halves, *refs):
-    w_refs = refs[:parts]
-    r_refs = refs[parts : 2 * parts]
-    ah_ref, al_ref, zones_ref = refs[2 * parts : 2 * parts + 3]
-    rel_refs = refs[2 * parts + 3 : 2 * parts + 3 + halves]
-    rim_ref, *outs = refs[2 * parts + 3 + halves : -2]
-    w_all, r_all = refs[-2:]
-    me = lax.axis_index("modes")
-    rows = parts * padded
+def unpack(chunk, padded, per):
+    packed = chunk[per * padded :, :]
+    rims = [packed]
+    for tile in range(1, padded // SUB):
+        rims.append(pltpu.roll(packed, LANES - 2 * NZ * tile, 1))
+    columns = [chunk[s * padded : (s + 1) * padded, :] for s in range(per)]
+    return jnp.concatenate(columns + [jnp.concatenate(rims, axis=0)], axis=1)
+
+
+def coupled(chunk, source, ah_ref, al_ref, zones, nreg, padded, per):
+    field = unpack(chunk, padded, per)
+    stacked = jnp.concatenate([jnp.where(zones == r, field, 0.0) for r in range(nreg)], axis=0)
+    high, low = split2(stacked)
+    return dot3(ah_ref[source], al_ref[source], high, low)
+
+
+def couple_kernel(parts, padded, per, nreg, count, *refs):
+    w_refs, r_refs = refs[:parts], refs[parts : parts + count]
+    ah_ref, al_ref, zones_ref, out_ref = refs[parts + count :]
+    me = lax.axis_index("modes")
+    zones = zones_ref[...]
+    applied = None
+    for k in range(count):
+        source = origin_of(R_SWAP, me, k, parts)
+        part = coupled(r_refs[k], source, ah_ref, al_ref, zones, nreg, padded, per)
+        applied = part if applied is None else applied + part
+    for k in range(parts):
+        at = pl.multiple_of(origin_of(W_SWAP, me, k, parts) * padded, SUB)
+        out_ref[pl.ds(at, padded), :] = unpack(w_refs[k], padded, per)
+    out_ref[...] = out_ref[...] - (0.8 / 6.0) * applied
+
+
+def relax_kernel(parts, padded, per, nreg, count, *refs):
+    r_refs = refs[: parts - count]
+    most_ref, ah_ref, al_ref, zones_ref, rel_ref, rim_ref, *outs, all_ref = refs[parts - count :]
+    me = lax.axis_index("modes")
     width = per * LANES
-    for k in range(parts):
-        source = lax.rem(me + (parts - k), parts)
-        at = pl.multiple_of(source * padded, SUB)
-        for chunk, dest in ((w_refs[k], w_all), (r_refs[k], r_all)):
-            for s in range(per):
-                dest[pl.ds(at, padded), s * LANES : (s + 1) * LANES] = chunk[
-                    s * padded : (s + 1) * padded, :
-                ]
-            packed = chunk[per * padded :, :]
-            for tile in range(padded // SUB):
-                spot = pl.multiple_of(at + tile * SUB, SUB)
-                shift = (LANES - 2 * NZ * tile) % LANES
-                part = pltpu.roll(packed, shift, 1) if shift else packed
-                dest[pl.ds(spot, SUB), width:] = part
-    r_high, r_low = split2(r_all[...])
     zones = zones_ref[...]
-    applied = jnp.zeros(r_all.shape, F32)
-    for r in range(nreg):
-        a_high = ah_ref[r * rows : (r + 1) * rows, :]
-        a_low = al_ref[r * rows : (r + 1) * rows, :]
-        applied = jnp.where(zones == r, dot3(a_high, a_low, r_high, r_low), applied)
-    w_all[...] = w_all[...] - (0.8 / 6.0) * applied
-    for h, rel_ref in enumerate(rel_refs):
-        rel_ref[...] = w_all[:, h * width // halves : (h + 1) * width // halves]
-    rim_ref[...] = w_all[:, width:]
+    applied = None
+    for k in range(count, parts):
+        source = origin_of(R_SWAP, me, k, parts)
+        part = coupled(r_refs[k - count], source, ah_ref, al_ref, zones, nreg, padded, per)
+        applied = part if applied is None else applied + part
+    relaxed = most_ref[...] - (0.8 / 6.0) * applied
+    rel_ref[...] = relaxed[:, :width]
+    rim_ref[...] = relaxed[:, width:]
+    all_ref[...] = relaxed[:, :width]
     for k, out in enumerate(outs):
-        target = lax.rem(me + k, parts)
-        at = pl.multiple_of(target * padded, SUB)
+        at = pl.multiple_of(target_of(B_SWAP, me, k, parts) * padded, SUB)
         for s in range(per):
-            out[s * padded : (s + 1) * padded, :] = w_all[
+            out[s * padded : (s + 1) * padded, :] = all_ref[
                 pl.ds(at, padded), s * LANES : (s + 1) * LANES
             ]
 
@@ -348,7 +385,7 @@
             heat[:, s * LANES : (s + 1) * LANES] * a_ref[pl.ds(me * per + half * own + s, 1), :]
         )
     for k, out in enumerate(outs):
-        target = lax.rem(me + k, parts)
+        target = target_of(H_SWAP, me, k, parts)
         at = pl.multiple_of(target * padded, SUB)
         for s in range(own):
             out[s * padded : (s + 1) * padded, :] = heat_ref[
@@ -356,31 +393,52 @@
             ]
 
 
+def flat_tiles(modes, groups, write, out_hbm, buffer, sems):
+    copies = []
+    for tile, start in enumerate(range(0, modes, SUB)):
+        count = min(SUB, modes - start)
+        write(start, count)
+        rows = pl.ds(start * groups, count * groups)
+        copy = pltpu.make_async_copy(buffer.at[rows], out_hbm.at[rows], sems.at[tile])
+        copy.start()
+        copies.append(copy)
+    for copy in copies:
+        copy.wait()
+
+
 def gather_kernel(parts, modes, padded, per, *refs):
-    chunks, out = refs[:parts], refs[parts]
-    me = lax.axis_index("modes")
-    for k in range(parts):
-        q = lax.rem(me + (parts - k), parts)
-        for s in range(per):
-            rows = chunks[k][s * padded : s * padded + modes, :]
-            out[pl.ds(q * per + s, modes, stride=parts * per), :] = rows
-
-
-def final_kernel(parts, modes, padded, per, halves, *refs):
-    chunks, base, out = refs[: parts * halves], refs[-2], refs[-1]
-    me = lax.axis_index("modes")
-    own = per // halves
-    for k in range(parts):
-        q = lax.rem(me + (parts - k), parts)
-        for s in range(per):
-            chunk = chunks[s // own * parts + k]
-            at = pl.multiple_of((q * per + s) * padded, SUB)
-            within = s % own * padded
-            rows = base[pl.ds(at, padded), :] + 0.1 * chunk[within : within + padded, :]
-            out[pl.ds(q * per + s, modes, stride=parts * per), :] = rows[:modes]
-
-
-def call(kernel, out_shape, args, scratch=(), smem=(), hbm=(), limit=VMEM_LIMIT):
+    chunks, (out_hbm, buffer, sems) = refs[:parts], refs[parts:]
+    me = lax.axis_index("modes")
+    groups = parts * per
+
+    def write(start, count):
+        for k in range(parts):
+            q = origin_of(B_SWAP, me, k, parts)
+            for s in range(per):
+                at = pl.ds(start * groups + q * per + s, count, stride=groups)
+                buffer[at, :] = chunks[k][s * padded + start : s * padded + start + count, :]
+
+    flat_tiles(modes, groups, write, out_hbm, buffer, sems)
+
+
+def final_kernel(parts, modes, padded, per, *refs):
+    chunks, (base, out_hbm, buffer, sems) = refs[:parts], refs[parts:]
+    me = lax.axis_index("modes")
+    groups = parts * per
+
+    def write(start, count):
+        for k in range(parts):
+            q = origin_of(H_SWAP, me, k, parts)
+            for s in range(per):
+                at = pl.multiple_of((q * per + s) * padded + start, SUB)
+                within = s * padded + start
+                rows = base[pl.ds(at, SUB), :] + 0.1 * chunks[k][within : within + SUB, :]
+                buffer[pl.ds(start * groups + q * per + s, count, stride=groups), :] = rows[:count]
+
+    flat_tiles(modes, groups, write, out_hbm, buffer, sems)
+
+
+def call(kernel, out_shape, args, scratch=(), smem=(), hbm=(), limit=VMEM_LIMIT, out_hbm=False):
     specs = [
         pl.BlockSpec(
             memory_space=pltpu.SMEM if i in smem else pltpu.HBM if i in hbm else pltpu.VMEM
@@ -388,25 +446,25 @@
         for i in range(len(args))
     ]
     many = isinstance(out_shape, (list, tuple))
-    vmem = pl.BlockSpec(memory_space=pltpu.VMEM)
+    where = pl.BlockSpec(memory_space=pltpu.HBM if out_hbm else pltpu.VMEM)
     nbytes = sum(x.size * x.dtype.itemsize for x in args)
     return pl.pallas_call(
         kernel,
         out_shape=out_shape,
         in_specs=specs,
-        out_specs=[vmem] * len(out_shape) if many else vmem,
+        out_specs=[where] * len(out_shape) if many else where,
         scratch_shapes=list(scratch),
         compiler_params=pltpu.CompilerParams(vmem_limit_bytes=limit),
         cost_estimate=pl.CostEstimate(flops=0, bytes_accessed=nbytes, transcendentals=0),
     )(*args)
 
 
-def exchange(chunks):
+def exchange(chunks, swap):
     parts = lax.axis_size("modes")
-    received = [chunks[0]]
+    received = list(chunks)
     for k in range(1, parts):
-        pairs = [(i, (i + k) % parts) for i in range(parts)]
-        received.append(lax.ppermute(chunks[k], "modes", pairs))
+        pairs = [(i, target_of(swap, i, k, parts)) for i in range(parts)]
+        received[k] = lax.ppermute(chunks[k], "modes", pairs)
     return received
 
 
@@ -451,7 +509,6 @@
     v, cur, temp = flat(voltage_expansion), flat(current_injection), flat(thermal_state)
     avg = average_electric_transport.reshape(groups, LANES)
     zone = material_zone.reshape(groups, LANES)
-    chunk = struct(per * padded, LANES)
     rimmed = struct(per * padded + SUB, LANES)
     grouped = pltpu.VMEM((groups * padded, LANES), F32)
 
@@ -465,13 +522,13 @@
         hbm=(0, 1, 2),
         limit=62 * 1024 * 1024,
     )
-    source = exchange(source)
+    source = exchange(source, W_SWAP)
     temp, source[1] = lax.optimization_barrier((temp, source[1]))
     a_high, a_low, b_high, b_low, w_high, w_low, lift, zones = call(
         functools.partial(tables_kernel, parts, modes, padded),
         [
-            struct(nreg * rows, rows, dtype=BF16),
-            struct(nreg * rows, rows, dtype=BF16),
+            struct(parts, rows, nreg * padded, dtype=BF16),
+            struct(parts, rows, nreg * padded, dtype=BF16),
             struct(points, rows, dtype=BF16),
             struct(points, rows, dtype=BF16),
             struct(rows, points, dtype=BF16),
@@ -494,24 +551,29 @@
         functools.partial(rough_kernel, parts, modes, padded, groups),
         [rimmed] * parts, [v, v_near, v_far], [grouped],
     )
-    rough = exchange(rough)
+    rough = exchange(rough, R_SWAP)
     t_near, t_far = halo(temp)
     base = call(
         functools.partial(thermal_kernel, modes, padded, groups),
         struct(groups * padded, LANES), [temp, t_near, t_far],
     )
     wide = (per + 1) * LANES
-    half_width = per * LANES // halves
-    results = call(
-        functools.partial(couple_kernel, parts, padded, per, nreg, halves),
-        [struct(rows, half_width)] * halves + [struct(rows, LANES)] + [chunk] * parts,
-        [*source, *rough, a_high, a_low, zones],
-        [pltpu.VMEM((rows, wide), F32), pltpu.VMEM((rows, wide), F32)],
-    )
-    relaxed, rim, back = results[:halves], results[halves], list(results[halves + 1 :])
+    count = parts - 1
+    most = call(
+        functools.partial(couple_kernel, parts, padded, per, nreg, count),
+        struct(rows, wide), [*source, *rough[:count], a_high, a_low, zones],
+    )
+    relaxed, rim, *back = call(
+        functools.partial(relax_kernel, parts, padded, per, nreg, count),
+        [struct(rows, per * LANES), struct(rows, LANES)]
+        + [struct(per * padded, LANES)] * parts,
+        [*rough[count:], most, a_high, a_low, zones],
+        [pltpu.VMEM((rows, per * LANES), F32)],
+    )
+    relaxed = [relaxed]
     beside = [halo(x) for x in relaxed]
-    base, rim, back[2] = lax.optimization_barrier((base, rim, back[2]))
-    back = exchange(back)
+    base, back[2] = lax.optimization_barrier((base, back[2]))
+    back = exchange(back, B_SWAP)
     part, spread = call(
         functools.partial(plane_kernel, nreg, halves),
         [struct(points, per * LANES)] * 2,
@@ -523,16 +585,17 @@
             functools.partial(joule_kernel, parts, padded, per, halves, half),
             [struct(per // halves * padded, LANES)] * parts,
             [*beside[half], part, spread, avg, b_high, b_low, w_high, w_low],
-            [pltpu.VMEM((rows, half_width), F32)],
+            [pltpu.VMEM((rows, per * LANES // halves), F32)],
         )
-        heat += exchange(pieces)
+        heat += exchange(pieces, H_SWAP)
+    tiled = [fields, pltpu.SemaphoreType.DMA((padded // SUB,))]
     relaxed_voltage = call(
         functools.partial(gather_kernel, parts, modes, padded, per),
-        struct(modes * groups, LANES), back,
+        struct(modes * groups, LANES), back, tiled, out_hbm=True,
     )
     advanced = call(
-        functools.partial(final_kernel, parts, modes, padded, per, halves),
-        struct(modes * groups, LANES), [*heat, base],
+        functools.partial(final_kernel, parts, modes, padded, per),
+        struct(modes * groups, LANES), [*heat, base], tiled, out_hbm=True,
     )
     shape = voltage_expansion.shape
     return relaxed_voltage.reshape(shape), advanced.reshape(shape)

time: 60.1 us -> 60 us (level)
  waiting for transfers between devices: 18.8 us -> 17.7 us
  starting transfers between devices: 26 us -> 26.8 us
    ppermute x3, waiting for transfers between devices: 6.39 us -> 4.32 us  [halo(): far = lax.ppermute(x, 'space', far)]
    ppermute x12, starting transfers between devices: 14.7 us -> 15.6 us  [exchange(): received[k] = lax.ppermute(chunks[k], 'modes', pairs)]
    ppermute x12, waiting for transfers between devices: 12.5 us -> 13.3 us  [exchange(): received[k] = lax.ppermute(chunks[k], 'modes', pairs)]
    pallas_call x9 -> x10, Pallas kernels: 13.5 us -> 13.8 us  [call(): pl.pallas_call(kernel, out_shape=out_shape, in_specs=specs, out_specs=[wh...]
  transfers between devices with their start and end apart: 18 -> 18, of which waited for: 8 -> 7; matrix products, arithmetic and copies ran while one was open for 0% -> 0% of each run, Pallas kernels for 21% -> 22%
where the time goes in v5:
time: 60 us; the launch traced here: 59.8 us
  starting transfers between devices  26.8 us (45%)
  waiting for transfers between devices  17.7 us (30%)
  Pallas kernels  13.8 us (23%)
  between operations  0.84 us (1%)
  local copies, waits for them, and re-layouts  0.71 us (1%)
    ppermute x12, starting transfers between devices, exchange(): received[k] = lax.ppermute(chunks[k], 'modes', pairs)  15.6 us
    pallas_call x10, Pallas kernels, call(): pl.pallas_call(kernel, out_shape=out_shape, in_specs=specs, out_specs=[wh...  13.8 us
    ppermute x12, waiting for transfers between devices, exchange(): received[k] = lax.ppermute(chunks[k], 'modes', pairs)  13.3 us
    ppermute x3, starting transfers between devices, halo(): far = lax.ppermute(x, 'space', far)  9.88 us
    ppermute x3, waiting for transfers between devices, halo(): far = lax.ppermute(x, 'space', far)  4.32 us
    ppermute x3, starting transfers between devices, halo(): return (lax.ppermute(x, 'space', near), far)  1.27 us
  transfers between devices with their start and end apart: 18, of which 7 were waited for; matrix products, arithmetic and copies ran while one was open for 0% of the time, Pallas kernels for 22%

profile of v5, /device:TPU:11, one launch (start us, length us, event | category | flops | bytes accessed | tf_op | source)
XLA Modules:
  0.0 59.8 jit_solution(10802982869942312293)
XLA Ops:
  1.4 3.0 %collective-permute-start.1 = (f32[880,128]{1,0:T(8,128)}, f32[880,128]{1,0:T(8,128)S(1)}, u32[]{:S(2)}, u32[]{:S(2)}) collective-permute-start(f32[880,128]{1,0:T(8,128)} %bitcast.11), channel_id=1, source_target_pairs={{4,8},{8,4},{12,16},{16,12},{20,24},{24,20},{5,9},{9,5},{13,17},{1... | collective-permute-start | bytes 1351688 | tf_op jit(solution)/shard_map/ppermute | solution.py:475
  4.4 2.4 %shard_map.106 = (f32[232,128]{1,0:T(8,128)}, f32[232,128]{1,0:T(8,128)}, f32[232,128]{1,0:T(8,128)}, f32[232,128]{1,0:T(8,128)}) custom-call(f32[880,128]{1,0:T(8,128)} %bitcast.12, f32[880,128]{1,0:T(8,128)} %bitcast.23, f32[16,128]{1,0:T(8,128)} %bitcast.17), custom_call_target="tpu_custom_call" | custom-call | bytes 909312 | tf_op jit(solution)/shard_map/pallas_call | solution.py:451
  6.9 1.3 %collective-permute-start.3 = (f32[232,128]{1,0:T(8,128)}, f32[232,128]{1,0:T(8,128)S(1)}, u32[]{:S(2)}, u32[]{:S(2)}) collective-permute-start(f32[232,128]{1,0:T(8,128)} %get-tuple-element.40), channel_id=1, source_target_pairs={{0,1},{1,2},{2,3},{3,0},{4,5},{5,6},{6,7},{7,4},{8,9},{9,10},{10,1... | collective-permute-start | bytes 356360 | tf_op jit(solution)/shard_map/ppermute | solution.py:467
  8.2 1.1 %collective-permute-start.4 = (f32[232,128]{1,0:T(8,128)}, f32[232,128]{1,0:T(8,128)S(1)}, u32[]{:S(2)}, u32[]{:S(2)}) collective-permute-start(f32[232,128]{1,0:T(8,128)} %get-tuple-element.42), channel_id=1, source_target_pairs={{0,2},{1,3},{2,0},{3,1},{4,6},{5,7},{6,4},{7,5},{8,10},{9,11},{10,... | collective-permute-start | bytes 356360 | tf_op jit(solution)/shard_map/ppermute | solution.py:467
  9.3 1.4 %collective-permute-start.5 = (f32[232,128]{1,0:T(8,128)}, f32[232,128]{1,0:T(8,128)S(1)}, u32[]{:S(2)}, u32[]{:S(2)}) collective-permute-start(f32[232,128]{1,0:T(8,128)} %get-tuple-element.43), channel_id=1, source_target_pairs={{0,3},{1,0},{2,1},{3,2},{4,7},{5,4},{6,5},{7,6},{8,11},{9,8},{10,9... | collective-permute-start | bytes 356360 | tf_op jit(solution)/shard_map/ppermute | solution.py:467
  11.4 3.9 %shard_map.104 = (bf16[4,224,224]{2,1,0:T(8,128)(2,1)S(1)}, bf16[4,224,224]{2,1,0:T(8,128)(2,1)S(1)}, bf16[512,224]{1,0:T(8,128)(2,1)S(1)}, bf16[512,224]{1,0:T(...) custom-call(s32[9,220]{1,0:T(8,128)S(1)} %bitcast.20, ...), custom_call_target="tpu_custom_call" | custom-call | bytes 36736 | tf_op jit(solution)/shard_map/pallas_call | solution.py:451
  15.3 1.1 %collective-permute-done.1.far_ref = f32[880,128]{1,0:T(8,128)S(1)} collective-permute-done((f32[880,128]{1,0:T(8,128)}, f32[880,128]{1,0:T(8,128)S(1)}, u32[]{:S(2)}, u32[]{:S(2)}) %collective-permute-start.1) | collective-permute-done | bytes 450592 | tf_op jit(solution)/shard_map/ppermute | solution.py:475
  16.4 0.9 %shard_map.105 = (f32[232,128]{1,0:T(8,128)S(1)}, f32[232,128]{1,0:T(8,128)S(1)}, f32[232,128]{1,0:T(8,128)S(1)}, f32[232,128]{1,0:T(8,128)S(1)}) custom-call(f32[880,128]{1,0:T(8,128)S(1)} %bitcast.13, f32[880,128]{1,0:T(8,128)S(1)} %collective-permute-done.near_ref, f32[880,128]{1,0:T(8,128)S(1)} %collective-permute-done.1.far_ref), custom_call_target="tpu_custom_call" | custom-call | bytes 1351680 | tf_op jit(solution)/shard_map/pallas_call | solution.py:451
  17.8 2.2 %collective-permute-start.7 = (f32[232,128]{1,0:T(8,128)S(1)}, f32[232,128]{1,0:T(8,128)S(1)}, u32[]{:S(2)}, u32[]{:S(2)}) collective-permute-start(f32[232,128]{1,0:T(8,128)S(1)} %get-tuple-element.46), channel_id=1, source_target_pairs={{0,2},{1,3},{2,0},{3,1},{4,6},{5,7},{6,4},{7,5},{8,10},{9,11},{10,... | collective-permute-start | bytes 356360 | tf_op jit(solution)/shard_map/ppermute | solution.py:467
  20.3 4.1 %collective-permute-start.10 = (f32[880,128]{1,0:T(8,128)S(1)}, f32[880,128]{1,0:T(8,128)S(1)}, u32[]{:S(2)}, u32[]{:S(2)}) collective-permute-start(f32[880,128]{1,0:T(8,128)S(1)} %bitcast.14), channel_id=1, source_target_pairs={{4,8},{8,4},{12,16},{16,12},{20,24},{24,20},{5,9},{9,5},{13,17},{1... | collective-permute-start | bytes 1351688 | tf_op jit(solution)/shard_map/ppermute | solution.py:475
  24.4 3.6 %collective-permute-done.7.refs_6_ = f32[232,128]{1,0:T(8,128)S(1)} collective-permute-done((f32[232,128]{1,0:T(8,128)S(1)}, f32[232,128]{1,0:T(8,128)S(1)}, u32[]{:S(2)}, u32[]{:S(2)}) %collective-permute-start.7) | collective-permute-done | bytes 118816 | tf_op jit(solution)/shard_map/ppermute | solution.py:467
  28.0 1.0 %shard_map.107.refs_1_ = f32[224,640]{1,0:T(8,128)S(1)} custom-call(f32[232,128]{1,0:T(8,128)S(1)} %copy-done.2, f32[232,128]{1,0:T(8,128)S(1)} %collective-permute-done.3.refs_1_, f32[232,128]{1,0:T(8,128)S(1)} %collective-permute-done.4.refs_2_, f32[232,128]{1,0:T(8,128)S(1)} %collective-permute-done.5.refs_3_, f32[232,128]{1,0:T(8,128)S(1)} %get-tuple-element.44.refs_4_, ...), custom_call_target="tpu_custom_call" | custom-call | bytes 1636864 | tf_op jit(solution)/shard_map/pallas_call | solution.py:451
  29.1 2.2 %collective-permute-done.2.refs_0_ = f32[232,128]{1,0:T(8,128)S(1)} collective-permute-done((f32[232,128]{1,0:T(8,128)S(1)}, f32[232,128]{1,0:T(8,128)S(1)}, u32[]{:S(2)}, u32[]{:S(2)}) %collective-permute-start.2) | collective-permute-done | bytes 118816 | tf_op jit(solution)/shard_map/ppermute | solution.py:467
  32.2 2.8 %collective-permute-start.14 = (f32[224,512]{1,0:T(8,128)S(1)}, f32[224,512]{1,0:T(8,128)S(1)}, u32[]{:S(2)}, u32[]{:S(2)}) collective-permute-start(f32[224,512]{1,0:T(8,128)S(1)} %get-tuple-element.56.refs_0_), channel_id=1, source_target_pairs={{4,8},{8,4},{12,16},{16,12},{20,24},{24,20},{5,9},{9,5},{13,17},{1... | collective-permute-start | bytes 1376264 | tf_op jit(solution)/shard_map/ppermute | solution.py:475
  35.8 3.9 %collective-permute-start.11 = (f32[224,128]{1,0:T(8,128)S(1)}, f32[224,128]{1,0:T(8,128)S(1)}, u32[]{:S(2)}, u32[]{:S(2)}) collective-permute-start(f32[224,128]{1,0:T(8,128)S(1)} %get-tuple-element.54), channel_id=1, source_target_pairs={{0,2},{1,3},{2,0},{3,1},{4,6},{5,7},{6,4},{7,5},{8,10},{9,11},{10,... | collective-permute-start | bytes 344072 | tf_op jit(solution)/shard_map/ppermute | solution.py:467
  39.7 1.5 %collective-permute-start.8 = (f32[224,128]{1,0:T(8,128)S(1)}, f32[224,128]{1,0:T(8,128)S(1)}, u32[]{:S(2)}, u32[]{:S(2)}) collective-permute-start(f32[224,128]{1,0:T(8,128)S(1)} %get-tuple-element.51), channel_id=1, source_target_pairs={{0,1},{1,2},{2,3},{3,0},{4,5},{5,6},{6,7},{7,4},{8,9},{9,10},{10,1... | collective-permute-start | bytes 344072 | tf_op jit(solution)/shard_map/ppermute | solution.py:467
  41.2 1.5 %shard_map.111 = (f32[512,512]{1,0:T(8,128)S(1)}, f32[512,512]{1,0:T(8,128)S(1)}) custom-call(f32[224,512]{1,0:T(8,128)S(1)} %get-tuple-element.56.refs_0_, f32[224,128]{1,0:T(8,128)S(1)} %get-tuple-element.57.refs_1_, s32[1,640]{1,0:T(1,128)S(1)} %get-tuple-element.49.refs_9_.refs_4_.refs_2_, bf16[512,224]{1,0:T(8,128)(2,1)S(1)} %get-tuple-element.58.refs_3_.bh_ref, ...), custom_call_target="tpu_custom_call" | custom-call | bytes 1165824 | tf_op jit(solution)/shard_map/pallas_call | solution.py:451
  42.7 3.2 %collective-permute-done.14.far_ref = f32[224,512]{1,0:T(8,128)S(1)} collective-permute-done((f32[224,512]{1,0:T(8,128)S(1)}, f32[224,512]{1,0:T(8,128)S(1)}, u32[]{:S(2)}, u32[]{:S(2)}) %collective-permute-start.14) | collective-permute-done | bytes 458784 | tf_op jit(solution)/shard_map/ppermute | solution.py:475
  45.9 1.2 %shard_map.112 = (f32[224,128]{1,0:T(8,128)S(1)}, f32[224,128]{1,0:T(8,128)S(1)}, f32[224,128]{1,0:T(8,128)S(1)}, f32[224,128]{1,0:T(8,128)S(1)}) custom-call(f32[224,512]{1,0:T(8,128)S(1)} %collective-permute-done.13.near_ref, f32[224,512]{1,0:T(8,128)S(1)} %collective-permute-done.14.far_ref, f32[512,512]{1,0:T(8,128)S(1)} %get-tuple-element.61.part_ref, ...), custom_call_target="tpu_custom_call" | custom-call | bytes 3940352 | tf_op jit(solution)/shard_map/pallas_call | solution.py:451
  47.7 2.4 %collective-permute-start.16 = (f32[224,128]{1,0:T(8,128)S(1)}, f32[224,128]{1,0:T(8,128)S(1)}, u32[]{:S(2)}, u32[]{:S(2)}) collective-permute-start(f32[224,128]{1,0:T(8,128)S(1)} %get-tuple-element.67), channel_id=1, source_target_pairs={{0,2},{1,3},{2,0},{3,1},{4,6},{5,7},{6,4},{7,5},{8,10},{9,11},{10,... | collective-permute-start | bytes 344072 | tf_op jit(solution)/shard_map/ppermute | solution.py:467
  50.6 0.8 %shard_map.110 = f32[880,128]{1,0:T(8,128)} custom-call(f32[224,128]{1,0:T(8,128)S(1)} %get-tuple-element.50.refs_0_, f32[224,128]{1,0:T(8,128)S(1)} %collective-permute-done.8.refs_1_, f32[224,128]{1,0:T(8,128)S(1)} %collective-permute-done.11.refs_2_, f32[224,128]{1,0:T(8,128)S(1)} %collective-permute-done.12.refs_3_), custom_call_target="tpu_custom_call" | custom-call | bytes 458752 | tf_op jit(solution)/shard_map/pallas_call | solution.py:451
  52.0 4.8 %collective-permute-done.16.refs_2_ = f32[224,128]{1,0:T(8,128)S(1)} collective-permute-done((f32[224,128]{1,0:T(8,128)S(1)}, f32[224,128]{1,0:T(8,128)S(1)}, u32[]{:S(2)}, u32[]{:S(2)}) %collective-permute-start.16) | collective-permute-done | bytes 114720 | tf_op jit(solution)/shard_map/ppermute | solution.py:467
  56.8 2.2 %collective-permute-done.17.refs_3_ = f32[224,128]{1,0:T(8,128)S(1)} collective-permute-done((f32[224,128]{1,0:T(8,128)S(1)}, f32[224,128]{1,0:T(8,128)S(1)}, u32[]{:S(2)}, u32[]{:S(2)}) %collective-permute-start.17) | collective-permute-done | bytes 114720 | tf_op jit(solution)/shard_map/ppermute | solution.py:467
  58.9 0.8 %shard_map.113 = f32[880,128]{1,0:T(8,128)} custom-call(f32[224,128]{1,0:T(8,128)S(1)} %get-tuple-element.65.refs_0_, f32[224,128]{1,0:T(8,128)S(1)} %collective-permute-done.15.refs_1_, f32[224,128]{1,0:T(8,128)S(1)} %collective-permute-done.16.refs_2_, f32[224,128]{1,0:T(8,128)S(1)} %collective-permute-done.17.refs_3_, f32[896,128]{1,0:T(8,128)S(1)} %shard_map.109.refs_4_), custom_call_target="tpu_custom_call" | custom-call | bytes 917504 | tf_op jit(solution)/shard_map/pallas_call | solution.py:451
  (40 shorter events, 5.7 us)
Async XLA Ops:
  0.6 14.7 %collective-permute-start = (f32[880,128]{1,0:T(8,128)}, f32[880,128]{1,0:T(8,128)S(1)}, u32[]{:S(2)}, u32[]{:S(2)}) collective-permute-start(f32[880,128]{1,0:T(8,128)} %bitcast.10), channel_id=1, source_target_pairs={{0,4},{4,0},{8,12},{12,8},{16,20},{20,16},{24,28},{28,24},{1,5},{5... | collective-permute-start | bytes 1351688 | tf_op jit(solution)/shard_map/ppermute | solution.py:476
  1.4 15.0 %collective-permute-start.1 = (f32[880,128]{1,0:T(8,128)}, f32[880,128]{1,0:T(8,128)S(1)}, u32[]{:S(2)}, u32[]{:S(2)}) collective-permute-start(f32[880,128]{1,0:T(8,128)} %bitcast.11), channel_id=1, source_target_pairs={{4,8},{8,4},{12,16},{16,12},{20,24},{24,20},{5,9},{9,5},{13,17},{1... | collective-permute-start | bytes 1351688 | tf_op jit(solution)/shard_map/ppermute | solution.py:475
  4.4 6.3 %copy-start.4 = (s32[512,9]{0,1:T(8,128)S(1)}, s32[512,9]{0,1:T(8,128)}, u32[]{:S(2)}) copy-start(s32[512,9]{0,1:T(8,128)} %param.16) | copy-start | bytes 55300
  4.4 6.3 %copy-start.5 = (s32[220,9]{0,1:T(8,128)S(1)}, s32[220,9]{0,1:T(8,128)}, u32[]{:S(2)}) copy-start(s32[220,9]{0,1:T(8,128)} %param.15) | copy-start | bytes 23764
  4.4 12.0 %copy-start = (f32[55,1,2048]{2,1,0:T(1,128)S(1)}, f32[55,1,2048]{2,1,0:T(1,128)}, u32[]{:S(2)}) copy-start(f32[55,1,2048]{2,1,0:T(1,128)} %param.9) | copy-start | bytes 1351684
  6.9 13.2 %collective-permute-start.3 = (f32[232,128]{1,0:T(8,128)}, f32[232,128]{1,0:T(8,128)S(1)}, u32[]{:S(2)}, u32[]{:S(2)}) collective-permute-start(f32[232,128]{1,0:T(8,128)} %get-tuple-element.40), channel_id=1, source_target_pairs={{0,1},{1,2},{2,3},{3,0},{4,5},{5,6},{6,7},{7,4},{8,9},{9,10},{10,1... | collective-permute-start | bytes 356360 | tf_op jit(solution)/shard_map/ppermute | solution.py:467
  8.2 12.0 %collective-permute-start.4 = (f32[232,128]{1,0:T(8,128)}, f32[232,128]{1,0:T(8,128)S(1)}, u32[]{:S(2)}, u32[]{:S(2)}) collective-permute-start(f32[232,128]{1,0:T(8,128)} %get-tuple-element.42), channel_id=1, source_target_pairs={{0,2},{1,3},{2,0},{3,1},{4,6},{5,7},{6,4},{7,5},{8,10},{9,11},{10,... | collective-permute-start | bytes 356360 | tf_op jit(solution)/shard_map/ppermute | solution.py:467
  9.3 15.0 %collective-permute-start.5 = (f32[232,128]{1,0:T(8,128)}, f32[232,128]{1,0:T(8,128)S(1)}, u32[]{:S(2)}, u32[]{:S(2)}) collective-permute-start(f32[232,128]{1,0:T(8,128)} %get-tuple-element.43), channel_id=1, source_target_pairs={{0,3},{1,0},{2,1},{3,2},{4,7},{5,4},{6,5},{7,6},{8,11},{9,8},{10,9... | collective-permute-start | bytes 356360 | tf_op jit(solution)/shard_map/ppermute | solution.py:467
  15.3 5.0 %copy-start.1 = (f32[55,1,2048]{2,1,0:T(1,128)S(1)}, f32[55,1,2048]{2,1,0:T(1,128)}, u32[]{:S(2)}) copy-start(f32[55,1,2048]{2,1,0:T(1,128)} %param.11) | copy-start | bytes 1351684
  15.3 12.7 %copy-start.2 = (f32[232,128]{1,0:T(8,128)S(1)}, f32[232,128]{1,0:T(8,128)}, u32[]{:S(2)}) copy-start(f32[232,128]{1,0:T(8,128)} %get-tuple-element.39.refs_0_) | copy-start | bytes 356356
  17.3 7.1 %collective-permute-start.6 = (f32[232,128]{1,0:T(8,128)S(1)}, f32[232,128]{1,0:T(8,128)S(1)}, u32[]{:S(2)}, u32[]{:S(2)}) collective-permute-start(f32[232,128]{1,0:T(8,128)S(1)} %get-tuple-element.45), channel_id=1, source_target_pairs={{0,1},{1,0},{2,3},{3,2},{4,5},{5,4},{6,7},{7,6},{8,9},{9,8},{10,11... | collective-permute-start | bytes 356360 | tf_op jit(solution)/shard_map/ppermute | solution.py:467
  17.8 10.2 %collective-permute-start.7 = (f32[232,128]{1,0:T(8,128)S(1)}, f32[232,128]{1,0:T(8,128)S(1)}, u32[]{:S(2)}, u32[]{:S(2)}) collective-permute-start(f32[232,128]{1,0:T(8,128)S(1)} %get-tuple-element.46), channel_id=1, source_target_pairs={{0,2},{1,3},{2,0},{3,1},{4,6},{5,7},{6,4},{7,5},{8,10},{9,11},{10,... | collective-permute-start | bytes 356360 | tf_op jit(solution)/shard_map/ppermute | solution.py:467
  20.0 11.2 %collective-permute-start.2 = (f32[232,128]{1,0:T(8,128)S(1)}, f32[232,128]{1,0:T(8,128)S(1)}, u32[]{:S(2)}, u32[]{:S(2)}) collective-permute-start(f32[232,128]{1,0:T(8,128)S(1)} %get-tuple-element.38), channel_id=1, source_target_pairs={{0,3},{1,2},{2,1},{3,0},{4,7},{5,6},{6,5},{7,4},{8,11},{9,10},{10,... | collective-permute-start | bytes 356360 | tf_op jit(solution)/shard_map/ppermute | solution.py:467
  20.3 14.8 %collective-permute-start.10 = (f32[880,128]{1,0:T(8,128)S(1)}, f32[880,128]{1,0:T(8,128)S(1)}, u32[]{:S(2)}, u32[]{:S(2)}) collective-permute-start(f32[880,128]{1,0:T(8,128)S(1)} %bitcast.14), channel_id=1, source_target_pairs={{4,8},{8,4},{12,16},{16,12},{20,24},{24,20},{5,9},{9,5},{13,17},{1... | collective-permute-start | bytes 1351688 | tf_op jit(solution)/shard_map/ppermute | solution.py:475
  24.3 10.8 %collective-permute-start.9 = (f32[880,128]{1,0:T(8,128)S(1)}, f32[880,128]{1,0:T(8,128)S(1)}, u32[]{:S(2)}, u32[]{:S(2)}) collective-permute-start(f32[880,128]{1,0:T(8,128)S(1)} %bitcast.15), channel_id=1, source_target_pairs={{0,4},{4,0},{8,12},{12,8},{16,20},{20,16},{24,28},{28,24},{1,5},{5... | collective-permute-start | bytes 1351688 | tf_op jit(solution)/shard_map/ppermute | solution.py:476
  31.8 10.9 %collective-permute-start.13 = (f32[224,512]{1,0:T(8,128)S(1)}, f32[224,512]{1,0:T(8,128)S(1)}, u32[]{:S(2)}, u32[]{:S(2)}) collective-permute-start(f32[224,512]{1,0:T(8,128)S(1)} %get-tuple-element.56.refs_0_), channel_id=1, source_target_pairs={{0,4},{4,0},{8,12},{12,8},{16,20},{20,16},{24,28},{28,24},{1,5},{5... | collective-permute-start | bytes 1376264 | tf_op jit(solution)/shard_map/ppermute | solution.py:476
  32.2 13.7 %collective-permute-start.14 = (f32[224,512]{1,0:T(8,128)S(1)}, f32[224,512]{1,0:T(8,128)S(1)}, u32[]{:S(2)}, u32[]{:S(2)}) collective-permute-start(f32[224,512]{1,0:T(8,128)S(1)} %get-tuple-element.56.refs_0_), channel_id=1, source_target_pairs={{4,8},{8,4},{12,16},{16,12},{20,24},{24,20},{5,9},{9,5},{13,17},{1... | collective-permute-start | bytes 1376264 | tf_op jit(solution)/shard_map/ppermute | solution.py:475
  35.8 14.3 %collective-permute-start.11 = (f32[224,128]{1,0:T(8,128)S(1)}, f32[224,128]{1,0:T(8,128)S(1)}, u32[]{:S(2)}, u32[]{:S(2)}) collective-permute-start(f32[224,128]{1,0:T(8,128)S(1)} %get-tuple-element.54), channel_id=1, source_target_pairs={{0,2},{1,3},{2,0},{3,1},{4,6},{5,7},{6,4},{7,5},{8,10},{9,11},{10,... | collective-permute-start | bytes 344072 | tf_op jit(solution)/shard_map/ppermute | solution.py:467
  39.7 10.9 %collective-permute-start.12 = (f32[224,128]{1,0:T(8,128)S(1)}, f32[224,128]{1,0:T(8,128)S(1)}, u32[]{:S(2)}, u32[]{:S(2)}) collective-permute-start(f32[224,128]{1,0:T(8,128)S(1)} %get-tuple-element.55), channel_id=1, source_target_pairs={{0,3},{1,0},{2,1},{3,2},{4,7},{5,4},{6,5},{7,6},{8,11},{9,8},{10,9... | collective-permute-start | bytes 344072 | tf_op jit(solution)/shard_map/ppermute | solution.py:467
  39.7 10.9 %collective-permute-start.8 = (f32[224,128]{1,0:T(8,128)S(1)}, f32[224,128]{1,0:T(8,128)S(1)}, u32[]{:S(2)}, u32[]{:S(2)}) collective-permute-start(f32[224,128]{1,0:T(8,128)S(1)} %get-tuple-element.51), channel_id=1, source_target_pairs={{0,1},{1,2},{2,3},{3,0},{4,5},{5,6},{6,7},{7,4},{8,9},{9,10},{10,1... | collective-permute-start | bytes 344072 | tf_op jit(solution)/shard_map/ppermute | solution.py:467
  41.2 4.8 %copy-start.3 = (f32[1,2048]{1,0:T(1,128)S(1)}, f32[1,2048]{1,0:T(1,128)}, u32[]{:S(2)}) copy-start(f32[1,2048]{1,0:T(1,128)} %param.12) | copy-start | bytes 24580
  47.1 4.9 %collective-permute-start.15 = (f32[224,128]{1,0:T(8,128)S(1)}, f32[224,128]{1,0:T(8,128)S(1)}, u32[]{:S(2)}, u32[]{:S(2)}) collective-permute-start(f32[224,128]{1,0:T(8,128)S(1)} %get-tuple-element.66), channel_id=1, source_target_pairs={{0,1},{1,2},{2,3},{3,0},{4,5},{5,6},{6,7},{7,4},{8,9},{9,10},{10,1... | collective-permute-start | bytes 344072 | tf_op jit(solution)/shard_map/ppermute | solution.py:467
  47.7 9.1 %collective-permute-start.16 = (f32[224,128]{1,0:T(8,128)S(1)}, f32[224,128]{1,0:T(8,128)S(1)}, u32[]{:S(2)}, u32[]{:S(2)}) collective-permute-start(f32[224,128]{1,0:T(8,128)S(1)} %get-tuple-element.67), channel_id=1, source_target_pairs={{0,2},{1,3},{2,0},{3,1},{4,6},{5,7},{6,4},{7,5},{8,10},{9,11},{10,... | collective-permute-start | bytes 344072 | tf_op jit(solution)/shard_map/ppermute | solution.py:467
  50.0 8.9 %collective-permute-start.17 = (f32[224,128]{1,0:T(8,128)S(1)}, f32[224,128]{1,0:T(8,128)S(1)}, u32[]{:S(2)}, u32[]{:S(2)}) collective-permute-start(f32[224,128]{1,0:T(8,128)S(1)} %get-tuple-element.68), channel_id=1, source_target_pairs={{0,3},{1,0},{2,1},{3,2},{4,7},{5,4},{6,5},{7,6},{8,11},{9,8},{10,9... | collective-permute-start | bytes 344072 | tf_op jit(solution)/shard_map/ppermute | solution.py:467
  (3 other events, 5.2 us)

commit v6 on v5

--- a/solution.py
+++ b/solution.py
@@ -70,13 +70,14 @@
 
 
 def load_group(ref, group, modes, groups):
-    return ref[pl.ds(group, modes, stride=groups), :]
-
-
-def pad_rows(x, rows):
-    if x.shape[0] == rows:
-        return x
-    return jnp.concatenate([x, jnp.zeros((rows - x.shape[0], x.shape[1]), x.dtype)], axis=0)
+    spare = modes % SUB
+    main = modes - spare
+    if not spare:
+        return ref[pl.ds(group, modes, stride=groups), :]
+    last = ref[pl.ds((modes - SUB) * groups + group, SUB, stride=groups), :]
+    row = lax.broadcasted_iota(jnp.int32, last.shape, 0)
+    last = jnp.where(row < spare, pltpu.roll(last, spare, 0), 0.0)
+    return jnp.concatenate([ref[pl.ds(group, main, stride=groups), :], last], axis=0)
 
 
 def emit_slots(swap, me, parts, grouped, outs, padded):
@@ -111,6 +112,7 @@
     for copy in copies:
         copy.start()
     me = lax.axis_index("modes")
+    row = lax.broadcasted_iota(jnp.int32, (SUB, LANES), 0)
     copies[0].wait()
     factor = 0.8 / (6.0 * a_ref[...])
     for tile, start in enumerate(starts):
@@ -118,20 +120,22 @@
         copies[2 * tile + 2].wait()
         count = min(SUB, modes - start)
         for g in range(groups):
-            rows = pl.ds(start * groups + g, count, stride=groups)
+            rows = pl.ds(start * groups + g, SUB, stride=groups)
             w = v_ref[rows, :] + j_ref[rows, :] * factor[g : g + 1]
-            grouped[g * padded + start : g * padded + start + SUB, :] = pad_rows(w, SUB)
+            if count < SUB:
+                w = jnp.where(row < count, w, 0.0)
+            grouped[g * padded + start : g * padded + start + SUB, :] = w
     emit_slots(W_SWAP, me, parts, grouped, outs, padded)
 
 
 def stencil_groups(x_ref, near_ref, far_ref, modes, groups, padded, emit):
     lane = lane_ids((padded, LANES))
     depth = lane % NZ
-    fields = [pad_rows(load_group(x_ref, g, modes, groups), padded) for g in range(groups)]
+    fields = [load_group(x_ref, g, modes, groups) for g in range(groups)]
     for g in range(groups):
         x = fields[g]
-        total = 6.0 * x - pad_rows(load_group(near_ref, g, modes, groups), padded)
-        total = total - pad_rows(load_group(far_ref, g, modes, groups), padded)
+        total = 6.0 * x - load_group(near_ref, g, modes, groups)
+        total = total - load_group(far_ref, g, modes, groups)
         total = total - jnp.where(depth < NZ - 1, pltpu.roll(x, LANES - 1, 1), 0.0)
         total = total - jnp.where(depth > 0, pltpu.roll(x, 1, 1), 0.0)
         right = fields[g + 1] if g + 1 < groups else jnp.zeros_like(x)
@@ -397,7 +401,7 @@
     copies = []
     for tile, start in enumerate(range(0, modes, SUB)):
         count = min(SUB, modes - start)
-        write(start, count)
+        write(start)
         rows = pl.ds(start * groups, count * groups)
         copy = pltpu.make_async_copy(buffer.at[rows], out_hbm.at[rows], sems.at[tile])
         copy.start()
@@ -411,12 +415,12 @@
     me = lax.axis_index("modes")
     groups = parts * per
 
-    def write(start, count):
+    def write(start):
         for k in range(parts):
             q = origin_of(B_SWAP, me, k, parts)
             for s in range(per):
-                at = pl.ds(start * groups + q * per + s, count, stride=groups)
-                buffer[at, :] = chunks[k][s * padded + start : s * padded + start + count, :]
+                at = pl.ds(start * groups + q * per + s, SUB, stride=groups)
+                buffer[at, :] = chunks[k][s * padded + start : s * padded + start + SUB, :]
 
     flat_tiles(modes, groups, write, out_hbm, buffer, sems)
 
@@ -426,14 +430,14 @@
     me = lax.axis_index("modes")
     groups = parts * per
 
-    def write(start, count):
+    def write(start):
         for k in range(parts):
             q = origin_of(H_SWAP, me, k, parts)
             for s in range(per):
                 at = pl.multiple_of((q * per + s) * padded + start, SUB)
                 within = s * padded + start
                 rows = base[pl.ds(at, SUB), :] + 0.1 * chunks[k][within : within + SUB, :]
-                buffer[pl.ds(start * groups + q * per + s, count, stride=groups), :] = rows[:count]
+                buffer[pl.ds(start * groups + q * per + s, SUB, stride=groups), :] = rows
 
     flat_tiles(modes, groups, write, out_hbm, buffer, sems)
 
@@ -496,7 +500,7 @@
     padded = -(-modes // SUB) * SUB
     halves = 1
     rows = parts * padded
-    assert planes == 1 and groups * LANES == columns and per * parts == groups
+    assert modes > SUB and planes == 1 and groups * LANES == columns and per * parts == groups
     assert polynomial_exponent_rows.shape[1] <= TILE16 and points % LANES == 0
     assert rows % TILE16 == 0 and 2 * NZ * padded <= SUB * LANES and 3 * nreg <= LANES
 
@@ -512,7 +516,7 @@
     rimmed = struct(per * padded + SUB, LANES)
     grouped = pltpu.VMEM((groups * padded, LANES), F32)
 
-    fields = pltpu.VMEM((modes * groups, LANES), F32)
+    fields = pltpu.VMEM((padded * groups, LANES), F32)
     v_near, v_far = halo(v)
     source = call(
         functools.partial(source_kernel, parts, modes, padded),

time: 60 us -> 60 us (level)
  no operation moved by 1% of the time
where the time goes in v6:
time: 60 us; the launch traced here: 59.8 us
  starting transfers between devices  26.8 us (45%)
  waiting for transfers between devices  17.7 us (30%)
  Pallas kernels  13.8 us (23%)
  between operations  0.84 us (1%)
  local copies, waits for them, and re-layouts  0.71 us (1%)
    ppermute x12, starting transfers between devices, exchange(): received[k] = lax.ppermute(chunks[k], 'modes', pairs)  15.7 us
    pallas_call x10, Pallas kernels, call(): pl.pallas_call(kernel, out_shape=out_shape, in_specs=specs, out_specs=[wh...  13.8 us
    ppermute x12, waiting for transfers between devices, exchange(): received[k] = lax.ppermute(chunks[k], 'modes', pairs)  13.3 us
    ppermute x3, starting transfers between devices, halo(): far = lax.ppermute(x, 'space', far)  9.88 us
    ppermute x3, waiting for transfers between devices, halo(): far = lax.ppermute(x, 'space', far)  4.31 us
    ppermute x3, starting transfers between devices, halo(): return (lax.ppermute(x, 'space', near), far)  1.27 us
  transfers between devices with their start and end apart: 18, of which 7 were waited for; matrix products, arithmetic and copies ran while one was open for 0% of the time, Pallas kernels for 22%

profile of v6, /device:TPU:11, one launch (start us, length us, event | category | flops | bytes accessed | tf_op | source)
XLA Modules:
  0.0 59.8 jit_solution(11358395614694157439)
XLA Ops:
  1.4 3.0 %collective-permute-start.1 = (f32[880,128]{1,0:T(8,128)}, f32[880,128]{1,0:T(8,128)S(1)}, u32[]{:S(2)}, u32[]{:S(2)}) collective-permute-start(f32[880,128]{1,0:T(8,128)} %bitcast.11), channel_id=1, source_target_pairs={{4,8},{8,4},{12,16},{16,12},{20,24},{24,20},{5,9},{9,5},{13,17},{1... | collective-permute-start | bytes 1351688 | tf_op jit(solution)/shard_map/ppermute | solution.py:479
  4.4 2.4 %shard_map.106 = (f32[232,128]{1,0:T(8,128)}, f32[232,128]{1,0:T(8,128)}, f32[232,128]{1,0:T(8,128)}, f32[232,128]{1,0:T(8,128)}) custom-call(f32[880,128]{1,0:T(8,128)} %bitcast.12, f32[880,128]{1,0:T(8,128)} %bitcast.23, f32[16,128]{1,0:T(8,128)} %bitcast.17), custom_call_target="tpu_custom_call" | custom-call | bytes 909312 | tf_op jit(solution)/shard_map/pallas_call | solution.py:455
  6.9 1.3 %collective-permute-start.3 = (f32[232,128]{1,0:T(8,128)}, f32[232,128]{1,0:T(8,128)S(1)}, u32[]{:S(2)}, u32[]{:S(2)}) collective-permute-start(f32[232,128]{1,0:T(8,128)} %get-tuple-element.40), channel_id=1, source_target_pairs={{0,1},{1,2},{2,3},{3,0},{4,5},{5,6},{6,7},{7,4},{8,9},{9,10},{10,1... | collective-permute-start | bytes 356360 | tf_op jit(solution)/shard_map/ppermute | solution.py:471
  8.2 1.1 %collective-permute-start.4 = (f32[232,128]{1,0:T(8,128)}, f32[232,128]{1,0:T(8,128)S(1)}, u32[]{:S(2)}, u32[]{:S(2)}) collective-permute-start(f32[232,128]{1,0:T(8,128)} %get-tuple-element.42), channel_id=1, source_target_pairs={{0,2},{1,3},{2,0},{3,1},{4,6},{5,7},{6,4},{7,5},{8,10},{9,11},{10,... | collective-permute-start | bytes 356360 | tf_op jit(solution)/shard_map/ppermute | solution.py:471
  9.3 1.4 %collective-permute-start.5 = (f32[232,128]{1,0:T(8,128)}, f32[232,128]{1,0:T(8,128)S(1)}, u32[]{:S(2)}, u32[]{:S(2)}) collective-permute-start(f32[232,128]{1,0:T(8,128)} %get-tuple-element.43), channel_id=1, source_target_pairs={{0,3},{1,0},{2,1},{3,2},{4,7},{5,4},{6,5},{7,6},{8,11},{9,8},{10,9... | collective-permute-start | bytes 356360 | tf_op jit(solution)/shard_map/ppermute | solution.py:471
  11.4 3.9 %shard_map.104 = (bf16[4,224,224]{2,1,0:T(8,128)(2,1)S(1)}, bf16[4,224,224]{2,1,0:T(8,128)(2,1)S(1)}, bf16[512,224]{1,0:T(8,128)(2,1)S(1)}, bf16[512,224]{1,0:T(...) custom-call(s32[9,220]{1,0:T(8,128)S(1)} %bitcast.20, ...), custom_call_target="tpu_custom_call" | custom-call | bytes 36736 | tf_op jit(solution)/shard_map/pallas_call | solution.py:455
  15.3 1.1 %collective-permute-done.1.far_ref = f32[880,128]{1,0:T(8,128)S(1)} collective-permute-done((f32[880,128]{1,0:T(8,128)}, f32[880,128]{1,0:T(8,128)S(1)}, u32[]{:S(2)}, u32[]{:S(2)}) %collective-permute-start.1) | collective-permute-done | bytes 450592 | tf_op jit(solution)/shard_map/ppermute | solution.py:479
  16.4 0.9 %shard_map.105 = (f32[232,128]{1,0:T(8,128)S(1)}, f32[232,128]{1,0:T(8,128)S(1)}, f32[232,128]{1,0:T(8,128)S(1)}, f32[232,128]{1,0:T(8,128)S(1)}) custom-call(f32[880,128]{1,0:T(8,128)S(1)} %bitcast.13, f32[880,128]{1,0:T(8,128)S(1)} %collective-permute-done.near_ref, f32[880,128]{1,0:T(8,128)S(1)} %collective-permute-done.1.far_ref), custom_call_target="tpu_custom_call" | custom-call | bytes 1351680 | tf_op jit(solution)/shard_map/pallas_call | solution.py:455
  17.8 2.2 %collective-permute-start.7 = (f32[232,128]{1,0:T(8,128)S(1)}, f32[232,128]{1,0:T(8,128)S(1)}, u32[]{:S(2)}, u32[]{:S(2)}) collective-permute-start(f32[232,128]{1,0:T(8,128)S(1)} %get-tuple-element.46), channel_id=1, source_target_pairs={{0,2},{1,3},{2,0},{3,1},{4,6},{5,7},{6,4},{7,5},{8,10},{9,11},{10,... | collective-permute-start | bytes 356360 | tf_op jit(solution)/shard_map/ppermute | solution.py:471
  20.3 4.0 %collective-permute-start.10 = (f32[880,128]{1,0:T(8,128)S(1)}, f32[880,128]{1,0:T(8,128)S(1)}, u32[]{:S(2)}, u32[]{:S(2)}) collective-permute-start(f32[880,128]{1,0:T(8,128)S(1)} %bitcast.14), channel_id=1, source_target_pairs={{4,8},{8,4},{12,16},{16,12},{20,24},{24,20},{5,9},{9,5},{13,17},{1... | collective-permute-start | bytes 1351688 | tf_op jit(solution)/shard_map/ppermute | solution.py:479
  24.4 3.6 %collective-permute-done.7.refs_6_ = f32[232,128]{1,0:T(8,128)S(1)} collective-permute-done((f32[232,128]{1,0:T(8,128)S(1)}, f32[232,128]{1,0:T(8,128)S(1)}, u32[]{:S(2)}, u32[]{:S(2)}) %collective-permute-start.7) | collective-permute-done | bytes 118816 | tf_op jit(solution)/shard_map/ppermute | solution.py:471
  28.0 1.0 %shard_map.107.refs_1_ = f32[224,640]{1,0:T(8,128)S(1)} custom-call(f32[232,128]{1,0:T(8,128)S(1)} %copy-done.2, f32[232,128]{1,0:T(8,128)S(1)} %collective-permute-done.3.refs_1_, f32[232,128]{1,0:T(8,128)S(1)} %collective-permute-done.4.refs_2_, f32[232,128]{1,0:T(8,128)S(1)} %collective-permute-done.5.refs_3_, f32[232,128]{1,0:T(8,128)S(1)} %get-tuple-element.44.refs_4_, ...), custom_call_target="tpu_custom_call" | custom-call | bytes 1636864 | tf_op jit(solution)/shard_map/pallas_call | solution.py:455
  29.1 2.2 %collective-permute-done.2.refs_0_ = f32[232,128]{1,0:T(8,128)S(1)} collective-permute-done((f32[232,128]{1,0:T(8,128)S(1)}, f32[232,128]{1,0:T(8,128)S(1)}, u32[]{:S(2)}, u32[]{:S(2)}) %collective-permute-start.2) | collective-permute-done | bytes 118816 | tf_op jit(solution)/shard_map/ppermute | solution.py:471
  32.2 2.8 %collective-permute-start.14 = (f32[224,512]{1,0:T(8,128)S(1)}, f32[224,512]{1,0:T(8,128)S(1)}, u32[]{:S(2)}, u32[]{:S(2)}) collective-permute-start(f32[224,512]{1,0:T(8,128)S(1)} %get-tuple-element.56.refs_0_), channel_id=1, source_target_pairs={{4,8},{8,4},{12,16},{16,12},{20,24},{24,20},{5,9},{9,5},{13,17},{1... | collective-permute-start | bytes 1376264 | tf_op jit(solution)/shard_map/ppermute | solution.py:479
  35.8 3.9 %collective-permute-start.11 = (f32[224,128]{1,0:T(8,128)S(1)}, f32[224,128]{1,0:T(8,128)S(1)}, u32[]{:S(2)}, u32[]{:S(2)}) collective-permute-start(f32[224,128]{1,0:T(8,128)S(1)} %get-tuple-element.54), channel_id=1, source_target_pairs={{0,2},{1,3},{2,0},{3,1},{4,6},{5,7},{6,4},{7,5},{8,10},{9,11},{10,... | collective-permute-start | bytes 344072 | tf_op jit(solution)/shard_map/ppermute | solution.py:471
  39.7 1.5 %collective-permute-start.8 = (f32[224,128]{1,0:T(8,128)S(1)}, f32[224,128]{1,0:T(8,128)S(1)}, u32[]{:S(2)}, u32[]{:S(2)}) collective-permute-start(f32[224,128]{1,0:T(8,128)S(1)} %get-tuple-element.51), channel_id=1, source_target_pairs={{0,1},{1,2},{2,3},{3,0},{4,5},{5,6},{6,7},{7,4},{8,9},{9,10},{10,1... | collective-permute-start | bytes 344072 | tf_op jit(solution)/shard_map/ppermute | solution.py:471
  41.2 1.5 %shard_map.111 = (f32[512,512]{1,0:T(8,128)S(1)}, f32[512,512]{1,0:T(8,128)S(1)}) custom-call(f32[224,512]{1,0:T(8,128)S(1)} %get-tuple-element.56.refs_0_, f32[224,128]{1,0:T(8,128)S(1)} %get-tuple-element.57.refs_1_, s32[1,640]{1,0:T(1,128)S(1)} %get-tuple-element.49.refs_9_.refs_4_.refs_2_, bf16[512,224]{1,0:T(8,128)(2,1)S(1)} %get-tuple-element.58.refs_3_.bh_ref, ...), custom_call_target="tpu_custom_call" | custom-call | bytes 1165824 | tf_op jit(solution)/shard_map/pallas_call | solution.py:455
  42.7 3.2 %collective-permute-done.14.far_ref = f32[224,512]{1,0:T(8,128)S(1)} collective-permute-done((f32[224,512]{1,0:T(8,128)S(1)}, f32[224,512]{1,0:T(8,128)S(1)}, u32[]{:S(2)}, u32[]{:S(2)}) %collective-permute-start.14) | collective-permute-done | bytes 458784 | tf_op jit(solution)/shard_map/ppermute | solution.py:479
  45.9 1.2 %shard_map.112 = (f32[224,128]{1,0:T(8,128)S(1)}, f32[224,128]{1,0:T(8,128)S(1)}, f32[224,128]{1,0:T(8,128)S(1)}, f32[224,128]{1,0:T(8,128)S(1)}) custom-call(f32[224,512]{1,0:T(8,128)S(1)} %collective-permute-done.13.near_ref, f32[224,512]{1,0:T(8,128)S(1)} %collective-permute-done.14.far_ref, f32[512,512]{1,0:T(8,128)S(1)} %get-tuple-element.61.part_ref, ...), custom_call_target="tpu_custom_call" | custom-call | bytes 3940352 | tf_op jit(solution)/shard_map/pallas_call | solution.py:455
  47.7 2.4 %collective-permute-start.16 = (f32[224,128]{1,0:T(8,128)S(1)}, f32[224,128]{1,0:T(8,128)S(1)}, u32[]{:S(2)}, u32[]{:S(2)}) collective-permute-start(f32[224,128]{1,0:T(8,128)S(1)} %get-tuple-element.67), channel_id=1, source_target_pairs={{0,2},{1,3},{2,0},{3,1},{4,6},{5,7},{6,4},{7,5},{8,10},{9,11},{10,... | collective-permute-start | bytes 344072 | tf_op jit(solution)/shard_map/ppermute | solution.py:471
  50.6 0.8 %shard_map.110 = f32[880,128]{1,0:T(8,128)} custom-call(f32[224,128]{1,0:T(8,128)S(1)} %get-tuple-element.50.refs_0_, f32[224,128]{1,0:T(8,128)S(1)} %collective-permute-done.8.refs_1_, f32[224,128]{1,0:T(8,128)S(1)} %collective-permute-done.11.refs_2_, f32[224,128]{1,0:T(8,128)S(1)} %collective-permute-done.12.refs_3_), custom_call_target="tpu_custom_call" | custom-call | bytes 458752 | tf_op jit(solution)/shard_map/pallas_call | solution.py:455
  52.0 4.8 %collective-permute-done.16.refs_2_ = f32[224,128]{1,0:T(8,128)S(1)} collective-permute-done((f32[224,128]{1,0:T(8,128)S(1)}, f32[224,128]{1,0:T(8,128)S(1)}, u32[]{:S(2)}, u32[]{:S(2)}) %collective-permute-start.16) | collective-permute-done | bytes 114720 | tf_op jit(solution)/shard_map/ppermute | solution.py:471
  56.8 2.2 %collective-permute-done.17.refs_3_ = f32[224,128]{1,0:T(8,128)S(1)} collective-permute-done((f32[224,128]{1,0:T(8,128)S(1)}, f32[224,128]{1,0:T(8,128)S(1)}, u32[]{:S(2)}, u32[]{:S(2)}) %collective-permute-start.17) | collective-permute-done | bytes 114720 | tf_op jit(solution)/shard_map/ppermute | solution.py:471
  58.9 0.8 %shard_map.113 = f32[880,128]{1,0:T(8,128)} custom-call(f32[224,128]{1,0:T(8,128)S(1)} %get-tuple-element.65.refs_0_, f32[224,128]{1,0:T(8,128)S(1)} %collective-permute-done.15.refs_1_, f32[224,128]{1,0:T(8,128)S(1)} %collective-permute-done.16.refs_2_, f32[224,128]{1,0:T(8,128)S(1)} %collective-permute-done.17.refs_3_, f32[896,128]{1,0:T(8,128)S(1)} %shard_map.109.refs_4_), custom_call_target="tpu_custom_call" | custom-call | bytes 917504 | tf_op jit(solution)/shard_map/pallas_call | solution.py:455
  (40 shorter events, 5.7 us)
Async XLA Ops:
  0.6 14.7 %collective-permute-start = (f32[880,128]{1,0:T(8,128)}, f32[880,128]{1,0:T(8,128)S(1)}, u32[]{:S(2)}, u32[]{:S(2)}) collective-permute-start(f32[880,128]{1,0:T(8,128)} %bitcast.10), channel_id=1, source_target_pairs={{0,4},{4,0},{8,12},{12,8},{16,20},{20,16},{24,28},{28,24},{1,5},{5... | collective-permute-start | bytes 1351688 | tf_op jit(solution)/shard_map/ppermute | solution.py:480
  1.4 15.0 %collective-permute-start.1 = (f32[880,128]{1,0:T(8,128)}, f32[880,128]{1,0:T(8,128)S(1)}, u32[]{:S(2)}, u32[]{:S(2)}) collective-permute-start(f32[880,128]{1,0:T(8,128)} %bitcast.11), channel_id=1, source_target_pairs={{4,8},{8,4},{12,16},{16,12},{20,24},{24,20},{5,9},{9,5},{13,17},{1... | collective-permute-start | bytes 1351688 | tf_op jit(solution)/shard_map/ppermute | solution.py:479
  4.4 6.3 %copy-start.4 = (s32[512,9]{0,1:T(8,128)S(1)}, s32[512,9]{0,1:T(8,128)}, u32[]{:S(2)}) copy-start(s32[512,9]{0,1:T(8,128)} %param.16) | copy-start | bytes 55300
  4.4 6.3 %copy-start.5 = (s32[220,9]{0,1:T(8,128)S(1)}, s32[220,9]{0,1:T(8,128)}, u32[]{:S(2)}) copy-start(s32[220,9]{0,1:T(8,128)} %param.15) | copy-start | bytes 23764
  4.4 12.0 %copy-start = (f32[55,1,2048]{2,1,0:T(1,128)S(1)}, f32[55,1,2048]{2,1,0:T(1,128)}, u32[]{:S(2)}) copy-start(f32[55,1,2048]{2,1,0:T(1,128)} %param.9) | copy-start | bytes 1351684
  6.9 13.2 %collective-permute-start.3 = (f32[232,128]{1,0:T(8,128)}, f32[232,128]{1,0:T(8,128)S(1)}, u32[]{:S(2)}, u32[]{:S(2)}) collective-permute-start(f32[232,128]{1,0:T(8,128)} %get-tuple-element.40), channel_id=1, source_target_pairs={{0,1},{1,2},{2,3},{3,0},{4,5},{5,6},{6,7},{7,4},{8,9},{9,10},{10,1... | collective-permute-start | bytes 356360 | tf_op jit(solution)/shard_map/ppermute | solution.py:471
  8.2 12.0 %collective-permute-start.4 = (f32[232,128]{1,0:T(8,128)}, f32[232,128]{1,0:T(8,128)S(1)}, u32[]{:S(2)}, u32[]{:S(2)}) collective-permute-start(f32[232,128]{1,0:T(8,128)} %get-tuple-element.42), channel_id=1, source_target_pairs={{0,2},{1,3},{2,0},{3,1},{4,6},{5,7},{6,4},{7,5},{8,10},{9,11},{10,... | collective-permute-start | bytes 356360 | tf_op jit(solution)/shard_map/ppermute | solution.py:471
  9.3 15.0 %collective-permute-start.5 = (f32[232,128]{1,0:T(8,128)}, f32[232,128]{1,0:T(8,128)S(1)}, u32[]{:S(2)}, u32[]{:S(2)}) collective-permute-start(f32[232,128]{1,0:T(8,128)} %get-tuple-element.43), channel_id=1, source_target_pairs={{0,3},{1,0},{2,1},{3,2},{4,7},{5,4},{6,5},{7,6},{8,11},{9,8},{10,9... | collective-permute-start | bytes 356360 | tf_op jit(solution)/shard_map/ppermute | solution.py:471
  15.3 5.0 %copy-start.1 = (f32[55,1,2048]{2,1,0:T(1,128)S(1)}, f32[55,1,2048]{2,1,0:T(1,128)}, u32[]{:S(2)}) copy-start(f32[55,1,2048]{2,1,0:T(1,128)} %param.11) | copy-start | bytes 1351684
  15.3 12.7 %copy-start.2 = (f32[232,128]{1,0:T(8,128)S(1)}, f32[232,128]{1,0:T(8,128)}, u32[]{:S(2)}) copy-start(f32[232,128]{1,0:T(8,128)} %get-tuple-element.39.refs_0_) | copy-start | bytes 356356
  17.3 7.1 %collective-permute-start.6 = (f32[232,128]{1,0:T(8,128)S(1)}, f32[232,128]{1,0:T(8,128)S(1)}, u32[]{:S(2)}, u32[]{:S(2)}) collective-permute-start(f32[232,128]{1,0:T(8,128)S(1)} %get-tuple-element.45), channel_id=1, source_target_pairs={{0,1},{1,0},{2,3},{3,2},{4,5},{5,4},{6,7},{7,6},{8,9},{9,8},{10,11... | collective-permute-start | bytes 356360 | tf_op jit(solution)/shard_map/ppermute | solution.py:471
  17.8 10.2 %collective-permute-start.7 = (f32[232,128]{1,0:T(8,128)S(1)}, f32[232,128]{1,0:T(8,128)S(1)}, u32[]{:S(2)}, u32[]{:S(2)}) collective-permute-start(f32[232,128]{1,0:T(8,128)S(1)} %get-tuple-element.46), channel_id=1, source_target_pairs={{0,2},{1,3},{2,0},{3,1},{4,6},{5,7},{6,4},{7,5},{8,10},{9,11},{10,... | collective-permute-start | bytes 356360 | tf_op jit(solution)/shard_map/ppermute | solution.py:471
  20.0 11.2 %collective-permute-start.2 = (f32[232,128]{1,0:T(8,128)S(1)}, f32[232,128]{1,0:T(8,128)S(1)}, u32[]{:S(2)}, u32[]{:S(2)}) collective-permute-start(f32[232,128]{1,0:T(8,128)S(1)} %get-tuple-element.38), channel_id=1, source_target_pairs={{0,3},{1,2},{2,1},{3,0},{4,7},{5,6},{6,5},{7,4},{8,11},{9,10},{10,... | collective-permute-start | bytes 356360 | tf_op jit(solution)/shard_map/ppermute | solution.py:471
  20.3 14.8 %collective-permute-start.10 = (f32[880,128]{1,0:T(8,128)S(1)}, f32[880,128]{1,0:T(8,128)S(1)}, u32[]{:S(2)}, u32[]{:S(2)}) collective-permute-start(f32[880,128]{1,0:T(8,128)S(1)} %bitcast.14), channel_id=1, source_target_pairs={{4,8},{8,4},{12,16},{16,12},{20,24},{24,20},{5,9},{9,5},{13,17},{1... | collective-permute-start | bytes 1351688 | tf_op jit(solution)/shard_map/ppermute | solution.py:479
  24.3 10.8 %collective-permute-start.9 = (f32[880,128]{1,0:T(8,128)S(1)}, f32[880,128]{1,0:T(8,128)S(1)}, u32[]{:S(2)}, u32[]{:S(2)}) collective-permute-start(f32[880,128]{1,0:T(8,128)S(1)} %bitcast.15), channel_id=1, source_target_pairs={{0,4},{4,0},{8,12},{12,8},{16,20},{20,16},{24,28},{28,24},{1,5},{5... | collective-permute-start | bytes 1351688 | tf_op jit(solution)/shard_map/ppermute | solution.py:480
  31.8 10.9 %collective-permute-start.13 = (f32[224,512]{1,0:T(8,128)S(1)}, f32[224,512]{1,0:T(8,128)S(1)}, u32[]{:S(2)}, u32[]{:S(2)}) collective-permute-start(f32[224,512]{1,0:T(8,128)S(1)} %get-tuple-element.56.refs_0_), channel_id=1, source_target_pairs={{0,4},{4,0},{8,12},{12,8},{16,20},{20,16},{24,28},{28,24},{1,5},{5... | collective-permute-start | bytes 1376264 | tf_op jit(solution)/shard_map/ppermute | solution.py:480
  32.2 13.7 %collective-permute-start.14 = (f32[224,512]{1,0:T(8,128)S(1)}, f32[224,512]{1,0:T(8,128)S(1)}, u32[]{:S(2)}, u32[]{:S(2)}) collective-permute-start(f32[224,512]{1,0:T(8,128)S(1)} %get-tuple-element.56.refs_0_), channel_id=1, source_target_pairs={{4,8},{8,4},{12,16},{16,12},{20,24},{24,20},{5,9},{9,5},{13,17},{1... | collective-permute-start | bytes 1376264 | tf_op jit(solution)/shard_map/ppermute | solution.py:479
  35.8 14.2 %collective-permute-start.11 = (f32[224,128]{1,0:T(8,128)S(1)}, f32[224,128]{1,0:T(8,128)S(1)}, u32[]{:S(2)}, u32[]{:S(2)}) collective-permute-start(f32[224,128]{1,0:T(8,128)S(1)} %get-tuple-element.54), channel_id=1, source_target_pairs={{0,2},{1,3},{2,0},{3,1},{4,6},{5,7},{6,4},{7,5},{8,10},{9,11},{10,... | collective-permute-start | bytes 344072 | tf_op jit(solution)/shard_map/ppermute | solution.py:471
  39.7 10.8 %collective-permute-start.12 = (f32[224,128]{1,0:T(8,128)S(1)}, f32[224,128]{1,0:T(8,128)S(1)}, u32[]{:S(2)}, u32[]{:S(2)}) collective-permute-start(f32[224,128]{1,0:T(8,128)S(1)} %get-tuple-element.55), channel_id=1, source_target_pairs={{0,3},{1,0},{2,1},{3,2},{4,7},{5,4},{6,5},{7,6},{8,11},{9,8},{10,9... | collective-permute-start | bytes 344072 | tf_op jit(solution)/shard_map/ppermute | solution.py:471
  39.7 10.8 %collective-permute-start.8 = (f32[224,128]{1,0:T(8,128)S(1)}, f32[224,128]{1,0:T(8,128)S(1)}, u32[]{:S(2)}, u32[]{:S(2)}) collective-permute-start(f32[224,128]{1,0:T(8,128)S(1)} %get-tuple-element.51), channel_id=1, source_target_pairs={{0,1},{1,2},{2,3},{3,0},{4,5},{5,6},{6,7},{7,4},{8,9},{9,10},{10,1... | collective-permute-start | bytes 344072 | tf_op jit(solution)/shard_map/ppermute | solution.py:471
  41.2 4.7 %copy-start.3 = (f32[1,2048]{1,0:T(1,128)S(1)}, f32[1,2048]{1,0:T(1,128)}, u32[]{:S(2)}) copy-start(f32[1,2048]{1,0:T(1,128)} %param.12) | copy-start | bytes 24580
  47.1 4.9 %collective-permute-start.15 = (f32[224,128]{1,0:T(8,128)S(1)}, f32[224,128]{1,0:T(8,128)S(1)}, u32[]{:S(2)}, u32[]{:S(2)}) collective-permute-start(f32[224,128]{1,0:T(8,128)S(1)} %get-tuple-element.66), channel_id=1, source_target_pairs={{0,1},{1,2},{2,3},{3,0},{4,5},{5,6},{6,7},{7,4},{8,9},{9,10},{10,1... | collective-permute-start | bytes 344072 | tf_op jit(solution)/shard_map/ppermute | solution.py:471
  47.7 9.1 %collective-permute-start.16 = (f32[224,128]{1,0:T(8,128)S(1)}, f32[224,128]{1,0:T(8,128)S(1)}, u32[]{:S(2)}, u32[]{:S(2)}) collective-permute-start(f32[224,128]{1,0:T(8,128)S(1)} %get-tuple-element.67), channel_id=1, source_target_pairs={{0,2},{1,3},{2,0},{3,1},{4,6},{5,7},{6,4},{7,5},{8,10},{9,11},{10,... | collective-permute-start | bytes 344072 | tf_op jit(solution)/shard_map/ppermute | solution.py:471
  50.0 8.9 %collective-permute-start.17 = (f32[224,128]{1,0:T(8,128)S(1)}, f32[224,128]{1,0:T(8,128)S(1)}, u32[]{:S(2)}, u32[]{:S(2)}) collective-permute-start(f32[224,128]{1,0:T(8,128)S(1)} %get-tuple-element.68), channel_id=1, source_target_pairs={{0,3},{1,0},{2,1},{3,2},{4,7},{5,4},{6,5},{7,6},{8,11},{9,8},{10,9... | collective-permute-start | bytes 344072 | tf_op jit(solution)/shard_map/ppermute | solution.py:471
  (3 other events, 5.2 us)

commit v7 on v6

--- a/solution.py
+++ b/solution.py
@@ -46,16 +46,20 @@
     return lax.broadcasted_iota(jnp.int32, shape, len(shape) - 1)
 
 
-def target_of(swap, me, k, parts):
+def target_of(route, me, k, parts):
+    swap, order = route
+    step = order(k, parts) if k else 0
     if swap and parts & (parts - 1) == 0:
-        return me ^ (swap(k, parts) if k else 0)
-    return (me + k) % parts if isinstance(me, int) else lax.rem(me + k, parts)
-
-
-def origin_of(swap, me, k, parts):
+        return me ^ step
+    return (me + step) % parts if isinstance(me, int) else lax.rem(me + step, parts)
+
+
+def origin_of(route, me, k, parts):
+    swap, order = route
+    step = order(k, parts) if k else 0
     if swap and parts & (parts - 1) == 0:
-        return me ^ (swap(k, parts) if k else 0)
-    return lax.rem(me + (parts - k), parts)
+        return me ^ step
+    return lax.rem(me + (parts - step), parts)
 
 
 def upward(k, parts):
@@ -66,7 +70,16 @@
     return parts - k
 
 
-W_SWAP, R_SWAP, B_SWAP, H_SWAP = None, upward, None, None
+def turned(k, parts):
+    return 1 + k % (parts - 1)
+
+
+W_ROUTE, R_ROUTE, B_ROUTE, H_ROUTE = (
+    (True, downward),
+    (True, upward),
+    (False, upward),
+    (False, turned),
+)
 
 
 def load_group(ref, group, modes, groups):
@@ -80,12 +93,12 @@
     return jnp.concatenate([ref[pl.ds(group, main, stride=groups), :], last], axis=0)
 
 
-def emit_slots(swap, me, parts, grouped, outs, padded):
+def emit_slots(route, me, parts, grouped, outs, padded):
     groups = grouped.shape[0] // padded
     per = groups // parts
     lane = lane_ids((padded, LANES))
     for k, out in enumerate(outs):
-        q = target_of(swap, me, k, parts)
+        q = target_of(route, me, k, parts)
         start = pl.multiple_of(q * (per * padded), SUB)
         out[: per * padded, :] = grouped[pl.ds(start, per * padded), :]
         before = pl.multiple_of(jnp.maximum(q * per - 1, 0) * padded, SUB)
@@ -125,7 +138,7 @@
             if count < SUB:
                 w = jnp.where(row < count, w, 0.0)
             grouped[g * padded + start : g * padded + start + SUB, :] = w
-    emit_slots(W_SWAP, me, parts, grouped, outs, padded)
+    emit_slots(W_ROUTE, me, parts, grouped, outs, padded)
 
 
 def stencil_groups(x_ref, near_ref, far_ref, modes, groups, padded, emit):
@@ -153,7 +166,7 @@
         grouped[g * padded : (g + 1) * padded, :] = total
 
     stencil_groups(v_ref, near_ref, far_ref, modes, groups, padded, emit)
-    emit_slots(R_SWAP, me, parts, grouped, outs, padded)
+    emit_slots(R_ROUTE, me, parts, grouped, outs, padded)
 
 
 def thermal_kernel(modes, padded, groups, t_ref, near_ref, far_ref, out_ref):
@@ -311,11 +324,11 @@
     zones = zones_ref[...]
     applied = None
     for k in range(count):
-        source = origin_of(R_SWAP, me, k, parts)
+        source = origin_of(R_ROUTE, me, k, parts)
         part = coupled(r_refs[k], source, ah_ref, al_ref, zones, nreg, padded, per)
         applied = part if applied is None else applied + part
     for k in range(parts):
-        at = pl.multiple_of(origin_of(W_SWAP, me, k, parts) * padded, SUB)
+        at = pl.multiple_of(origin_of(W_ROUTE, me, k, parts) * padded, SUB)
         out_ref[pl.ds(at, padded), :] = unpack(w_refs[k], padded, per)
     out_ref[...] = out_ref[...] - (0.8 / 6.0) * applied
 
@@ -328,7 +341,7 @@
     zones = zones_ref[...]
     applied = None
     for k in range(count, parts):
-        source = origin_of(R_SWAP, me, k, parts)
+        source = origin_of(R_ROUTE, me, k, parts)
         part = coupled(r_refs[k - count], source, ah_ref, al_ref, zones, nreg, padded, per)
         applied = part if applied is None else applied + part
     relaxed = most_ref[...] - (0.8 / 6.0) * applied
@@ -336,7 +349,7 @@
     rim_ref[...] = relaxed[:, width:]
     all_ref[...] = relaxed[:, :width]
     for k, out in enumerate(outs):
-        at = pl.multiple_of(target_of(B_SWAP, me, k, parts) * padded, SUB)
+        at = pl.multiple_of(target_of(B_ROUTE, me, k, parts) * padded, SUB)
         for s in range(per):
             out[s * padded : (s + 1) * padded, :] = all_ref[
                 pl.ds(at, padded), s * LANES : (s + 1) * LANES
@@ -389,7 +402,7 @@
             heat[:, s * LANES : (s + 1) * LANES] * a_ref[pl.ds(me * per + half * own + s, 1), :]
         )
     for k, out in enumerate(outs):
-        target = target_of(H_SWAP, me, k, parts)
+        target = target_of(H_ROUTE, me, k, parts)
         at = pl.multiple_of(target * padded, SUB)
         for s in range(own):
             out[s * padded : (s + 1) * padded, :] = heat_ref[
@@ -417,7 +430,7 @@
 
     def write(start):
         for k in range(parts):
-            q = origin_of(B_SWAP, me, k, parts)
+            q = origin_of(B_ROUTE, me, k, parts)
             for s in range(per):
                 at = pl.ds(start * groups + q * per + s, SUB, stride=groups)
                 buffer[at, :] = chunks[k][s * padded + start : s * padded + start + SUB, :]
@@ -432,7 +445,7 @@
 
     def write(start):
         for k in range(parts):
-            q = origin_of(H_SWAP, me, k, parts)
+            q = origin_of(H_ROUTE, me, k, parts)
             for s in range(per):
                 at = pl.multiple_of((q * per + s) * padded + start, SUB)
                 within = s * padded + start
@@ -463,11 +476,11 @@
     )(*args)
 
 
-def exchange(chunks, swap):
+def exchange(chunks, route):
     parts = lax.axis_size("modes")
     received = list(chunks)
     for k in range(1, parts):
-        pairs = [(i, target_of(swap, i, k, parts)) for i in range(parts)]
+        pairs = [(i, target_of(route, i, k, parts)) for i in range(parts)]
         received[k] = lax.ppermute(chunks[k], "modes", pairs)
     return received
 
@@ -526,7 +539,7 @@
         hbm=(0, 1, 2),
         limit=62 * 1024 * 1024,
     )
-    source = exchange(source, W_SWAP)
+    source = exchange(source, W_ROUTE)
     temp, source[1] = lax.optimization_barrier((temp, source[1]))
     a_high, a_low, b_high, b_low, w_high, w_low, lift, zones = call(
         functools.partial(tables_kernel, parts, modes, padded),
@@ -555,7 +568,7 @@
         functools.partial(rough_kernel, parts, modes, padded, groups),
         [rimmed] * parts, [v, v_near, v_far], [grouped],
     )
-    rough = exchange(rough, R_SWAP)
+    rough = exchange(rough, R_ROUTE)
     t_near, t_far = halo(temp)
     base = call(
         functools.partial(thermal_kernel, modes, padded, groups),
@@ -577,7 +590,7 @@
     relaxed = [relaxed]
     beside = [halo(x) for x in relaxed]
     base, back[2] = lax.optimization_barrier((base, back[2]))
-    back = exchange(back, B_SWAP)
+    back = exchange(back, B_ROUTE)
     part, spread = call(
         functools.partial(plane_kernel, nreg, halves),
         [struct(points, per * LANES)] * 2,
@@ -591,7 +604,7 @@
             [*beside[half], part, spread, avg, b_high, b_low, w_high, w_low],
             [pltpu.VMEM((rows, per * LANES // halves), F32)],
         )
-        heat += exchange(pieces, H_SWAP)
+        heat += exchange(pieces, H_ROUTE)
     tiled = [fields, pltpu.SemaphoreType.DMA((padded // SUB,))]
     relaxed_voltage = call(
         functools.partial(gather_kernel, parts, modes, padded, per),

time: 60 us -> 58.9 us (0.982)
  waiting for transfers between devices: 17.7 us -> 16.3 us
    ppermute x12, waiting for transfers between devices: 13.3 us -> 11.6 us  [exchange(): received[k] = lax.ppermute(chunks[k], 'modes', pairs)]
where the time goes in v7:
time: 58.9 us; the launch traced here: 58.6 us
  starting transfers between devices  27 us (46%)
  waiting for transfers between devices  16.3 us (28%)
  Pallas kernels  13.8 us (23%)
  between operations  0.83 us (1%)
  local copies, waits for them, and re-layouts  0.71 us (1%)
    ppermute x12, starting transfers between devices, exchange(): received[k] = lax.ppermute(chunks[k], 'modes', pairs)  16 us
    pallas_call x10, Pallas kernels, call(): pl.pallas_call(kernel, out_shape=out_shape, in_specs=specs, out_specs=[wh...  13.8 us
    ppermute x12, waiting for transfers between devices, exchange(): received[k] = lax.ppermute(chunks[k], 'modes', pairs)  11.6 us
    ppermute x3, starting transfers between devices, halo(): far = lax.ppermute(x, 'space', far)  9.86 us
    ppermute x3, waiting for transfers between devices, halo(): far = lax.ppermute(x, 'space', far)  4.7 us
  transfers between devices with their start and end apart: 18, of which 7 were waited for; matrix products, arithmetic and copies ran while one was open for 0% of the time, Pallas kernels for 22%

profile of v7, /device:TPU:11, one launch (start us, length us, event | category | flops | bytes accessed | tf_op | source)
XLA Modules:
  0.0 58.6 jit_solution(10887793050177305695)
XLA Ops:
  1.4 3.0 %collective-permute-start.1 = (f32[880,128]{1,0:T(8,128)}, f32[880,128]{1,0:T(8,128)S(1)}, u32[]{:S(2)}, u32[]{:S(2)}) collective-permute-start(f32[880,128]{1,0:T(8,128)} %bitcast.11), channel_id=1, source_target_pairs={{4,8},{8,4},{12,16},{16,12},{20,24},{24,20},{5,9},{9,5},{13,17},{1... | collective-permute-start | bytes 1351688 | tf_op jit(solution)/shard_map/ppermute | solution.py:492
  4.4 2.4 %shard_map.106 = (f32[232,128]{1,0:T(8,128)}, f32[232,128]{1,0:T(8,128)}, f32[232,128]{1,0:T(8,128)}, f32[232,128]{1,0:T(8,128)}) custom-call(f32[880,128]{1,0:T(8,128)} %bitcast.12, f32[880,128]{1,0:T(8,128)} %bitcast.23, f32[16,128]{1,0:T(8,128)} %bitcast.17), custom_call_target="tpu_custom_call" | custom-call | bytes 909312 | tf_op jit(solution)/shard_map/pallas_call | solution.py:468
  6.8 1.4 %collective-permute-start.3 = (f32[232,128]{1,0:T(8,128)}, f32[232,128]{1,0:T(8,128)S(1)}, u32[]{:S(2)}, u32[]{:S(2)}) collective-permute-start(f32[232,128]{1,0:T(8,128)} %get-tuple-element.40), channel_id=1, source_target_pairs={{0,3},{1,2},{2,1},{3,0},{4,7},{5,6},{6,5},{7,4},{8,11},{9,10},{10,... | collective-permute-start | bytes 356360 | tf_op jit(solution)/shard_map/ppermute | solution.py:484
  8.2 1.1 %collective-permute-start.4 = (f32[232,128]{1,0:T(8,128)}, f32[232,128]{1,0:T(8,128)S(1)}, u32[]{:S(2)}, u32[]{:S(2)}) collective-permute-start(f32[232,128]{1,0:T(8,128)} %get-tuple-element.42), channel_id=1, source_target_pairs={{0,2},{1,3},{2,0},{3,1},{4,6},{5,7},{6,4},{7,5},{8,10},{9,11},{10,... | collective-permute-start | bytes 356360 | tf_op jit(solution)/shard_map/ppermute | solution.py:484
  9.3 1.1 %collective-permute-start.5 = (f32[232,128]{1,0:T(8,128)}, f32[232,128]{1,0:T(8,128)S(1)}, u32[]{:S(2)}, u32[]{:S(2)}) collective-permute-start(f32[232,128]{1,0:T(8,128)} %get-tuple-element.43), channel_id=1, source_target_pairs={{0,1},{1,0},{2,3},{3,2},{4,5},{5,4},{6,7},{7,6},{8,9},{9,8},{10,11... | collective-permute-start | bytes 356360 | tf_op jit(solution)/shard_map/ppermute | solution.py:484
  11.1 3.9 %shard_map.104 = (bf16[4,224,224]{2,1,0:T(8,128)(2,1)S(1)}, bf16[4,224,224]{2,1,0:T(8,128)(2,1)S(1)}, bf16[512,224]{1,0:T(8,128)(2,1)S(1)}, bf16[512,224]{1,0:T(...) custom-call(s32[9,220]{1,0:T(8,128)S(1)} %bitcast.20, ...), custom_call_target="tpu_custom_call" | custom-call | bytes 36736 | tf_op jit(solution)/shard_map/pallas_call | solution.py:468
  15.0 1.4 %collective-permute-done.1.far_ref = f32[880,128]{1,0:T(8,128)S(1)} collective-permute-done((f32[880,128]{1,0:T(8,128)}, f32[880,128]{1,0:T(8,128)S(1)}, u32[]{:S(2)}, u32[]{:S(2)}) %collective-permute-start.1) | collective-permute-done | bytes 450592 | tf_op jit(solution)/shard_map/ppermute | solution.py:492
  16.4 0.9 %shard_map.105 = (f32[232,128]{1,0:T(8,128)S(1)}, f32[232,128]{1,0:T(8,128)S(1)}, f32[232,128]{1,0:T(8,128)S(1)}, f32[232,128]{1,0:T(8,128)S(1)}) custom-call(f32[880,128]{1,0:T(8,128)S(1)} %bitcast.13, f32[880,128]{1,0:T(8,128)S(1)} %collective-permute-done.near_ref, f32[880,128]{1,0:T(8,128)S(1)} %collective-permute-done.1.far_ref), custom_call_target="tpu_custom_call" | custom-call | bytes 1351680 | tf_op jit(solution)/shard_map/pallas_call | solution.py:468
  17.5 2.6 %collective-permute-start.7 = (f32[232,128]{1,0:T(8,128)S(1)}, f32[232,128]{1,0:T(8,128)S(1)}, u32[]{:S(2)}, u32[]{:S(2)}) collective-permute-start(f32[232,128]{1,0:T(8,128)S(1)} %get-tuple-element.46), channel_id=1, source_target_pairs={{0,2},{1,3},{2,0},{3,1},{4,6},{5,7},{6,4},{7,5},{8,10},{9,11},{10,... | collective-permute-start | bytes 356360 | tf_op jit(solution)/shard_map/ppermute | solution.py:484
  20.1 4.0 %collective-permute-start.10 = (f32[880,128]{1,0:T(8,128)S(1)}, f32[880,128]{1,0:T(8,128)S(1)}, u32[]{:S(2)}, u32[]{:S(2)}) collective-permute-start(f32[880,128]{1,0:T(8,128)S(1)} %bitcast.14), channel_id=1, source_target_pairs={{4,8},{8,4},{12,16},{16,12},{20,24},{24,20},{5,9},{9,5},{13,17},{1... | collective-permute-start | bytes 1351688 | tf_op jit(solution)/shard_map/ppermute | solution.py:492
  24.3 4.0 %collective-permute-done.7.refs_6_ = f32[232,128]{1,0:T(8,128)S(1)} collective-permute-done((f32[232,128]{1,0:T(8,128)S(1)}, f32[232,128]{1,0:T(8,128)S(1)}, u32[]{:S(2)}, u32[]{:S(2)}) %collective-permute-start.7) | collective-permute-done | bytes 118816 | tf_op jit(solution)/shard_map/ppermute | solution.py:484
  28.3 1.0 %shard_map.107.refs_1_ = f32[224,640]{1,0:T(8,128)S(1)} custom-call(f32[232,128]{1,0:T(8,128)S(1)} %copy-done.2, f32[232,128]{1,0:T(8,128)S(1)} %collective-permute-done.3.refs_1_, f32[232,128]{1,0:T(8,128)S(1)} %collective-permute-done.4.refs_2_, f32[232,128]{1,0:T(8,128)S(1)} %collective-permute-done.5.refs_3_, f32[232,128]{1,0:T(8,128)S(1)} %get-tuple-element.44.refs_4_, ...), custom_call_target="tpu_custom_call" | custom-call | bytes 1636864 | tf_op jit(solution)/shard_map/pallas_call | solution.py:468
  29.3 1.3 %collective-permute-done.2.refs_0_ = f32[232,128]{1,0:T(8,128)S(1)} collective-permute-done((f32[232,128]{1,0:T(8,128)S(1)}, f32[232,128]{1,0:T(8,128)S(1)}, u32[]{:S(2)}, u32[]{:S(2)}) %collective-permute-start.2) | collective-permute-done | bytes 118816 | tf_op jit(solution)/shard_map/ppermute | solution.py:484
  31.4 2.8 %collective-permute-start.14 = (f32[224,512]{1,0:T(8,128)S(1)}, f32[224,512]{1,0:T(8,128)S(1)}, u32[]{:S(2)}, u32[]{:S(2)}) collective-permute-start(f32[224,512]{1,0:T(8,128)S(1)} %get-tuple-element.56.refs_0_), channel_id=1, source_target_pairs={{4,8},{8,4},{12,16},{16,12},{20,24},{24,20},{5,9},{9,5},{13,17},{1... | collective-permute-start | bytes 1376264 | tf_op jit(solution)/shard_map/ppermute | solution.py:492
  35.5 3.8 %collective-permute-start.11 = (f32[224,128]{1,0:T(8,128)S(1)}, f32[224,128]{1,0:T(8,128)S(1)}, u32[]{:S(2)}, u32[]{:S(2)}) collective-permute-start(f32[224,128]{1,0:T(8,128)S(1)} %get-tuple-element.54), channel_id=1, source_target_pairs={{0,2},{1,3},{2,0},{3,1},{4,6},{5,7},{6,4},{7,5},{8,10},{9,11},{10,... | collective-permute-start | bytes 344072 | tf_op jit(solution)/shard_map/ppermute | solution.py:484
  39.4 1.5 %collective-permute-start.8 = (f32[224,128]{1,0:T(8,128)S(1)}, f32[224,128]{1,0:T(8,128)S(1)}, u32[]{:S(2)}, u32[]{:S(2)}) collective-permute-start(f32[224,128]{1,0:T(8,128)S(1)} %get-tuple-element.51), channel_id=1, source_target_pairs={{0,1},{1,2},{2,3},{3,0},{4,5},{5,6},{6,7},{7,4},{8,9},{9,10},{10,1... | collective-permute-start | bytes 344072 | tf_op jit(solution)/shard_map/ppermute | solution.py:484
  40.8 1.5 %shard_map.111 = (f32[512,512]{1,0:T(8,128)S(1)}, f32[512,512]{1,0:T(8,128)S(1)}) custom-call(f32[224,512]{1,0:T(8,128)S(1)} %get-tuple-element.56.refs_0_, f32[224,128]{1,0:T(8,128)S(1)} %get-tuple-element.57.refs_1_, s32[1,640]{1,0:T(1,128)S(1)} %get-tuple-element.49.refs_9_.refs_4_.refs_2_, bf16[512,224]{1,0:T(8,128)(2,1)S(1)} %get-tuple-element.58.refs_3_.bh_ref, ...), custom_call_target="tpu_custom_call" | custom-call | bytes 1165824 | tf_op jit(solution)/shard_map/pallas_call | solution.py:468
  42.4 2.7 %collective-permute-done.14.far_ref = f32[224,512]{1,0:T(8,128)S(1)} collective-permute-done((f32[224,512]{1,0:T(8,128)S(1)}, f32[224,512]{1,0:T(8,128)S(1)}, u32[]{:S(2)}, u32[]{:S(2)}) %collective-permute-start.14) | collective-permute-done | bytes 458784 | tf_op jit(solution)/shard_map/ppermute | solution.py:492
  45.1 1.2 %shard_map.112 = (f32[224,128]{1,0:T(8,128)S(1)}, f32[224,128]{1,0:T(8,128)S(1)}, f32[224,128]{1,0:T(8,128)S(1)}, f32[224,128]{1,0:T(8,128)S(1)}) custom-call(f32[224,512]{1,0:T(8,128)S(1)} %collective-permute-done.13.near_ref, f32[224,512]{1,0:T(8,128)S(1)} %collective-permute-done.14.far_ref, f32[512,512]{1,0:T(8,128)S(1)} %get-tuple-element.61.part_ref, ...), custom_call_target="tpu_custom_call" | custom-call | bytes 3940352 | tf_op jit(solution)/shard_map/pallas_call | solution.py:468
  46.3 2.8 %collective-permute-start.15 = (f32[224,128]{1,0:T(8,128)S(1)}, f32[224,128]{1,0:T(8,128)S(1)}, u32[]{:S(2)}, u32[]{:S(2)}) collective-permute-start(f32[224,128]{1,0:T(8,128)S(1)} %get-tuple-element.66), channel_id=1, source_target_pairs={{0,2},{1,3},{2,0},{3,1},{4,6},{5,7},{6,4},{7,5},{8,10},{9,11},{10,... | collective-permute-start | bytes 344072 | tf_op jit(solution)/shard_map/ppermute | solution.py:484
  49.1 1.5 %collective-permute-start.17 = (f32[224,128]{1,0:T(8,128)S(1)}, f32[224,128]{1,0:T(8,128)S(1)}, u32[]{:S(2)}, u32[]{:S(2)}) collective-permute-start(f32[224,128]{1,0:T(8,128)S(1)} %get-tuple-element.68), channel_id=1, source_target_pairs={{0,1},{1,2},{2,3},{3,0},{4,5},{5,6},{6,7},{7,4},{8,9},{9,10},{10,1... | collective-permute-start | bytes 344072 | tf_op jit(solution)/shard_map/ppermute | solution.py:484
  51.4 4.6 %collective-permute-done.15.refs_1_ = f32[224,128]{1,0:T(8,128)S(1)} collective-permute-done((f32[224,128]{1,0:T(8,128)S(1)}, f32[224,128]{1,0:T(8,128)S(1)}, u32[]{:S(2)}, u32[]{:S(2)}) %collective-permute-start.15) | collective-permute-done | bytes 114720 | tf_op jit(solution)/shard_map/ppermute | solution.py:484
  56.0 1.7 %collective-permute-done.16.refs_2_ = f32[224,128]{1,0:T(8,128)S(1)} collective-permute-done((f32[224,128]{1,0:T(8,128)S(1)}, f32[224,128]{1,0:T(8,128)S(1)}, u32[]{:S(2)}, u32[]{:S(2)}) %collective-permute-start.16) | collective-permute-done | bytes 114720 | tf_op jit(solution)/shard_map/ppermute | solution.py:484
  57.8 0.9 %shard_map.113 = f32[880,128]{1,0:T(8,128)} custom-call(f32[224,128]{1,0:T(8,128)S(1)} %get-tuple-element.65.refs_0_, f32[224,128]{1,0:T(8,128)S(1)} %collective-permute-done.15.refs_1_, f32[224,128]{1,0:T(8,128)S(1)} %collective-permute-done.16.refs_2_, f32[224,128]{1,0:T(8,128)S(1)} %collective-permute-done.17.refs_3_, f32[896,128]{1,0:T(8,128)S(1)} %shard_map.109.refs_4_), custom_call_target="tpu_custom_call" | custom-call | bytes 917504 | tf_op jit(solution)/shard_map/pallas_call | solution.py:468
  (40 shorter events, 4.7 us)
Async XLA Ops:
  0.6 14.4 %collective-permute-start = (f32[880,128]{1,0:T(8,128)}, f32[880,128]{1,0:T(8,128)S(1)}, u32[]{:S(2)}, u32[]{:S(2)}) collective-permute-start(f32[880,128]{1,0:T(8,128)} %bitcast.10), channel_id=1, source_target_pairs={{0,4},{4,0},{8,12},{12,8},{16,20},{20,16},{24,28},{28,24},{1,5},{5... | collective-permute-start | bytes 1351688 | tf_op jit(solution)/shard_map/ppermute | solution.py:493
  1.4 15.0 %collective-permute-start.1 = (f32[880,128]{1,0:T(8,128)}, f32[880,128]{1,0:T(8,128)S(1)}, u32[]{:S(2)}, u32[]{:S(2)}) collective-permute-start(f32[880,128]{1,0:T(8,128)} %bitcast.11), channel_id=1, source_target_pairs={{4,8},{8,4},{12,16},{16,12},{20,24},{24,20},{5,9},{9,5},{13,17},{1... | collective-permute-start | bytes 1351688 | tf_op jit(solution)/shard_map/ppermute | solution.py:492
  4.4 6.0 %copy-start.4 = (s32[512,9]{0,1:T(8,128)S(1)}, s32[512,9]{0,1:T(8,128)}, u32[]{:S(2)}) copy-start(s32[512,9]{0,1:T(8,128)} %param.16) | copy-start | bytes 55300
  4.4 6.0 %copy-start.5 = (s32[220,9]{0,1:T(8,128)S(1)}, s32[220,9]{0,1:T(8,128)}, u32[]{:S(2)}) copy-start(s32[220,9]{0,1:T(8,128)} %param.15) | copy-start | bytes 23764
  4.4 12.0 %copy-start = (f32[55,1,2048]{2,1,0:T(1,128)S(1)}, f32[55,1,2048]{2,1,0:T(1,128)}, u32[]{:S(2)}) copy-start(f32[55,1,2048]{2,1,0:T(1,128)} %param.9) | copy-start | bytes 1351684
  6.8 13.3 %collective-permute-start.3 = (f32[232,128]{1,0:T(8,128)}, f32[232,128]{1,0:T(8,128)S(1)}, u32[]{:S(2)}, u32[]{:S(2)}) collective-permute-start(f32[232,128]{1,0:T(8,128)} %get-tuple-element.40), channel_id=1, source_target_pairs={{0,3},{1,2},{2,1},{3,0},{4,7},{5,6},{6,5},{7,4},{8,11},{9,10},{10,... | collective-permute-start | bytes 356360 | tf_op jit(solution)/shard_map/ppermute | solution.py:484
  8.2 11.9 %collective-permute-start.4 = (f32[232,128]{1,0:T(8,128)}, f32[232,128]{1,0:T(8,128)S(1)}, u32[]{:S(2)}, u32[]{:S(2)}) collective-permute-start(f32[232,128]{1,0:T(8,128)} %get-tuple-element.42), channel_id=1, source_target_pairs={{0,2},{1,3},{2,0},{3,1},{4,6},{5,7},{6,4},{7,5},{8,10},{9,11},{10,... | collective-permute-start | bytes 356360 | tf_op jit(solution)/shard_map/ppermute | solution.py:484
  9.3 14.9 %collective-permute-start.5 = (f32[232,128]{1,0:T(8,128)}, f32[232,128]{1,0:T(8,128)S(1)}, u32[]{:S(2)}, u32[]{:S(2)}) collective-permute-start(f32[232,128]{1,0:T(8,128)} %get-tuple-element.43), channel_id=1, source_target_pairs={{0,1},{1,0},{2,3},{3,2},{4,5},{5,4},{6,7},{7,6},{8,9},{9,8},{10,11... | collective-permute-start | bytes 356360 | tf_op jit(solution)/shard_map/ppermute | solution.py:484
  15.0 5.1 %copy-start.1 = (f32[55,1,2048]{2,1,0:T(1,128)S(1)}, f32[55,1,2048]{2,1,0:T(1,128)}, u32[]{:S(2)}) copy-start(f32[55,1,2048]{2,1,0:T(1,128)} %param.11) | copy-start | bytes 1351684
  15.0 13.3 %copy-start.2 = (f32[232,128]{1,0:T(8,128)S(1)}, f32[232,128]{1,0:T(8,128)}, u32[]{:S(2)}) copy-start(f32[232,128]{1,0:T(8,128)} %get-tuple-element.39.refs_0_) | copy-start | bytes 356356
  17.3 7.0 %collective-permute-start.6 = (f32[232,128]{1,0:T(8,128)S(1)}, f32[232,128]{1,0:T(8,128)S(1)}, u32[]{:S(2)}, u32[]{:S(2)}) collective-permute-start(f32[232,128]{1,0:T(8,128)S(1)} %get-tuple-element.45), channel_id=1, source_target_pairs={{0,1},{1,0},{2,3},{3,2},{4,5},{5,4},{6,7},{7,6},{8,9},{9,8},{10,11... | collective-permute-start | bytes 356360 | tf_op jit(solution)/shard_map/ppermute | solution.py:484
  17.5 10.8 %collective-permute-start.7 = (f32[232,128]{1,0:T(8,128)S(1)}, f32[232,128]{1,0:T(8,128)S(1)}, u32[]{:S(2)}, u32[]{:S(2)}) collective-permute-start(f32[232,128]{1,0:T(8,128)S(1)} %get-tuple-element.46), channel_id=1, source_target_pairs={{0,2},{1,3},{2,0},{3,1},{4,6},{5,7},{6,4},{7,5},{8,10},{9,11},{10,... | collective-permute-start | bytes 356360 | tf_op jit(solution)/shard_map/ppermute | solution.py:484
  20.1 10.5 %collective-permute-start.2 = (f32[232,128]{1,0:T(8,128)S(1)}, f32[232,128]{1,0:T(8,128)S(1)}, u32[]{:S(2)}, u32[]{:S(2)}) collective-permute-start(f32[232,128]{1,0:T(8,128)S(1)} %get-tuple-element.38), channel_id=1, source_target_pairs={{0,3},{1,2},{2,1},{3,0},{4,7},{5,6},{6,5},{7,4},{8,11},{9,10},{10,... | collective-permute-start | bytes 356360 | tf_op jit(solution)/shard_map/ppermute | solution.py:484
  20.1 14.7 %collective-permute-start.10 = (f32[880,128]{1,0:T(8,128)S(1)}, f32[880,128]{1,0:T(8,128)S(1)}, u32[]{:S(2)}, u32[]{:S(2)}) collective-permute-start(f32[880,128]{1,0:T(8,128)S(1)} %bitcast.14), channel_id=1, source_target_pairs={{4,8},{8,4},{12,16},{16,12},{20,24},{24,20},{5,9},{9,5},{13,17},{1... | collective-permute-start | bytes 1351688 | tf_op jit(solution)/shard_map/ppermute | solution.py:492
  24.2 10.6 %collective-permute-start.9 = (f32[880,128]{1,0:T(8,128)S(1)}, f32[880,128]{1,0:T(8,128)S(1)}, u32[]{:S(2)}, u32[]{:S(2)}) collective-permute-start(f32[880,128]{1,0:T(8,128)S(1)} %bitcast.15), channel_id=1, source_target_pairs={{0,4},{4,0},{8,12},{12,8},{16,20},{20,16},{24,28},{28,24},{1,5},{5... | collective-permute-start | bytes 1351688 | tf_op jit(solution)/shard_map/ppermute | solution.py:493
  31.1 11.2 %collective-permute-start.13 = (f32[224,512]{1,0:T(8,128)S(1)}, f32[224,512]{1,0:T(8,128)S(1)}, u32[]{:S(2)}, u32[]{:S(2)}) collective-permute-start(f32[224,512]{1,0:T(8,128)S(1)} %get-tuple-element.56.refs_0_), channel_id=1, source_target_pairs={{0,4},{4,0},{8,12},{12,8},{16,20},{20,16},{24,28},{28,24},{1,5},{5... | collective-permute-start | bytes 1376264 | tf_op jit(solution)/shard_map/ppermute | solution.py:493
  31.4 13.7 %collective-permute-start.14 = (f32[224,512]{1,0:T(8,128)S(1)}, f32[224,512]{1,0:T(8,128)S(1)}, u32[]{:S(2)}, u32[]{:S(2)}) collective-permute-start(f32[224,512]{1,0:T(8,128)S(1)} %get-tuple-element.56.refs_0_), channel_id=1, source_target_pairs={{4,8},{8,4},{12,16},{16,12},{20,24},{24,20},{5,9},{9,5},{13,17},{1... | collective-permute-start | bytes 1376264 | tf_op jit(solution)/shard_map/ppermute | solution.py:492
  35.5 13.6 %collective-permute-start.11 = (f32[224,128]{1,0:T(8,128)S(1)}, f32[224,128]{1,0:T(8,128)S(1)}, u32[]{:S(2)}, u32[]{:S(2)}) collective-permute-start(f32[224,128]{1,0:T(8,128)S(1)} %get-tuple-element.54), channel_id=1, source_target_pairs={{0,2},{1,3},{2,0},{3,1},{4,6},{5,7},{6,4},{7,5},{8,10},{9,11},{10,... | collective-permute-start | bytes 344072 | tf_op jit(solution)/shard_map/ppermute | solution.py:484
  39.4 11.2 %collective-permute-start.12 = (f32[224,128]{1,0:T(8,128)S(1)}, f32[224,128]{1,0:T(8,128)S(1)}, u32[]{:S(2)}, u32[]{:S(2)}) collective-permute-start(f32[224,128]{1,0:T(8,128)S(1)} %get-tuple-element.55), channel_id=1, source_target_pairs={{0,3},{1,0},{2,1},{3,2},{4,7},{5,4},{6,5},{7,6},{8,11},{9,8},{10,9... | collective-permute-start | bytes 344072 | tf_op jit(solution)/shard_map/ppermute | solution.py:484
  39.4 11.2 %collective-permute-start.8 = (f32[224,128]{1,0:T(8,128)S(1)}, f32[224,128]{1,0:T(8,128)S(1)}, u32[]{:S(2)}, u32[]{:S(2)}) collective-permute-start(f32[224,128]{1,0:T(8,128)S(1)} %get-tuple-element.51), channel_id=1, source_target_pairs={{0,1},{1,2},{2,3},{3,0},{4,5},{5,6},{6,7},{7,4},{8,9},{9,10},{10,1... | collective-permute-start | bytes 344072 | tf_op jit(solution)/shard_map/ppermute | solution.py:484
  40.8 4.3 %copy-start.3 = (f32[1,2048]{1,0:T(1,128)S(1)}, f32[1,2048]{1,0:T(1,128)}, u32[]{:S(2)}) copy-start(f32[1,2048]{1,0:T(1,128)} %param.12) | copy-start | bytes 24580
  46.3 9.8 %collective-permute-start.15 = (f32[224,128]{1,0:T(8,128)S(1)}, f32[224,128]{1,0:T(8,128)S(1)}, u32[]{:S(2)}, u32[]{:S(2)}) collective-permute-start(f32[224,128]{1,0:T(8,128)S(1)} %get-tuple-element.66), channel_id=1, source_target_pairs={{0,2},{1,3},{2,0},{3,1},{4,6},{5,7},{6,4},{7,5},{8,10},{9,11},{10,... | collective-permute-start | bytes 344072 | tf_op jit(solution)/shard_map/ppermute | solution.py:484
  49.1 8.7 %collective-permute-start.16 = (f32[224,128]{1,0:T(8,128)S(1)}, f32[224,128]{1,0:T(8,128)S(1)}, u32[]{:S(2)}, u32[]{:S(2)}) collective-permute-start(f32[224,128]{1,0:T(8,128)S(1)} %get-tuple-element.67), channel_id=1, source_target_pairs={{0,3},{1,0},{2,1},{3,2},{4,7},{5,4},{6,5},{7,6},{8,11},{9,8},{10,9... | collective-permute-start | bytes 344072 | tf_op jit(solution)/shard_map/ppermute | solution.py:484
  49.1 8.6 %collective-permute-start.17 = (f32[224,128]{1,0:T(8,128)S(1)}, f32[224,128]{1,0:T(8,128)S(1)}, u32[]{:S(2)}, u32[]{:S(2)}) collective-permute-start(f32[224,128]{1,0:T(8,128)S(1)} %get-tuple-element.68), channel_id=1, source_target_pairs={{0,1},{1,2},{2,3},{3,0},{4,5},{5,6},{6,7},{7,4},{8,9},{9,10},{10,1... | collective-permute-start | bytes 344072 | tf_op jit(solution)/shard_map/ppermute | solution.py:484
  (3 other events, 5.0 us)

commit v8 on v7

--- a/solution.py
+++ b/solution.py
@@ -66,20 +66,18 @@
     return k
 
 
-def downward(k, parts):
-    return parts - k
-
-
-def turned(k, parts):
-    return 1 + k % (parts - 1)
-
-
-W_ROUTE, R_ROUTE, B_ROUTE, H_ROUTE = (
-    (True, downward),
-    (True, upward),
-    (False, upward),
-    (False, turned),
-)
+def longest_first(k, parts):
+    return (k - 2) % (parts - 1) + 1
+
+
+def longest_last(k, parts):
+    return parts - 1 - k if k < parts - 1 else k
+
+
+W_ROUTE = (True, longest_first)
+R_ROUTE = (True, longest_last)
+B_ROUTE = (False, upward)
+H_ROUTE = (False, longest_last)
 
 
 def load_group(ref, group, modes, groups):

time: 58.9 us -> 57.9 us (0.983)
  waiting for transfers between devices: 16.3 us -> 14.6 us
  starting transfers between devices: 27 us -> 27.7 us
    ppermute x12, waiting for transfers between devices: 11.6 us -> 9.9 us  [exchange(): received[k] = lax.ppermute(chunks[k], 'modes', pairs)]
  transfers between devices with their start and end apart: 18 -> 18, of which waited for: 7 -> 9; matrix products, arithmetic and copies ran while one was open for 0% -> 0% of each run, Pallas kernels for 22% -> 22%
where the time goes in v8:
time: 57.9 us; the launch traced here: 57.6 us
  starting transfers between devices  27.7 us (48%)
  waiting for transfers between devices  14.6 us (25%)
  Pallas kernels  13.8 us (24%)
  between operations  0.82 us (1%)
  local copies, waits for them, and re-layouts  0.71 us (1%)
    ppermute x12, starting transfers between devices, exchange(): received[k] = lax.ppermute(chunks[k], 'modes', pairs)  16.2 us
    pallas_call x10, Pallas kernels, call(): pl.pallas_call(kernel, out_shape=out_shape, in_specs=specs, out_specs=[wh...  13.8 us
    ppermute x3, starting transfers between devices, halo(): far = lax.ppermute(x, 'space', far)  10.2 us
    ppermute x12, waiting for transfers between devices, exchange(): received[k] = lax.ppermute(chunks[k], 'modes', pairs)  9.9 us
    ppermute x3, waiting for transfers between devices, halo(): far = lax.ppermute(x, 'space', far)  4.66 us
    ppermute x3, starting transfers between devices, halo(): return (lax.ppermute(x, 'space', near), far)  1.26 us
  transfers between devices with their start and end apart: 18, of which 9 were waited for; matrix products, arithmetic and copies ran while one was open for 0% of the time, Pallas kernels for 22%

profile of v8, /device:TPU:11, one launch (start us, length us, event | category | flops | bytes accessed | tf_op | source)
XLA Modules:
  0.0 57.6 jit_solution(16883695852974510628)
XLA Ops:
  1.4 3.0 %collective-permute-start.1 = (f32[880,128]{1,0:T(8,128)}, f32[880,128]{1,0:T(8,128)S(1)}, u32[]{:S(2)}, u32[]{:S(2)}) collective-permute-start(f32[880,128]{1,0:T(8,128)} %bitcast.11), channel_id=1, source_target_pairs={{4,8},{8,4},{12,16},{16,12},{20,24},{24,20},{5,9},{9,5},{13,17},{1... | collective-permute-start | bytes 1351688 | tf_op jit(solution)/shard_map/ppermute | solution.py:490
  4.4 2.4 %shard_map.106 = (f32[232,128]{1,0:T(8,128)}, f32[232,128]{1,0:T(8,128)}, f32[232,128]{1,0:T(8,128)}, f32[232,128]{1,0:T(8,128)}) custom-call(f32[880,128]{1,0:T(8,128)} %bitcast.12, f32[880,128]{1,0:T(8,128)} %bitcast.23, f32[16,128]{1,0:T(8,128)} %bitcast.17), custom_call_target="tpu_custom_call" | custom-call | bytes 909312 | tf_op jit(solution)/shard_map/pallas_call | solution.py:466
  6.8 1.4 %collective-permute-start.3 = (f32[232,128]{1,0:T(8,128)}, f32[232,128]{1,0:T(8,128)S(1)}, u32[]{:S(2)}, u32[]{:S(2)}) collective-permute-start(f32[232,128]{1,0:T(8,128)} %get-tuple-element.40), channel_id=1, source_target_pairs={{0,3},{1,2},{2,1},{3,0},{4,7},{5,6},{6,5},{7,4},{8,11},{9,10},{10,... | collective-permute-start | bytes 356360 | tf_op jit(solution)/shard_map/ppermute | solution.py:482
  8.2 2.2 %collective-permute-start.4 = (f32[232,128]{1,0:T(8,128)}, f32[232,128]{1,0:T(8,128)S(1)}, u32[]{:S(2)}, u32[]{:S(2)}) collective-permute-start(f32[232,128]{1,0:T(8,128)} %get-tuple-element.42), channel_id=1, source_target_pairs={{0,1},{1,0},{2,3},{3,2},{4,5},{5,4},{6,7},{7,6},{8,9},{9,8},{10,11... | collective-permute-start | bytes 356360 | tf_op jit(solution)/shard_map/ppermute | solution.py:482
  11.1 3.9 %shard_map.104 = (bf16[4,224,224]{2,1,0:T(8,128)(2,1)S(1)}, bf16[4,224,224]{2,1,0:T(8,128)(2,1)S(1)}, bf16[512,224]{1,0:T(8,128)(2,1)S(1)}, bf16[512,224]{1,0:T(...) custom-call(s32[9,220]{1,0:T(8,128)S(1)} %bitcast.20, ...), custom_call_target="tpu_custom_call" | custom-call | bytes 36736 | tf_op jit(solution)/shard_map/pallas_call | solution.py:466
  15.0 1.7 %collective-permute-done.1.far_ref = f32[880,128]{1,0:T(8,128)S(1)} collective-permute-done((f32[880,128]{1,0:T(8,128)}, f32[880,128]{1,0:T(8,128)S(1)}, u32[]{:S(2)}, u32[]{:S(2)}) %collective-permute-start.1) | collective-permute-done | bytes 450592 | tf_op jit(solution)/shard_map/ppermute | solution.py:490
  16.7 0.9 %shard_map.105 = (f32[232,128]{1,0:T(8,128)S(1)}, f32[232,128]{1,0:T(8,128)S(1)}, f32[232,128]{1,0:T(8,128)S(1)}, f32[232,128]{1,0:T(8,128)S(1)}) custom-call(f32[880,128]{1,0:T(8,128)S(1)} %bitcast.13, f32[880,128]{1,0:T(8,128)S(1)} %collective-permute-done.near_ref, f32[880,128]{1,0:T(8,128)S(1)} %collective-permute-done.1.far_ref), custom_call_target="tpu_custom_call" | custom-call | bytes 1351680 | tf_op jit(solution)/shard_map/pallas_call | solution.py:466
  17.6 2.4 %collective-permute-start.6 = (f32[232,128]{1,0:T(8,128)S(1)}, f32[232,128]{1,0:T(8,128)S(1)}, u32[]{:S(2)}, u32[]{:S(2)}) collective-permute-start(f32[232,128]{1,0:T(8,128)S(1)} %get-tuple-element.45), channel_id=1, source_target_pairs={{0,2},{1,3},{2,0},{3,1},{4,6},{5,7},{6,4},{7,5},{8,10},{9,11},{10,... | collective-permute-start | bytes 356360 | tf_op jit(solution)/shard_map/ppermute | solution.py:482
  20.3 3.8 %collective-permute-start.10 = (f32[880,128]{1,0:T(8,128)S(1)}, f32[880,128]{1,0:T(8,128)S(1)}, u32[]{:S(2)}, u32[]{:S(2)}) collective-permute-start(f32[880,128]{1,0:T(8,128)S(1)} %bitcast.14), channel_id=1, source_target_pairs={{4,8},{8,4},{12,16},{16,12},{20,24},{24,20},{5,9},{9,5},{13,17},{1... | collective-permute-start | bytes 1351688 | tf_op jit(solution)/shard_map/ppermute | solution.py:490
  24.6 1.2 %collective-permute-done.7.refs_6_ = f32[232,128]{1,0:T(8,128)S(1)} collective-permute-done((f32[232,128]{1,0:T(8,128)S(1)}, f32[232,128]{1,0:T(8,128)S(1)}, u32[]{:S(2)}, u32[]{:S(2)}) %collective-permute-start.7) | collective-permute-done | bytes 118816 | tf_op jit(solution)/shard_map/ppermute | solution.py:482
  25.8 1.0 %shard_map.107.refs_1_ = f32[224,640]{1,0:T(8,128)S(1)} custom-call(f32[232,128]{1,0:T(8,128)S(1)} %copy-done.2, f32[232,128]{1,0:T(8,128)S(1)} %collective-permute-done.3.refs_1_, f32[232,128]{1,0:T(8,128)S(1)} %collective-permute-done.4.refs_2_, f32[232,128]{1,0:T(8,128)S(1)} %collective-permute-done.5.refs_3_, f32[232,128]{1,0:T(8,128)S(1)} %get-tuple-element.44.refs_4_, ...), custom_call_target="tpu_custom_call" | custom-call | bytes 1636864 | tf_op jit(solution)/shard_map/pallas_call | solution.py:466
  26.8 3.1 %collective-permute-done.2.refs_0_ = f32[232,128]{1,0:T(8,128)S(1)} collective-permute-done((f32[232,128]{1,0:T(8,128)S(1)}, f32[232,128]{1,0:T(8,128)S(1)}, u32[]{:S(2)}, u32[]{:S(2)}) %collective-permute-start.2) | collective-permute-done | bytes 118816 | tf_op jit(solution)/shard_map/ppermute | solution.py:482
  30.9 3.3 %collective-permute-start.14 = (f32[224,512]{1,0:T(8,128)S(1)}, f32[224,512]{1,0:T(8,128)S(1)}, u32[]{:S(2)}, u32[]{:S(2)}) collective-permute-start(f32[224,512]{1,0:T(8,128)S(1)} %get-tuple-element.56.refs_0_), channel_id=1, source_target_pairs={{4,8},{8,4},{12,16},{16,12},{20,24},{24,20},{5,9},{9,5},{13,17},{1... | collective-permute-start | bytes 1376264 | tf_op jit(solution)/shard_map/ppermute | solution.py:490
  35.5 4.2 %collective-permute-start.11 = (f32[224,128]{1,0:T(8,128)S(1)}, f32[224,128]{1,0:T(8,128)S(1)}, u32[]{:S(2)}, u32[]{:S(2)}) collective-permute-start(f32[224,128]{1,0:T(8,128)S(1)} %get-tuple-element.54), channel_id=1, source_target_pairs={{0,2},{1,3},{2,0},{3,1},{4,6},{5,7},{6,4},{7,5},{8,10},{9,11},{10,... | collective-permute-start | bytes 344072 | tf_op jit(solution)/shard_map/ppermute | solution.py:482
  39.7 1.5 %collective-permute-start.8 = (f32[224,128]{1,0:T(8,128)S(1)}, f32[224,128]{1,0:T(8,128)S(1)}, u32[]{:S(2)}, u32[]{:S(2)}) collective-permute-start(f32[224,128]{1,0:T(8,128)S(1)} %get-tuple-element.51), channel_id=1, source_target_pairs={{0,1},{1,2},{2,3},{3,0},{4,5},{5,6},{6,7},{7,4},{8,9},{9,10},{10,1... | collective-permute-start | bytes 344072 | tf_op jit(solution)/shard_map/ppermute | solution.py:482
  41.2 1.5 %shard_map.111 = (f32[512,512]{1,0:T(8,128)S(1)}, f32[512,512]{1,0:T(8,128)S(1)}) custom-call(f32[224,512]{1,0:T(8,128)S(1)} %get-tuple-element.56.refs_0_, f32[224,128]{1,0:T(8,128)S(1)} %get-tuple-element.57.refs_1_, s32[1,640]{1,0:T(1,128)S(1)} %get-tuple-element.49.refs_9_.refs_4_.refs_2_, bf16[512,224]{1,0:T(8,128)(2,1)S(1)} %get-tuple-element.58.refs_3_.bh_ref, ...), custom_call_target="tpu_custom_call" | custom-call | bytes 1165824 | tf_op jit(solution)/shard_map/pallas_call | solution.py:466
  42.7 2.4 %collective-permute-done.14.far_ref = f32[224,512]{1,0:T(8,128)S(1)} collective-permute-done((f32[224,512]{1,0:T(8,128)S(1)}, f32[224,512]{1,0:T(8,128)S(1)}, u32[]{:S(2)}, u32[]{:S(2)}) %collective-permute-start.14) | collective-permute-done | bytes 458784 | tf_op jit(solution)/shard_map/ppermute | solution.py:490
  45.1 1.2 %shard_map.112 = (f32[224,128]{1,0:T(8,128)S(1)}, f32[224,128]{1,0:T(8,128)S(1)}, f32[224,128]{1,0:T(8,128)S(1)}, f32[224,128]{1,0:T(8,128)S(1)}) custom-call(f32[224,512]{1,0:T(8,128)S(1)} %collective-permute-done.13.near_ref, f32[224,512]{1,0:T(8,128)S(1)} %collective-permute-done.14.far_ref, f32[512,512]{1,0:T(8,128)S(1)} %get-tuple-element.61.part_ref, ...), custom_call_target="tpu_custom_call" | custom-call | bytes 3940352 | tf_op jit(solution)/shard_map/pallas_call | solution.py:466
  46.3 2.8 %collective-permute-start.15 = (f32[224,128]{1,0:T(8,128)S(1)}, f32[224,128]{1,0:T(8,128)S(1)}, u32[]{:S(2)}, u32[]{:S(2)}) collective-permute-start(f32[224,128]{1,0:T(8,128)S(1)} %get-tuple-element.66), channel_id=1, source_target_pairs={{0,2},{1,3},{2,0},{3,1},{4,6},{5,7},{6,4},{7,5},{8,10},{9,11},{10,... | collective-permute-start | bytes 344072 | tf_op jit(solution)/shard_map/ppermute | solution.py:482
  49.1 1.5 %collective-permute-start.17 = (f32[224,128]{1,0:T(8,128)S(1)}, f32[224,128]{1,0:T(8,128)S(1)}, u32[]{:S(2)}, u32[]{:S(2)}) collective-permute-start(f32[224,128]{1,0:T(8,128)S(1)} %get-tuple-element.68), channel_id=1, source_target_pairs={{0,3},{1,0},{2,1},{3,2},{4,7},{5,4},{6,5},{7,6},{8,11},{9,8},{10,9... | collective-permute-start | bytes 344072 | tf_op jit(solution)/shard_map/ppermute | solution.py:482
  50.6 0.8 %shard_map.110 = f32[880,128]{1,0:T(8,128)} custom-call(f32[224,128]{1,0:T(8,128)S(1)} %get-tuple-element.50.refs_0_, f32[224,128]{1,0:T(8,128)S(1)} %collective-permute-done.8.refs_1_, f32[224,128]{1,0:T(8,128)S(1)} %collective-permute-done.11.refs_2_, f32[224,128]{1,0:T(8,128)S(1)} %collective-permute-done.12.refs_3_), custom_call_target="tpu_custom_call" | custom-call | bytes 458752 | tf_op jit(solution)/shard_map/pallas_call | solution.py:466
  51.4 2.1 %collective-permute-done.15.refs_1_ = f32[224,128]{1,0:T(8,128)S(1)} collective-permute-done((f32[224,128]{1,0:T(8,128)S(1)}, f32[224,128]{1,0:T(8,128)S(1)}, u32[]{:S(2)}, u32[]{:S(2)}) %collective-permute-start.15) | collective-permute-done | bytes 114720 | tf_op jit(solution)/shard_map/ppermute | solution.py:482
  53.5 2.8 %collective-permute-done.16.refs_2_ = f32[224,128]{1,0:T(8,128)S(1)} collective-permute-done((f32[224,128]{1,0:T(8,128)S(1)}, f32[224,128]{1,0:T(8,128)S(1)}, u32[]{:S(2)}, u32[]{:S(2)}) %collective-permute-start.16) | collective-permute-done | bytes 114720 | tf_op jit(solution)/shard_map/ppermute | solution.py:482
  56.7 0.8 %shard_map.113 = f32[880,128]{1,0:T(8,128)} custom-call(f32[224,128]{1,0:T(8,128)S(1)} %get-tuple-element.65.refs_0_, f32[224,128]{1,0:T(8,128)S(1)} %collective-permute-done.15.refs_1_, f32[224,128]{1,0:T(8,128)S(1)} %collective-permute-done.16.refs_2_, f32[224,128]{1,0:T(8,128)S(1)} %collective-permute-done.17.refs_3_, f32[896,128]{1,0:T(8,128)S(1)} %shard_map.109.refs_4_), custom_call_target="tpu_custom_call" | custom-call | bytes 917504 | tf_op jit(solution)/shard_map/pallas_call | solution.py:466
  (40 shorter events, 4.9 us)
Async XLA Ops:
  0.6 14.4 %collective-permute-start = (f32[880,128]{1,0:T(8,128)}, f32[880,128]{1,0:T(8,128)S(1)}, u32[]{:S(2)}, u32[]{:S(2)}) collective-permute-start(f32[880,128]{1,0:T(8,128)} %bitcast.10), channel_id=1, source_target_pairs={{0,4},{4,0},{8,12},{12,8},{16,20},{20,16},{24,28},{28,24},{1,5},{5... | collective-permute-start | bytes 1351688 | tf_op jit(solution)/shard_map/ppermute | solution.py:491
  1.4 15.3 %collective-permute-start.1 = (f32[880,128]{1,0:T(8,128)}, f32[880,128]{1,0:T(8,128)S(1)}, u32[]{:S(2)}, u32[]{:S(2)}) collective-permute-start(f32[880,128]{1,0:T(8,128)} %bitcast.11), channel_id=1, source_target_pairs={{4,8},{8,4},{12,16},{16,12},{20,24},{24,20},{5,9},{9,5},{13,17},{1... | collective-permute-start | bytes 1351688 | tf_op jit(solution)/shard_map/ppermute | solution.py:490
  4.4 6.0 %copy-start.4 = (s32[512,9]{0,1:T(8,128)S(1)}, s32[512,9]{0,1:T(8,128)}, u32[]{:S(2)}) copy-start(s32[512,9]{0,1:T(8,128)} %param.16) | copy-start | bytes 55300
  4.4 6.0 %copy-start.5 = (s32[220,9]{0,1:T(8,128)S(1)}, s32[220,9]{0,1:T(8,128)}, u32[]{:S(2)}) copy-start(s32[220,9]{0,1:T(8,128)} %param.15) | copy-start | bytes 23764
  4.4 12.3 %copy-start = (f32[55,1,2048]{2,1,0:T(1,128)S(1)}, f32[55,1,2048]{2,1,0:T(1,128)}, u32[]{:S(2)}) copy-start(f32[55,1,2048]{2,1,0:T(1,128)} %param.9) | copy-start | bytes 1351684
  6.8 13.1 %collective-permute-start.3 = (f32[232,128]{1,0:T(8,128)}, f32[232,128]{1,0:T(8,128)S(1)}, u32[]{:S(2)}, u32[]{:S(2)}) collective-permute-start(f32[232,128]{1,0:T(8,128)} %get-tuple-element.40), channel_id=1, source_target_pairs={{0,3},{1,2},{2,1},{3,0},{4,7},{5,6},{6,5},{7,4},{8,11},{9,10},{10,... | collective-permute-start | bytes 356360 | tf_op jit(solution)/shard_map/ppermute | solution.py:482
  8.2 12.1 %collective-permute-start.4 = (f32[232,128]{1,0:T(8,128)}, f32[232,128]{1,0:T(8,128)S(1)}, u32[]{:S(2)}, u32[]{:S(2)}) collective-permute-start(f32[232,128]{1,0:T(8,128)} %get-tuple-element.42), channel_id=1, source_target_pairs={{0,1},{1,0},{2,3},{3,2},{4,5},{5,4},{6,7},{7,6},{8,9},{9,8},{10,11... | collective-permute-start | bytes 356360 | tf_op jit(solution)/shard_map/ppermute | solution.py:482
  10.4 13.8 %collective-permute-start.5 = (f32[232,128]{1,0:T(8,128)}, f32[232,128]{1,0:T(8,128)S(1)}, u32[]{:S(2)}, u32[]{:S(2)}) collective-permute-start(f32[232,128]{1,0:T(8,128)} %get-tuple-element.43), channel_id=1, source_target_pairs={{0,2},{1,3},{2,0},{3,1},{4,6},{5,7},{6,4},{7,5},{8,10},{9,11},{10,... | collective-permute-start | bytes 356360 | tf_op jit(solution)/shard_map/ppermute | solution.py:482
  15.0 5.3 %copy-start.1 = (f32[55,1,2048]{2,1,0:T(1,128)S(1)}, f32[55,1,2048]{2,1,0:T(1,128)}, u32[]{:S(2)}) copy-start(f32[55,1,2048]{2,1,0:T(1,128)} %param.11) | copy-start | bytes 1351684
  15.0 10.8 %copy-start.2 = (f32[232,128]{1,0:T(8,128)S(1)}, f32[232,128]{1,0:T(8,128)}, u32[]{:S(2)}) copy-start(f32[232,128]{1,0:T(8,128)} %get-tuple-element.39.refs_0_) | copy-start | bytes 356356
  17.6 7.0 %collective-permute-start.6 = (f32[232,128]{1,0:T(8,128)S(1)}, f32[232,128]{1,0:T(8,128)S(1)}, u32[]{:S(2)}, u32[]{:S(2)}) collective-permute-start(f32[232,128]{1,0:T(8,128)S(1)} %get-tuple-element.45), channel_id=1, source_target_pairs={{0,2},{1,3},{2,0},{3,1},{4,6},{5,7},{6,4},{7,5},{8,10},{9,11},{10,... | collective-permute-start | bytes 356360 | tf_op jit(solution)/shard_map/ppermute | solution.py:482
  20.0 5.8 %collective-permute-start.7 = (f32[232,128]{1,0:T(8,128)S(1)}, f32[232,128]{1,0:T(8,128)S(1)}, u32[]{:S(2)}, u32[]{:S(2)}) collective-permute-start(f32[232,128]{1,0:T(8,128)S(1)} %get-tuple-element.46), channel_id=1, source_target_pairs={{0,1},{1,0},{2,3},{3,2},{4,5},{5,4},{6,7},{7,6},{8,9},{9,8},{10,11... | collective-permute-start | bytes 356360 | tf_op jit(solution)/shard_map/ppermute | solution.py:482
  20.0 10.0 %collective-permute-start.2 = (f32[232,128]{1,0:T(8,128)S(1)}, f32[232,128]{1,0:T(8,128)S(1)}, u32[]{:S(2)}, u32[]{:S(2)}) collective-permute-start(f32[232,128]{1,0:T(8,128)S(1)} %get-tuple-element.38), channel_id=1, source_target_pairs={{0,3},{1,2},{2,1},{3,0},{4,7},{5,6},{6,5},{7,4},{8,11},{9,10},{10,... | collective-permute-start | bytes 356360 | tf_op jit(solution)/shard_map/ppermute | solution.py:482
  20.3 14.5 %collective-permute-start.10 = (f32[880,128]{1,0:T(8,128)S(1)}, f32[880,128]{1,0:T(8,128)S(1)}, u32[]{:S(2)}, u32[]{:S(2)}) collective-permute-start(f32[880,128]{1,0:T(8,128)S(1)} %bitcast.14), channel_id=1, source_target_pairs={{4,8},{8,4},{12,16},{16,12},{20,24},{24,20},{5,9},{9,5},{13,17},{1... | collective-permute-start | bytes 1351688 | tf_op jit(solution)/shard_map/ppermute | solution.py:490
  24.2 10.6 %collective-permute-start.9 = (f32[880,128]{1,0:T(8,128)S(1)}, f32[880,128]{1,0:T(8,128)S(1)}, u32[]{:S(2)}, u32[]{:S(2)}) collective-permute-start(f32[880,128]{1,0:T(8,128)S(1)} %bitcast.15), channel_id=1, source_target_pairs={{0,4},{4,0},{8,12},{12,8},{16,20},{20,16},{24,28},{28,24},{1,5},{5... | collective-permute-start | bytes 1351688 | tf_op jit(solution)/shard_map/ppermute | solution.py:491
  30.4 12.2 %collective-permute-start.13 = (f32[224,512]{1,0:T(8,128)S(1)}, f32[224,512]{1,0:T(8,128)S(1)}, u32[]{:S(2)}, u32[]{:S(2)}) collective-permute-start(f32[224,512]{1,0:T(8,128)S(1)} %get-tuple-element.56.refs_0_), channel_id=1, source_target_pairs={{0,4},{4,0},{8,12},{12,8},{16,20},{20,16},{24,28},{28,24},{1,5},{5... | collective-permute-start | bytes 1376264 | tf_op jit(solution)/shard_map/ppermute | solution.py:491
  30.9 14.2 %collective-permute-start.14 = (f32[224,512]{1,0:T(8,128)S(1)}, f32[224,512]{1,0:T(8,128)S(1)}, u32[]{:S(2)}, u32[]{:S(2)}) collective-permute-start(f32[224,512]{1,0:T(8,128)S(1)} %get-tuple-element.56.refs_0_), channel_id=1, source_target_pairs={{4,8},{8,4},{12,16},{16,12},{20,24},{24,20},{5,9},{9,5},{13,17},{1... | collective-permute-start | bytes 1376264 | tf_op jit(solution)/shard_map/ppermute | solution.py:490
  35.5 13.6 %collective-permute-start.11 = (f32[224,128]{1,0:T(8,128)S(1)}, f32[224,128]{1,0:T(8,128)S(1)}, u32[]{:S(2)}, u32[]{:S(2)}) collective-permute-start(f32[224,128]{1,0:T(8,128)S(1)} %get-tuple-element.54), channel_id=1, source_target_pairs={{0,2},{1,3},{2,0},{3,1},{4,6},{5,7},{6,4},{7,5},{8,10},{9,11},{10,... | collective-permute-start | bytes 344072 | tf_op jit(solution)/shard_map/ppermute | solution.py:482
  39.7 10.9 %collective-permute-start.12 = (f32[224,128]{1,0:T(8,128)S(1)}, f32[224,128]{1,0:T(8,128)S(1)}, u32[]{:S(2)}, u32[]{:S(2)}) collective-permute-start(f32[224,128]{1,0:T(8,128)S(1)} %get-tuple-element.55), channel_id=1, source_target_pairs={{0,3},{1,0},{2,1},{3,2},{4,7},{5,4},{6,5},{7,6},{8,11},{9,8},{10,9... | collective-permute-start | bytes 344072 | tf_op jit(solution)/shard_map/ppermute | solution.py:482
  39.7 10.9 %collective-permute-start.8 = (f32[224,128]{1,0:T(8,128)S(1)}, f32[224,128]{1,0:T(8,128)S(1)}, u32[]{:S(2)}, u32[]{:S(2)}) collective-permute-start(f32[224,128]{1,0:T(8,128)S(1)} %get-tuple-element.51), channel_id=1, source_target_pairs={{0,1},{1,2},{2,3},{3,0},{4,5},{5,6},{6,7},{7,4},{8,9},{9,10},{10,1... | collective-permute-start | bytes 344072 | tf_op jit(solution)/shard_map/ppermute | solution.py:482
  41.2 3.9 %copy-start.3 = (f32[1,2048]{1,0:T(1,128)S(1)}, f32[1,2048]{1,0:T(1,128)}, u32[]{:S(2)}) copy-start(f32[1,2048]{1,0:T(1,128)} %param.12) | copy-start | bytes 24580
  46.3 7.2 %collective-permute-start.15 = (f32[224,128]{1,0:T(8,128)S(1)}, f32[224,128]{1,0:T(8,128)S(1)}, u32[]{:S(2)}, u32[]{:S(2)}) collective-permute-start(f32[224,128]{1,0:T(8,128)S(1)} %get-tuple-element.66), channel_id=1, source_target_pairs={{0,2},{1,3},{2,0},{3,1},{4,6},{5,7},{6,4},{7,5},{8,10},{9,11},{10,... | collective-permute-start | bytes 344072 | tf_op jit(solution)/shard_map/ppermute | solution.py:482
  49.1 7.2 %collective-permute-start.16 = (f32[224,128]{1,0:T(8,128)S(1)}, f32[224,128]{1,0:T(8,128)S(1)}, u32[]{:S(2)}, u32[]{:S(2)}) collective-permute-start(f32[224,128]{1,0:T(8,128)S(1)} %get-tuple-element.67), channel_id=1, source_target_pairs={{0,1},{1,2},{2,3},{3,0},{4,5},{5,6},{6,7},{7,4},{8,9},{9,10},{10,1... | collective-permute-start | bytes 344072 | tf_op jit(solution)/shard_map/ppermute | solution.py:482
  49.1 7.6 %collective-permute-start.17 = (f32[224,128]{1,0:T(8,128)S(1)}, f32[224,128]{1,0:T(8,128)S(1)}, u32[]{:S(2)}, u32[]{:S(2)}) collective-permute-start(f32[224,128]{1,0:T(8,128)S(1)} %get-tuple-element.68), channel_id=1, source_target_pairs={{0,3},{1,0},{2,1},{3,2},{4,7},{5,4},{6,5},{7,6},{8,11},{9,8},{10,9... | collective-permute-start | bytes 344072 | tf_op jit(solution)/shard_map/ppermute | solution.py:482
  (3 other events, 5.0 us)

commit v9 on v8

--- a/solution.py
+++ b/solution.py
@@ -573,7 +573,7 @@
         struct(groups * padded, LANES), [temp, t_near, t_far],
     )
     wide = (per + 1) * LANES
-    count = parts - 1
+    count = max(1, parts // 2)
     most = call(
         functools.partial(couple_kernel, parts, padded, per, nreg, count),
         struct(rows, wide), [*source, *rough[:count], a_high, a_low, zones],

time: 57.9 us -> 58.1 us (level)
  no operation moved by 1% of the time
where the time goes in v9:
time: 58.1 us; the launch traced here: 57.8 us
  starting transfers between devices  27.4 us (47%)
  waiting for transfers between devices  15.1 us (26%)
  Pallas kernels  13.8 us (24%)
  between operations  0.82 us (1%)
  local copies, waits for them, and re-layouts  0.71 us (1%)
    ppermute x12, starting transfers between devices, exchange(): received[k] = lax.ppermute(chunks[k], 'modes', pairs)  16 us
    pallas_call x10, Pallas kernels, call(): pl.pallas_call(kernel, out_shape=out_shape, in_specs=specs, out_specs=[wh...  13.8 us
    ppermute x12, waiting for transfers between devices, exchange(): received[k] = lax.ppermute(chunks[k], 'modes', pairs)  10.4 us
    ppermute x3, starting transfers between devices, halo(): far = lax.ppermute(x, 'space', far)  10.2 us
    ppermute x3, waiting for transfers between devices, halo(): far = lax.ppermute(x, 'space', far)  4.64 us
    ppermute x3, starting transfers between devices, halo(): return (lax.ppermute(x, 'space', near), far)  1.26 us
  transfers between devices with their start and end apart: 18, of which 9 were waited for; matrix products, arithmetic and copies ran while one was open for 0% of the time, Pallas kernels for 22%

profile of v9, /device:TPU:11, one launch (start us, length us, event | category | flops | bytes accessed | tf_op | source)
XLA Modules:
  0.0 57.8 jit_solution(16209606014589044249)
XLA Ops:
  1.4 3.0 %collective-permute-start.1 = (f32[880,128]{1,0:T(8,128)}, f32[880,128]{1,0:T(8,128)S(1)}, u32[]{:S(2)}, u32[]{:S(2)}) collective-permute-start(f32[880,128]{1,0:T(8,128)} %bitcast.11), channel_id=1, source_target_pairs={{4,8},{8,4},{12,16},{16,12},{20,24},{24,20},{5,9},{9,5},{13,17},{1... | collective-permute-start | bytes 1351688 | tf_op jit(solution)/shard_map/ppermute | solution.py:490
  4.4 2.4 %shard_map.106 = (f32[232,128]{1,0:T(8,128)}, f32[232,128]{1,0:T(8,128)}, f32[232,128]{1,0:T(8,128)}, f32[232,128]{1,0:T(8,128)}) custom-call(f32[880,128]{1,0:T(8,128)} %bitcast.12, f32[880,128]{1,0:T(8,128)} %bitcast.23, f32[16,128]{1,0:T(8,128)} %bitcast.17), custom_call_target="tpu_custom_call" | custom-call | bytes 909312 | tf_op jit(solution)/shard_map/pallas_call | solution.py:466
  6.8 1.4 %collective-permute-start.4 = (f32[232,128]{1,0:T(8,128)}, f32[232,128]{1,0:T(8,128)S(1)}, u32[]{:S(2)}, u32[]{:S(2)}) collective-permute-start(f32[232,128]{1,0:T(8,128)} %get-tuple-element.41), channel_id=1, source_target_pairs={{0,3},{1,2},{2,1},{3,0},{4,7},{5,6},{6,5},{7,4},{8,11},{9,10},{10,... | collective-permute-start | bytes 356360 | tf_op jit(solution)/shard_map/ppermute | solution.py:482
  8.2 2.2 %collective-permute-start.5 = (f32[232,128]{1,0:T(8,128)}, f32[232,128]{1,0:T(8,128)S(1)}, u32[]{:S(2)}, u32[]{:S(2)}) collective-permute-start(f32[232,128]{1,0:T(8,128)} %get-tuple-element.43), channel_id=1, source_target_pairs={{0,1},{1,0},{2,3},{3,2},{4,5},{5,4},{6,7},{7,6},{8,9},{9,8},{10,11... | collective-permute-start | bytes 356360 | tf_op jit(solution)/shard_map/ppermute | solution.py:482
  11.1 3.9 %shard_map.104 = (bf16[4,224,224]{2,1,0:T(8,128)(2,1)S(1)}, bf16[4,224,224]{2,1,0:T(8,128)(2,1)S(1)}, bf16[512,224]{1,0:T(8,128)(2,1)S(1)}, bf16[512,224]{1,0:T(...) custom-call(s32[9,220]{1,0:T(8,128)S(1)} %bitcast.20, ...), custom_call_target="tpu_custom_call" | custom-call | bytes 36736 | tf_op jit(solution)/shard_map/pallas_call | solution.py:466
  15.0 1.7 %collective-permute-done.1.far_ref = f32[880,128]{1,0:T(8,128)S(1)} collective-permute-done((f32[880,128]{1,0:T(8,128)}, f32[880,128]{1,0:T(8,128)S(1)}, u32[]{:S(2)}, u32[]{:S(2)}) %collective-permute-start.1) | collective-permute-done | bytes 450592 | tf_op jit(solution)/shard_map/ppermute | solution.py:490
  16.7 0.9 %shard_map.105 = (f32[232,128]{1,0:T(8,128)S(1)}, f32[232,128]{1,0:T(8,128)S(1)}, f32[232,128]{1,0:T(8,128)S(1)}, f32[232,128]{1,0:T(8,128)S(1)}) custom-call(f32[880,128]{1,0:T(8,128)S(1)} %bitcast.13, f32[880,128]{1,0:T(8,128)S(1)} %collective-permute-done.near_ref, f32[880,128]{1,0:T(8,128)S(1)} %collective-permute-done.1.far_ref), custom_call_target="tpu_custom_call" | custom-call | bytes 1351680 | tf_op jit(solution)/shard_map/pallas_call | solution.py:466
  17.6 2.4 %collective-permute-start.7 = (f32[232,128]{1,0:T(8,128)S(1)}, f32[232,128]{1,0:T(8,128)S(1)}, u32[]{:S(2)}, u32[]{:S(2)}) collective-permute-start(f32[232,128]{1,0:T(8,128)S(1)} %get-tuple-element.46), channel_id=1, source_target_pairs={{0,2},{1,3},{2,0},{3,1},{4,6},{5,7},{6,4},{7,5},{8,10},{9,11},{10,... | collective-permute-start | bytes 356360 | tf_op jit(solution)/shard_map/ppermute | solution.py:482
  20.3 3.8 %collective-permute-start.10 = (f32[880,128]{1,0:T(8,128)S(1)}, f32[880,128]{1,0:T(8,128)S(1)}, u32[]{:S(2)}, u32[]{:S(2)}) collective-permute-start(f32[880,128]{1,0:T(8,128)S(1)} %bitcast.14), channel_id=1, source_target_pairs={{4,8},{8,4},{12,16},{16,12},{20,24},{24,20},{5,9},{9,5},{13,17},{1... | collective-permute-start | bytes 1351688 | tf_op jit(solution)/shard_map/ppermute | solution.py:490
  24.6 0.8 %shard_map.107.refs_2_ = f32[224,640]{1,0:T(8,128)S(1)} custom-call(f32[232,128]{1,0:T(8,128)S(1)} %copy-done.2, f32[232,128]{1,0:T(8,128)S(1)} %collective-permute-done.4.refs_1_, f32[232,128]{1,0:T(8,128)S(1)} %collective-permute-done.5.refs_2_, f32[232,128]{1,0:T(8,128)S(1)} %collective-permute-done.6.refs_3_, f32[232,128]{1,0:T(8,128)S(1)} %get-tuple-element.45.refs_4_, ...), custom_call_target="tpu_custom_call" | custom-call | bytes 1518080 | tf_op jit(solution)/shard_map/pallas_call | solution.py:466
  25.8 4.2 %collective-permute-done.3.refs_1_ = f32[232,128]{1,0:T(8,128)S(1)} collective-permute-done((f32[232,128]{1,0:T(8,128)S(1)}, f32[232,128]{1,0:T(8,128)S(1)}, u32[]{:S(2)}, u32[]{:S(2)}) %collective-permute-start.3) | collective-permute-done | bytes 118816 | tf_op jit(solution)/shard_map/ppermute | solution.py:482
  29.9 0.8 %shard_map.108 = (f32[224,512]{1,0:T(8,128)S(1)}, f32[224,128]{1,0:T(8,128)S(1)}, f32[224,128]{1,0:T(8,128)S(1)}, f32[224,128]{1,0:T(8,128)S(1)}, f32[224,128]{1,0:T(8,128)S(1)}, /*index=5*/f32[224,128]{1,0:T(8,128)S(1)}) custom-call(f32[232,128]{1,0:T(8,128)S(1)} %collective-permute-done.2.refs_0_, f32[232,128]{1,0:T(8,128)S(1)} %collective-permute-done.3.refs_1_, ...), custom_call_target="tpu_custom_call" | custom-call | bytes 1616384 | tf_op jit(solution)/shard_map/pallas_call | solution.py:466
  31.2 3.3 %collective-permute-start.14 = (f32[224,512]{1,0:T(8,128)S(1)}, f32[224,512]{1,0:T(8,128)S(1)}, u32[]{:S(2)}, u32[]{:S(2)}) collective-permute-start(f32[224,512]{1,0:T(8,128)S(1)} %get-tuple-element.56.refs_0_), channel_id=1, source_target_pairs={{4,8},{8,4},{12,16},{16,12},{20,24},{24,20},{5,9},{9,5},{13,17},{1... | collective-permute-start | bytes 1376264 | tf_op jit(solution)/shard_map/ppermute | solution.py:490
  35.6 4.2 %collective-permute-start.11 = (f32[224,128]{1,0:T(8,128)S(1)}, f32[224,128]{1,0:T(8,128)S(1)}, u32[]{:S(2)}, u32[]{:S(2)}) collective-permute-start(f32[224,128]{1,0:T(8,128)S(1)} %get-tuple-element.54), channel_id=1, source_target_pairs={{0,2},{1,3},{2,0},{3,1},{4,6},{5,7},{6,4},{7,5},{8,10},{9,11},{10,... | collective-permute-start | bytes 344072 | tf_op jit(solution)/shard_map/ppermute | solution.py:482
  39.7 1.5 %collective-permute-start.8 = (f32[224,128]{1,0:T(8,128)S(1)}, f32[224,128]{1,0:T(8,128)S(1)}, u32[]{:S(2)}, u32[]{:S(2)}) collective-permute-start(f32[224,128]{1,0:T(8,128)S(1)} %get-tuple-element.51), channel_id=1, source_target_pairs={{0,1},{1,2},{2,3},{3,0},{4,5},{5,6},{6,7},{7,4},{8,9},{9,10},{10,1... | collective-permute-start | bytes 344072 | tf_op jit(solution)/shard_map/ppermute | solution.py:482
  41.2 1.5 %shard_map.111 = (f32[512,512]{1,0:T(8,128)S(1)}, f32[512,512]{1,0:T(8,128)S(1)}) custom-call(f32[224,512]{1,0:T(8,128)S(1)} %get-tuple-element.56.refs_0_, f32[224,128]{1,0:T(8,128)S(1)} %get-tuple-element.57.refs_1_, s32[1,640]{1,0:T(1,128)S(1)} %get-tuple-element.49.refs_8_.refs_5_.refs_2_, bf16[512,224]{1,0:T(8,128)(2,1)S(1)} %get-tuple-element.58.refs_3_.bh_ref, ...), custom_call_target="tpu_custom_call" | custom-call | bytes 1165824 | tf_op jit(solution)/shard_map/pallas_call | solution.py:466
  42.7 2.7 %collective-permute-done.14.far_ref = f32[224,512]{1,0:T(8,128)S(1)} collective-permute-done((f32[224,512]{1,0:T(8,128)S(1)}, f32[224,512]{1,0:T(8,128)S(1)}, u32[]{:S(2)}, u32[]{:S(2)}) %collective-permute-start.14) | collective-permute-done | bytes 458784 | tf_op jit(solution)/shard_map/ppermute | solution.py:490
  45.4 1.1 %shard_map.112 = (f32[224,128]{1,0:T(8,128)S(1)}, f32[224,128]{1,0:T(8,128)S(1)}, f32[224,128]{1,0:T(8,128)S(1)}, f32[224,128]{1,0:T(8,128)S(1)}) custom-call(f32[224,512]{1,0:T(8,128)S(1)} %collective-permute-done.13.near_ref, f32[224,512]{1,0:T(8,128)S(1)} %collective-permute-done.14.far_ref, f32[512,512]{1,0:T(8,128)S(1)} %get-tuple-element.61.part_ref, ...), custom_call_target="tpu_custom_call" | custom-call | bytes 3940352 | tf_op jit(solution)/shard_map/pallas_call | solution.py:466
  46.6 2.5 %collective-permute-start.15 = (f32[224,128]{1,0:T(8,128)S(1)}, f32[224,128]{1,0:T(8,128)S(1)}, u32[]{:S(2)}, u32[]{:S(2)}) collective-permute-start(f32[224,128]{1,0:T(8,128)S(1)} %get-tuple-element.66), channel_id=1, source_target_pairs={{0,2},{1,3},{2,0},{3,1},{4,6},{5,7},{6,4},{7,5},{8,10},{9,11},{10,... | collective-permute-start | bytes 344072 | tf_op jit(solution)/shard_map/ppermute | solution.py:482
  49.1 1.5 %collective-permute-start.17 = (f32[224,128]{1,0:T(8,128)S(1)}, f32[224,128]{1,0:T(8,128)S(1)}, u32[]{:S(2)}, u32[]{:S(2)}) collective-permute-start(f32[224,128]{1,0:T(8,128)S(1)} %get-tuple-element.68), channel_id=1, source_target_pairs={{0,3},{1,0},{2,1},{3,2},{4,7},{5,4},{6,5},{7,6},{8,11},{9,8},{10,9... | collective-permute-start | bytes 344072 | tf_op jit(solution)/shard_map/ppermute | solution.py:482
  50.6 0.8 %shard_map.110 = f32[880,128]{1,0:T(8,128)} custom-call(f32[224,128]{1,0:T(8,128)S(1)} %get-tuple-element.50.refs_0_, f32[224,128]{1,0:T(8,128)S(1)} %collective-permute-done.8.refs_1_, f32[224,128]{1,0:T(8,128)S(1)} %collective-permute-done.11.refs_2_, f32[224,128]{1,0:T(8,128)S(1)} %collective-permute-done.12.refs_3_), custom_call_target="tpu_custom_call" | custom-call | bytes 458752 | tf_op jit(solution)/shard_map/pallas_call | solution.py:466
  51.4 1.8 %collective-permute-done.15.refs_1_ = f32[224,128]{1,0:T(8,128)S(1)} collective-permute-done((f32[224,128]{1,0:T(8,128)S(1)}, f32[224,128]{1,0:T(8,128)S(1)}, u32[]{:S(2)}, u32[]{:S(2)}) %collective-permute-start.15) | collective-permute-done | bytes 114720 | tf_op jit(solution)/shard_map/ppermute | solution.py:482
  53.2 3.1 %collective-permute-done.16.refs_2_ = f32[224,128]{1,0:T(8,128)S(1)} collective-permute-done((f32[224,128]{1,0:T(8,128)S(1)}, f32[224,128]{1,0:T(8,128)S(1)}, u32[]{:S(2)}, u32[]{:S(2)}) %collective-permute-start.16) | collective-permute-done | bytes 114720 | tf_op jit(solution)/shard_map/ppermute | solution.py:482
  57.0 0.8 %shard_map.113 = f32[880,128]{1,0:T(8,128)} custom-call(f32[224,128]{1,0:T(8,128)S(1)} %get-tuple-element.65.refs_0_, f32[224,128]{1,0:T(8,128)S(1)} %collective-permute-done.15.refs_1_, f32[224,128]{1,0:T(8,128)S(1)} %collective-permute-done.16.refs_2_, f32[224,128]{1,0:T(8,128)S(1)} %collective-permute-done.17.refs_3_, f32[896,128]{1,0:T(8,128)S(1)} %shard_map.109.refs_4_), custom_call_target="tpu_custom_call" | custom-call | bytes 917504 | tf_op jit(solution)/shard_map/pallas_call | solution.py:466
  (40 shorter events, 4.8 us)
Async XLA Ops:
  0.6 14.4 %collective-permute-start = (f32[880,128]{1,0:T(8,128)}, f32[880,128]{1,0:T(8,128)S(1)}, u32[]{:S(2)}, u32[]{:S(2)}) collective-permute-start(f32[880,128]{1,0:T(8,128)} %bitcast.10), channel_id=1, source_target_pairs={{0,4},{4,0},{8,12},{12,8},{16,20},{20,16},{24,28},{28,24},{1,5},{5... | collective-permute-start | bytes 1351688 | tf_op jit(solution)/shard_map/ppermute | solution.py:491
  1.4 15.3 %collective-permute-start.1 = (f32[880,128]{1,0:T(8,128)}, f32[880,128]{1,0:T(8,128)S(1)}, u32[]{:S(2)}, u32[]{:S(2)}) collective-permute-start(f32[880,128]{1,0:T(8,128)} %bitcast.11), channel_id=1, source_target_pairs={{4,8},{8,4},{12,16},{16,12},{20,24},{24,20},{5,9},{9,5},{13,17},{1... | collective-permute-start | bytes 1351688 | tf_op jit(solution)/shard_map/ppermute | solution.py:490
  4.4 6.0 %copy-start.4 = (s32[512,9]{0,1:T(8,128)S(1)}, s32[512,9]{0,1:T(8,128)}, u32[]{:S(2)}) copy-start(s32[512,9]{0,1:T(8,128)} %param.16) | copy-start | bytes 55300
  4.4 6.0 %copy-start.5 = (s32[220,9]{0,1:T(8,128)S(1)}, s32[220,9]{0,1:T(8,128)}, u32[]{:S(2)}) copy-start(s32[220,9]{0,1:T(8,128)} %param.15) | copy-start | bytes 23764
  4.4 12.3 %copy-start = (f32[55,1,2048]{2,1,0:T(1,128)S(1)}, f32[55,1,2048]{2,1,0:T(1,128)}, u32[]{:S(2)}) copy-start(f32[55,1,2048]{2,1,0:T(1,128)} %param.9) | copy-start | bytes 1351684
  6.8 13.1 %collective-permute-start.4 = (f32[232,128]{1,0:T(8,128)}, f32[232,128]{1,0:T(8,128)S(1)}, u32[]{:S(2)}, u32[]{:S(2)}) collective-permute-start(f32[232,128]{1,0:T(8,128)} %get-tuple-element.41), channel_id=1, source_target_pairs={{0,3},{1,2},{2,1},{3,0},{4,7},{5,6},{6,5},{7,4},{8,11},{9,10},{10,... | collective-permute-start | bytes 356360 | tf_op jit(solution)/shard_map/ppermute | solution.py:482
  8.2 12.1 %collective-permute-start.5 = (f32[232,128]{1,0:T(8,128)}, f32[232,128]{1,0:T(8,128)S(1)}, u32[]{:S(2)}, u32[]{:S(2)}) collective-permute-start(f32[232,128]{1,0:T(8,128)} %get-tuple-element.43), channel_id=1, source_target_pairs={{0,1},{1,0},{2,3},{3,2},{4,5},{5,4},{6,7},{7,6},{8,9},{9,8},{10,11... | collective-permute-start | bytes 356360 | tf_op jit(solution)/shard_map/ppermute | solution.py:482
  10.4 13.8 %collective-permute-start.6 = (f32[232,128]{1,0:T(8,128)}, f32[232,128]{1,0:T(8,128)S(1)}, u32[]{:S(2)}, u32[]{:S(2)}) collective-permute-start(f32[232,128]{1,0:T(8,128)} %get-tuple-element.44), channel_id=1, source_target_pairs={{0,2},{1,3},{2,0},{3,1},{4,6},{5,7},{6,4},{7,5},{8,10},{9,11},{10,... | collective-permute-start | bytes 356360 | tf_op jit(solution)/shard_map/ppermute | solution.py:482
  15.0 5.3 %copy-start.1 = (f32[55,1,2048]{2,1,0:T(1,128)S(1)}, f32[55,1,2048]{2,1,0:T(1,128)}, u32[]{:S(2)}) copy-start(f32[55,1,2048]{2,1,0:T(1,128)} %param.11) | copy-start | bytes 1351684
  15.0 9.6 %copy-start.2 = (f32[232,128]{1,0:T(8,128)S(1)}, f32[232,128]{1,0:T(8,128)}, u32[]{:S(2)}) copy-start(f32[232,128]{1,0:T(8,128)} %get-tuple-element.40.refs_0_) | copy-start | bytes 356356
  17.6 7.0 %collective-permute-start.7 = (f32[232,128]{1,0:T(8,128)S(1)}, f32[232,128]{1,0:T(8,128)S(1)}, u32[]{:S(2)}, u32[]{:S(2)}) collective-permute-start(f32[232,128]{1,0:T(8,128)S(1)} %get-tuple-element.46), channel_id=1, source_target_pairs={{0,2},{1,3},{2,0},{3,1},{4,6},{5,7},{6,4},{7,5},{8,10},{9,11},{10,... | collective-permute-start | bytes 356360 | tf_op jit(solution)/shard_map/ppermute | solution.py:482
  20.0 5.8 %collective-permute-start.2 = (f32[232,128]{1,0:T(8,128)S(1)}, f32[232,128]{1,0:T(8,128)S(1)}, u32[]{:S(2)}, u32[]{:S(2)}) collective-permute-start(f32[232,128]{1,0:T(8,128)S(1)} %get-tuple-element.38), channel_id=1, source_target_pairs={{0,1},{1,0},{2,3},{3,2},{4,5},{5,4},{6,7},{7,6},{8,9},{9,8},{10,11... | collective-permute-start | bytes 356360 | tf_op jit(solution)/shard_map/ppermute | solution.py:482
  20.0 10.0 %collective-permute-start.3 = (f32[232,128]{1,0:T(8,128)S(1)}, f32[232,128]{1,0:T(8,128)S(1)}, u32[]{:S(2)}, u32[]{:S(2)}) collective-permute-start(f32[232,128]{1,0:T(8,128)S(1)} %get-tuple-element.39), channel_id=1, source_target_pairs={{0,3},{1,2},{2,1},{3,0},{4,7},{5,6},{6,5},{7,4},{8,11},{9,10},{10,... | collective-permute-start | bytes 356360 | tf_op jit(solution)/shard_map/ppermute | solution.py:482
  20.3 14.5 %collective-permute-start.10 = (f32[880,128]{1,0:T(8,128)S(1)}, f32[880,128]{1,0:T(8,128)S(1)}, u32[]{:S(2)}, u32[]{:S(2)}) collective-permute-start(f32[880,128]{1,0:T(8,128)S(1)} %bitcast.14), channel_id=1, source_target_pairs={{4,8},{8,4},{12,16},{16,12},{20,24},{24,20},{5,9},{9,5},{13,17},{1... | collective-permute-start | bytes 1351688 | tf_op jit(solution)/shard_map/ppermute | solution.py:490
  24.2 10.6 %collective-permute-start.9 = (f32[880,128]{1,0:T(8,128)S(1)}, f32[880,128]{1,0:T(8,128)S(1)}, u32[]{:S(2)}, u32[]{:S(2)}) collective-permute-start(f32[880,128]{1,0:T(8,128)S(1)} %bitcast.15), channel_id=1, source_target_pairs={{0,4},{4,0},{8,12},{12,8},{16,20},{20,16},{24,28},{28,24},{1,5},{5... | collective-permute-start | bytes 1351688 | tf_op jit(solution)/shard_map/ppermute | solution.py:491
  30.7 12.0 %collective-permute-start.13 = (f32[224,512]{1,0:T(8,128)S(1)}, f32[224,512]{1,0:T(8,128)S(1)}, u32[]{:S(2)}, u32[]{:S(2)}) collective-permute-start(f32[224,512]{1,0:T(8,128)S(1)} %get-tuple-element.56.refs_0_), channel_id=1, source_target_pairs={{0,4},{4,0},{8,12},{12,8},{16,20},{20,16},{24,28},{28,24},{1,5},{5... | collective-permute-start | bytes 1376264 | tf_op jit(solution)/shard_map/ppermute | solution.py:491
  31.2 14.2 %collective-permute-start.14 = (f32[224,512]{1,0:T(8,128)S(1)}, f32[224,512]{1,0:T(8,128)S(1)}, u32[]{:S(2)}, u32[]{:S(2)}) collective-permute-start(f32[224,512]{1,0:T(8,128)S(1)} %get-tuple-element.56.refs_0_), channel_id=1, source_target_pairs={{4,8},{8,4},{12,16},{16,12},{20,24},{24,20},{5,9},{9,5},{13,17},{1... | collective-permute-start | bytes 1376264 | tf_op jit(solution)/shard_map/ppermute | solution.py:490
  35.6 13.6 %collective-permute-start.11 = (f32[224,128]{1,0:T(8,128)S(1)}, f32[224,128]{1,0:T(8,128)S(1)}, u32[]{:S(2)}, u32[]{:S(2)}) collective-permute-start(f32[224,128]{1,0:T(8,128)S(1)} %get-tuple-element.54), channel_id=1, source_target_pairs={{0,2},{1,3},{2,0},{3,1},{4,6},{5,7},{6,4},{7,5},{8,10},{9,11},{10,... | collective-permute-start | bytes 344072 | tf_op jit(solution)/shard_map/ppermute | solution.py:482
  39.7 10.8 %collective-permute-start.12 = (f32[224,128]{1,0:T(8,128)S(1)}, f32[224,128]{1,0:T(8,128)S(1)}, u32[]{:S(2)}, u32[]{:S(2)}) collective-permute-start(f32[224,128]{1,0:T(8,128)S(1)} %get-tuple-element.55), channel_id=1, source_target_pairs={{0,3},{1,0},{2,1},{3,2},{4,7},{5,4},{6,5},{7,6},{8,11},{9,8},{10,9... | collective-permute-start | bytes 344072 | tf_op jit(solution)/shard_map/ppermute | solution.py:482
  39.7 10.8 %collective-permute-start.8 = (f32[224,128]{1,0:T(8,128)S(1)}, f32[224,128]{1,0:T(8,128)S(1)}, u32[]{:S(2)}, u32[]{:S(2)}) collective-permute-start(f32[224,128]{1,0:T(8,128)S(1)} %get-tuple-element.51), channel_id=1, source_target_pairs={{0,1},{1,2},{2,3},{3,0},{4,5},{5,6},{6,7},{7,4},{8,9},{9,10},{10,1... | collective-permute-start | bytes 344072 | tf_op jit(solution)/shard_map/ppermute | solution.py:482
  41.2 4.2 %copy-start.3 = (f32[1,2048]{1,0:T(1,128)S(1)}, f32[1,2048]{1,0:T(1,128)}, u32[]{:S(2)}) copy-start(f32[1,2048]{1,0:T(1,128)} %param.12) | copy-start | bytes 24580
  46.6 6.6 %collective-permute-start.15 = (f32[224,128]{1,0:T(8,128)S(1)}, f32[224,128]{1,0:T(8,128)S(1)}, u32[]{:S(2)}, u32[]{:S(2)}) collective-permute-start(f32[224,128]{1,0:T(8,128)S(1)} %get-tuple-element.66), channel_id=1, source_target_pairs={{0,2},{1,3},{2,0},{3,1},{4,6},{5,7},{6,4},{7,5},{8,10},{9,11},{10,... | collective-permute-start | bytes 344072 | tf_op jit(solution)/shard_map/ppermute | solution.py:482
  49.1 7.2 %collective-permute-start.16 = (f32[224,128]{1,0:T(8,128)S(1)}, f32[224,128]{1,0:T(8,128)S(1)}, u32[]{:S(2)}, u32[]{:S(2)}) collective-permute-start(f32[224,128]{1,0:T(8,128)S(1)} %get-tuple-element.67), channel_id=1, source_target_pairs={{0,1},{1,2},{2,3},{3,0},{4,5},{5,6},{6,7},{7,4},{8,9},{9,10},{10,1... | collective-permute-start | bytes 344072 | tf_op jit(solution)/shard_map/ppermute | solution.py:482
  49.1 7.9 %collective-permute-start.17 = (f32[224,128]{1,0:T(8,128)S(1)}, f32[224,128]{1,0:T(8,128)S(1)}, u32[]{:S(2)}, u32[]{:S(2)}) collective-permute-start(f32[224,128]{1,0:T(8,128)S(1)} %get-tuple-element.68), channel_id=1, source_target_pairs={{0,3},{1,0},{2,1},{3,2},{4,7},{5,4},{6,5},{7,6},{8,11},{9,8},{10,9... | collective-permute-start | bytes 344072 | tf_op jit(solution)/shard_map/ppermute | solution.py:482
  (3 other events, 5.0 us)

commit v10 on v8

--- a/solution.py
+++ b/solution.py
@@ -333,7 +333,7 @@
 
 def relax_kernel(parts, padded, per, nreg, count, *refs):
     r_refs = refs[: parts - count]
-    most_ref, ah_ref, al_ref, zones_ref, rel_ref, rim_ref, *outs, all_ref = refs[parts - count :]
+    most_ref, ah_ref, al_ref, zones_ref, rel_ref, rim_ref, *outs = refs[parts - count :]
     me = lax.axis_index("modes")
     width = per * LANES
     zones = zones_ref[...]
@@ -345,11 +345,10 @@
     relaxed = most_ref[...] - (0.8 / 6.0) * applied
     rel_ref[...] = relaxed[:, :width]
     rim_ref[...] = relaxed[:, width:]
-    all_ref[...] = relaxed[:, :width]
     for k, out in enumerate(outs):
         at = pl.multiple_of(target_of(B_ROUTE, me, k, parts) * padded, SUB)
         for s in range(per):
-            out[s * padded : (s + 1) * padded, :] = all_ref[
+            out[s * padded : (s + 1) * padded, :] = rel_ref[
                 pl.ds(at, padded), s * LANES : (s + 1) * LANES
             ]
 
@@ -583,7 +582,6 @@
         [struct(rows, per * LANES), struct(rows, LANES)]
         + [struct(per * padded, LANES)] * parts,
         [*rough[count:], most, a_high, a_low, zones],
-        [pltpu.VMEM((rows, per * LANES), F32)],
     )
     relaxed = [relaxed]
     beside = [halo(x) for x in relaxed]

time: 57.9 us -> 57.9 us (level)
  no operation moved by 1% of the time
where the time goes in v10:
time: 57.9 us; the launch traced here: 57.5 us
  starting transfers between devices  27.7 us (48%)
  waiting for transfers between devices  14.6 us (25%)
  Pallas kernels  13.7 us (24%)
  between operations  0.82 us (1%)
  local copies, waits for them, and re-layouts  0.71 us (1%)
    ppermute x12, starting transfers between devices, exchange(): received[k] = lax.ppermute(chunks[k], 'modes', pairs)  16.3 us
    pallas_call x10, Pallas kernels, call(): pl.pallas_call(kernel, out_shape=out_shape, in_specs=specs, out_specs=[wh...  13.7 us
    ppermute x3, starting transfers between devices, halo(): far = lax.ppermute(x, 'space', far)  10.2 us
    ppermute x12, waiting for transfers between devices, exchange(): received[k] = lax.ppermute(chunks[k], 'modes', pairs)  9.89 us
    ppermute x3, waiting for transfers between devices, halo(): far = lax.ppermute(x, 'space', far)  4.66 us
    ppermute x3, starting transfers between devices, halo(): return (lax.ppermute(x, 'space', near), far)  1.26 us
  transfers between devices with their start and end apart: 18, of which 9 were waited for; matrix products, arithmetic and copies ran while one was open for 0% of the time, Pallas kernels for 22%

profile of v10, /device:TPU:11, one launch (start us, length us, event | category | flops | bytes accessed | tf_op | source)
XLA Modules:
  0.0 57.5 jit_solution(14743553083076122300)
XLA Ops:
  1.4 3.0 %collective-permute-start.1 = (f32[880,128]{1,0:T(8,128)}, f32[880,128]{1,0:T(8,128)S(1)}, u32[]{:S(2)}, u32[]{:S(2)}) collective-permute-start(f32[880,128]{1,0:T(8,128)} %bitcast.11), channel_id=1, source_target_pairs={{4,8},{8,4},{12,16},{16,12},{20,24},{24,20},{5,9},{9,5},{13,17},{1... | collective-permute-start | bytes 1351688 | tf_op jit(solution)/shard_map/ppermute | solution.py:489
  4.4 2.4 %shard_map.106 = (f32[232,128]{1,0:T(8,128)}, f32[232,128]{1,0:T(8,128)}, f32[232,128]{1,0:T(8,128)}, f32[232,128]{1,0:T(8,128)}) custom-call(f32[880,128]{1,0:T(8,128)} %bitcast.12, f32[880,128]{1,0:T(8,128)} %bitcast.23, f32[16,128]{1,0:T(8,128)} %bitcast.17), custom_call_target="tpu_custom_call" | custom-call | bytes 909312 | tf_op jit(solution)/shard_map/pallas_call | solution.py:465
  6.8 1.4 %collective-permute-start.3 = (f32[232,128]{1,0:T(8,128)}, f32[232,128]{1,0:T(8,128)S(1)}, u32[]{:S(2)}, u32[]{:S(2)}) collective-permute-start(f32[232,128]{1,0:T(8,128)} %get-tuple-element.40), channel_id=1, source_target_pairs={{0,3},{1,2},{2,1},{3,0},{4,7},{5,6},{6,5},{7,4},{8,11},{9,10},{10,... | collective-permute-start | bytes 356360 | tf_op jit(solution)/shard_map/ppermute | solution.py:481
  8.2 2.2 %collective-permute-start.4 = (f32[232,128]{1,0:T(8,128)}, f32[232,128]{1,0:T(8,128)S(1)}, u32[]{:S(2)}, u32[]{:S(2)}) collective-permute-start(f32[232,128]{1,0:T(8,128)} %get-tuple-element.42), channel_id=1, source_target_pairs={{0,1},{1,0},{2,3},{3,2},{4,5},{5,4},{6,7},{7,6},{8,9},{9,8},{10,11... | collective-permute-start | bytes 356360 | tf_op jit(solution)/shard_map/ppermute | solution.py:481
  11.1 3.9 %shard_map.104 = (bf16[4,224,224]{2,1,0:T(8,128)(2,1)S(1)}, bf16[4,224,224]{2,1,0:T(8,128)(2,1)S(1)}, bf16[512,224]{1,0:T(8,128)(2,1)S(1)}, bf16[512,224]{1,0:T(...) custom-call(s32[9,220]{1,0:T(8,128)S(1)} %bitcast.20, ...), custom_call_target="tpu_custom_call" | custom-call | bytes 36736 | tf_op jit(solution)/shard_map/pallas_call | solution.py:465
  15.0 1.7 %collective-permute-done.1.far_ref = f32[880,128]{1,0:T(8,128)S(1)} collective-permute-done((f32[880,128]{1,0:T(8,128)}, f32[880,128]{1,0:T(8,128)S(1)}, u32[]{:S(2)}, u32[]{:S(2)}) %collective-permute-start.1) | collective-permute-done | bytes 450592 | tf_op jit(solution)/shard_map/ppermute | solution.py:489
  16.7 0.9 %shard_map.105 = (f32[232,128]{1,0:T(8,128)S(1)}, f32[232,128]{1,0:T(8,128)S(1)}, f32[232,128]{1,0:T(8,128)S(1)}, f32[232,128]{1,0:T(8,128)S(1)}) custom-call(f32[880,128]{1,0:T(8,128)S(1)} %bitcast.13, f32[880,128]{1,0:T(8,128)S(1)} %collective-permute-done.near_ref, f32[880,128]{1,0:T(8,128)S(1)} %collective-permute-done.1.far_ref), custom_call_target="tpu_custom_call" | custom-call | bytes 1351680 | tf_op jit(solution)/shard_map/pallas_call | solution.py:465
  17.6 2.4 %collective-permute-start.6 = (f32[232,128]{1,0:T(8,128)S(1)}, f32[232,128]{1,0:T(8,128)S(1)}, u32[]{:S(2)}, u32[]{:S(2)}) collective-permute-start(f32[232,128]{1,0:T(8,128)S(1)} %get-tuple-element.45), channel_id=1, source_target_pairs={{0,2},{1,3},{2,0},{3,1},{4,6},{5,7},{6,4},{7,5},{8,10},{9,11},{10,... | collective-permute-start | bytes 356360 | tf_op jit(solution)/shard_map/ppermute | solution.py:481
  20.3 3.8 %collective-permute-start.10 = (f32[880,128]{1,0:T(8,128)S(1)}, f32[880,128]{1,0:T(8,128)S(1)}, u32[]{:S(2)}, u32[]{:S(2)}) collective-permute-start(f32[880,128]{1,0:T(8,128)S(1)} %bitcast.14), channel_id=1, source_target_pairs={{4,8},{8,4},{12,16},{16,12},{20,24},{24,20},{5,9},{9,5},{13,17},{1... | collective-permute-start | bytes 1351688 | tf_op jit(solution)/shard_map/ppermute | solution.py:489
  24.6 1.2 %collective-permute-done.7.refs_6_ = f32[232,128]{1,0:T(8,128)S(1)} collective-permute-done((f32[232,128]{1,0:T(8,128)S(1)}, f32[232,128]{1,0:T(8,128)S(1)}, u32[]{:S(2)}, u32[]{:S(2)}) %collective-permute-start.7) | collective-permute-done | bytes 118816 | tf_op jit(solution)/shard_map/ppermute | solution.py:481
  25.8 1.0 %shard_map.107.refs_1_ = f32[224,640]{1,0:T(8,128)S(1)} custom-call(f32[232,128]{1,0:T(8,128)S(1)} %copy-done.2, f32[232,128]{1,0:T(8,128)S(1)} %collective-permute-done.3.refs_1_, f32[232,128]{1,0:T(8,128)S(1)} %collective-permute-done.4.refs_2_, f32[232,128]{1,0:T(8,128)S(1)} %collective-permute-done.5.refs_3_, f32[232,128]{1,0:T(8,128)S(1)} %get-tuple-element.44.refs_4_, ...), custom_call_target="tpu_custom_call" | custom-call | bytes 1636864 | tf_op jit(solution)/shard_map/pallas_call | solution.py:465
  26.8 3.1 %collective-permute-done.2.refs_0_ = f32[232,128]{1,0:T(8,128)S(1)} collective-permute-done((f32[232,128]{1,0:T(8,128)S(1)}, f32[232,128]{1,0:T(8,128)S(1)}, u32[]{:S(2)}, u32[]{:S(2)}) %collective-permute-start.2) | collective-permute-done | bytes 118816 | tf_op jit(solution)/shard_map/ppermute | solution.py:481
  30.9 3.3 %collective-permute-start.14 = (f32[224,512]{1,0:T(8,128)S(1)}, f32[224,512]{1,0:T(8,128)S(1)}, u32[]{:S(2)}, u32[]{:S(2)}) collective-permute-start(f32[224,512]{1,0:T(8,128)S(1)} %get-tuple-element.56.refs_0_), channel_id=1, source_target_pairs={{4,8},{8,4},{12,16},{16,12},{20,24},{24,20},{5,9},{9,5},{13,17},{1... | collective-permute-start | bytes 1376264 | tf_op jit(solution)/shard_map/ppermute | solution.py:489
  35.5 4.2 %collective-permute-start.11 = (f32[224,128]{1,0:T(8,128)S(1)}, f32[224,128]{1,0:T(8,128)S(1)}, u32[]{:S(2)}, u32[]{:S(2)}) collective-permute-start(f32[224,128]{1,0:T(8,128)S(1)} %get-tuple-element.54), channel_id=1, source_target_pairs={{0,2},{1,3},{2,0},{3,1},{4,6},{5,7},{6,4},{7,5},{8,10},{9,11},{10,... | collective-permute-start | bytes 344072 | tf_op jit(solution)/shard_map/ppermute | solution.py:481
  39.7 1.5 %collective-permute-start.8 = (f32[224,128]{1,0:T(8,128)S(1)}, f32[224,128]{1,0:T(8,128)S(1)}, u32[]{:S(2)}, u32[]{:S(2)}) collective-permute-start(f32[224,128]{1,0:T(8,128)S(1)} %get-tuple-element.51), channel_id=1, source_target_pairs={{0,1},{1,2},{2,3},{3,0},{4,5},{5,6},{6,7},{7,4},{8,9},{9,10},{10,1... | collective-permute-start | bytes 344072 | tf_op jit(solution)/shard_map/ppermute | solution.py:481
  41.2 1.5 %shard_map.111 = (f32[512,512]{1,0:T(8,128)S(1)}, f32[512,512]{1,0:T(8,128)S(1)}) custom-call(f32[224,512]{1,0:T(8,128)S(1)} %get-tuple-element.56.refs_0_, f32[224,128]{1,0:T(8,128)S(1)} %get-tuple-element.57.refs_1_, s32[1,640]{1,0:T(1,128)S(1)} %get-tuple-element.49.refs_9_.refs_4_.refs_2_, bf16[512,224]{1,0:T(8,128)(2,1)S(1)} %get-tuple-element.58.refs_3_.bh_ref, ...), custom_call_target="tpu_custom_call" | custom-call | bytes 1165824 | tf_op jit(solution)/shard_map/pallas_call | solution.py:465
  42.7 2.4 %collective-permute-done.14.far_ref = f32[224,512]{1,0:T(8,128)S(1)} collective-permute-done((f32[224,512]{1,0:T(8,128)S(1)}, f32[224,512]{1,0:T(8,128)S(1)}, u32[]{:S(2)}, u32[]{:S(2)}) %collective-permute-start.14) | collective-permute-done | bytes 458784 | tf_op jit(solution)/shard_map/ppermute | solution.py:489
  45.1 1.2 %shard_map.112 = (f32[224,128]{1,0:T(8,128)S(1)}, f32[224,128]{1,0:T(8,128)S(1)}, f32[224,128]{1,0:T(8,128)S(1)}, f32[224,128]{1,0:T(8,128)S(1)}) custom-call(f32[224,512]{1,0:T(8,128)S(1)} %collective-permute-done.13.near_ref, f32[224,512]{1,0:T(8,128)S(1)} %collective-permute-done.14.far_ref, f32[512,512]{1,0:T(8,128)S(1)} %get-tuple-element.61.part_ref, ...), custom_call_target="tpu_custom_call" | custom-call | bytes 3940352 | tf_op jit(solution)/shard_map/pallas_call | solution.py:465
  46.3 2.8 %collective-permute-start.15 = (f32[224,128]{1,0:T(8,128)S(1)}, f32[224,128]{1,0:T(8,128)S(1)}, u32[]{:S(2)}, u32[]{:S(2)}) collective-permute-start(f32[224,128]{1,0:T(8,128)S(1)} %get-tuple-element.66), channel_id=1, source_target_pairs={{0,2},{1,3},{2,0},{3,1},{4,6},{5,7},{6,4},{7,5},{8,10},{9,11},{10,... | collective-permute-start | bytes 344072 | tf_op jit(solution)/shard_map/ppermute | solution.py:481
  49.1 1.5 %collective-permute-start.17 = (f32[224,128]{1,0:T(8,128)S(1)}, f32[224,128]{1,0:T(8,128)S(1)}, u32[]{:S(2)}, u32[]{:S(2)}) collective-permute-start(f32[224,128]{1,0:T(8,128)S(1)} %get-tuple-element.68), channel_id=1, source_target_pairs={{0,3},{1,0},{2,1},{3,2},{4,7},{5,4},{6,5},{7,6},{8,11},{9,8},{10,9... | collective-permute-start | bytes 344072 | tf_op jit(solution)/shard_map/ppermute | solution.py:481
  50.6 0.8 %shard_map.110 = f32[880,128]{1,0:T(8,128)} custom-call(f32[224,128]{1,0:T(8,128)S(1)} %get-tuple-element.50.refs_0_, f32[224,128]{1,0:T(8,128)S(1)} %collective-permute-done.8.refs_1_, f32[224,128]{1,0:T(8,128)S(1)} %collective-permute-done.11.refs_2_, f32[224,128]{1,0:T(8,128)S(1)} %collective-permute-done.12.refs_3_), custom_call_target="tpu_custom_call" | custom-call | bytes 458752 | tf_op jit(solution)/shard_map/pallas_call | solution.py:465
  51.4 2.1 %collective-permute-done.15.refs_1_ = f32[224,128]{1,0:T(8,128)S(1)} collective-permute-done((f32[224,128]{1,0:T(8,128)S(1)}, f32[224,128]{1,0:T(8,128)S(1)}, u32[]{:S(2)}, u32[]{:S(2)}) %collective-permute-start.15) | collective-permute-done | bytes 114720 | tf_op jit(solution)/shard_map/ppermute | solution.py:481
  53.5 2.8 %collective-permute-done.16.refs_2_ = f32[224,128]{1,0:T(8,128)S(1)} collective-permute-done((f32[224,128]{1,0:T(8,128)S(1)}, f32[224,128]{1,0:T(8,128)S(1)}, u32[]{:S(2)}, u32[]{:S(2)}) %collective-permute-start.16) | collective-permute-done | bytes 114720 | tf_op jit(solution)/shard_map/ppermute | solution.py:481
  56.7 0.8 %shard_map.113 = f32[880,128]{1,0:T(8,128)} custom-call(f32[224,128]{1,0:T(8,128)S(1)} %get-tuple-element.65.refs_0_, f32[224,128]{1,0:T(8,128)S(1)} %collective-permute-done.15.refs_1_, f32[224,128]{1,0:T(8,128)S(1)} %collective-permute-done.16.refs_2_, f32[224,128]{1,0:T(8,128)S(1)} %collective-permute-done.17.refs_3_, f32[896,128]{1,0:T(8,128)S(1)} %shard_map.109.refs_4_), custom_call_target="tpu_custom_call" | custom-call | bytes 917504 | tf_op jit(solution)/shard_map/pallas_call | solution.py:465
  (40 shorter events, 4.9 us)
Async XLA Ops:
  0.6 14.4 %collective-permute-start = (f32[880,128]{1,0:T(8,128)}, f32[880,128]{1,0:T(8,128)S(1)}, u32[]{:S(2)}, u32[]{:S(2)}) collective-permute-start(f32[880,128]{1,0:T(8,128)} %bitcast.10), channel_id=1, source_target_pairs={{0,4},{4,0},{8,12},{12,8},{16,20},{20,16},{24,28},{28,24},{1,5},{5... | collective-permute-start | bytes 1351688 | tf_op jit(solution)/shard_map/ppermute | solution.py:490
  1.4 15.3 %collective-permute-start.1 = (f32[880,128]{1,0:T(8,128)}, f32[880,128]{1,0:T(8,128)S(1)}, u32[]{:S(2)}, u32[]{:S(2)}) collective-permute-start(f32[880,128]{1,0:T(8,128)} %bitcast.11), channel_id=1, source_target_pairs={{4,8},{8,4},{12,16},{16,12},{20,24},{24,20},{5,9},{9,5},{13,17},{1... | collective-permute-start | bytes 1351688 | tf_op jit(solution)/shard_map/ppermute | solution.py:489
  4.4 6.0 %copy-start.4 = (s32[512,9]{0,1:T(8,128)S(1)}, s32[512,9]{0,1:T(8,128)}, u32[]{:S(2)}) copy-start(s32[512,9]{0,1:T(8,128)} %param.16) | copy-start | bytes 55300
  4.4 6.0 %copy-start.5 = (s32[220,9]{0,1:T(8,128)S(1)}, s32[220,9]{0,1:T(8,128)}, u32[]{:S(2)}) copy-start(s32[220,9]{0,1:T(8,128)} %param.15) | copy-start | bytes 23764
  4.4 12.3 %copy-start = (f32[55,1,2048]{2,1,0:T(1,128)S(1)}, f32[55,1,2048]{2,1,0:T(1,128)}, u32[]{:S(2)}) copy-start(f32[55,1,2048]{2,1,0:T(1,128)} %param.9) | copy-start | bytes 1351684
  6.8 13.1 %collective-permute-start.3 = (f32[232,128]{1,0:T(8,128)}, f32[232,128]{1,0:T(8,128)S(1)}, u32[]{:S(2)}, u32[]{:S(2)}) collective-permute-start(f32[232,128]{1,0:T(8,128)} %get-tuple-element.40), channel_id=1, source_target_pairs={{0,3},{1,2},{2,1},{3,0},{4,7},{5,6},{6,5},{7,4},{8,11},{9,10},{10,... | collective-permute-start | bytes 356360 | tf_op jit(solution)/shard_map/ppermute | solution.py:481
  8.2 12.1 %collective-permute-start.4 = (f32[232,128]{1,0:T(8,128)}, f32[232,128]{1,0:T(8,128)S(1)}, u32[]{:S(2)}, u32[]{:S(2)}) collective-permute-start(f32[232,128]{1,0:T(8,128)} %get-tuple-element.42), channel_id=1, source_target_pairs={{0,1},{1,0},{2,3},{3,2},{4,5},{5,4},{6,7},{7,6},{8,9},{9,8},{10,11... | collective-permute-start | bytes 356360 | tf_op jit(solution)/shard_map/ppermute | solution.py:481
  10.4 13.8 %collective-permute-start.5 = (f32[232,128]{1,0:T(8,128)}, f32[232,128]{1,0:T(8,128)S(1)}, u32[]{:S(2)}, u32[]{:S(2)}) collective-permute-start(f32[232,128]{1,0:T(8,128)} %get-tuple-element.43), channel_id=1, source_target_pairs={{0,2},{1,3},{2,0},{3,1},{4,6},{5,7},{6,4},{7,5},{8,10},{9,11},{10,... | collective-permute-start | bytes 356360 | tf_op jit(solution)/shard_map/ppermute | solution.py:481
  15.0 5.3 %copy-start.1 = (f32[55,1,2048]{2,1,0:T(1,128)S(1)}, f32[55,1,2048]{2,1,0:T(1,128)}, u32[]{:S(2)}) copy-start(f32[55,1,2048]{2,1,0:T(1,128)} %param.11) | copy-start | bytes 1351684
  15.0 10.8 %copy-start.2 = (f32[232,128]{1,0:T(8,128)S(1)}, f32[232,128]{1,0:T(8,128)}, u32[]{:S(2)}) copy-start(f32[232,128]{1,0:T(8,128)} %get-tuple-element.39.refs_0_) | copy-start | bytes 356356
  17.6 7.0 %collective-permute-start.6 = (f32[232,128]{1,0:T(8,128)S(1)}, f32[232,128]{1,0:T(8,128)S(1)}, u32[]{:S(2)}, u32[]{:S(2)}) collective-permute-start(f32[232,128]{1,0:T(8,128)S(1)} %get-tuple-element.45), channel_id=1, source_target_pairs={{0,2},{1,3},{2,0},{3,1},{4,6},{5,7},{6,4},{7,5},{8,10},{9,11},{10,... | collective-permute-start | bytes 356360 | tf_op jit(solution)/shard_map/ppermute | solution.py:481
  20.0 5.8 %collective-permute-start.7 = (f32[232,128]{1,0:T(8,128)S(1)}, f32[232,128]{1,0:T(8,128)S(1)}, u32[]{:S(2)}, u32[]{:S(2)}) collective-permute-start(f32[232,128]{1,0:T(8,128)S(1)} %get-tuple-element.46), channel_id=1, source_target_pairs={{0,1},{1,0},{2,3},{3,2},{4,5},{5,4},{6,7},{7,6},{8,9},{9,8},{10,11... | collective-permute-start | bytes 356360 | tf_op jit(solution)/shard_map/ppermute | solution.py:481
  20.0 10.0 %collective-permute-start.2 = (f32[232,128]{1,0:T(8,128)S(1)}, f32[232,128]{1,0:T(8,128)S(1)}, u32[]{:S(2)}, u32[]{:S(2)}) collective-permute-start(f32[232,128]{1,0:T(8,128)S(1)} %get-tuple-element.38), channel_id=1, source_target_pairs={{0,3},{1,2},{2,1},{3,0},{4,7},{5,6},{6,5},{7,4},{8,11},{9,10},{10,... | collective-permute-start | bytes 356360 | tf_op jit(solution)/shard_map/ppermute | solution.py:481
  20.3 14.5 %collective-permute-start.10 = (f32[880,128]{1,0:T(8,128)S(1)}, f32[880,128]{1,0:T(8,128)S(1)}, u32[]{:S(2)}, u32[]{:S(2)}) collective-permute-start(f32[880,128]{1,0:T(8,128)S(1)} %bitcast.14), channel_id=1, source_target_pairs={{4,8},{8,4},{12,16},{16,12},{20,24},{24,20},{5,9},{9,5},{13,17},{1... | collective-permute-start | bytes 1351688 | tf_op jit(solution)/shard_map/ppermute | solution.py:489
  24.2 10.6 %collective-permute-start.9 = (f32[880,128]{1,0:T(8,128)S(1)}, f32[880,128]{1,0:T(8,128)S(1)}, u32[]{:S(2)}, u32[]{:S(2)}) collective-permute-start(f32[880,128]{1,0:T(8,128)S(1)} %bitcast.15), channel_id=1, source_target_pairs={{0,4},{4,0},{8,12},{12,8},{16,20},{20,16},{24,28},{28,24},{1,5},{5... | collective-permute-start | bytes 1351688 | tf_op jit(solution)/shard_map/ppermute | solution.py:490
  30.4 12.2 %collective-permute-start.13 = (f32[224,512]{1,0:T(8,128)S(1)}, f32[224,512]{1,0:T(8,128)S(1)}, u32[]{:S(2)}, u32[]{:S(2)}) collective-permute-start(f32[224,512]{1,0:T(8,128)S(1)} %get-tuple-element.56.refs_0_), channel_id=1, source_target_pairs={{0,4},{4,0},{8,12},{12,8},{16,20},{20,16},{24,28},{28,24},{1,5},{5... | collective-permute-start | bytes 1376264 | tf_op jit(solution)/shard_map/ppermute | solution.py:490
  30.9 14.2 %collective-permute-start.14 = (f32[224,512]{1,0:T(8,128)S(1)}, f32[224,512]{1,0:T(8,128)S(1)}, u32[]{:S(2)}, u32[]{:S(2)}) collective-permute-start(f32[224,512]{1,0:T(8,128)S(1)} %get-tuple-element.56.refs_0_), channel_id=1, source_target_pairs={{4,8},{8,4},{12,16},{16,12},{20,24},{24,20},{5,9},{9,5},{13,17},{1... | collective-permute-start | bytes 1376264 | tf_op jit(solution)/shard_map/ppermute | solution.py:489
  35.5 13.6 %collective-permute-start.11 = (f32[224,128]{1,0:T(8,128)S(1)}, f32[224,128]{1,0:T(8,128)S(1)}, u32[]{:S(2)}, u32[]{:S(2)}) collective-permute-start(f32[224,128]{1,0:T(8,128)S(1)} %get-tuple-element.54), channel_id=1, source_target_pairs={{0,2},{1,3},{2,0},{3,1},{4,6},{5,7},{6,4},{7,5},{8,10},{9,11},{10,... | collective-permute-start | bytes 344072 | tf_op jit(solution)/shard_map/ppermute | solution.py:481
  39.7 10.9 %collective-permute-start.12 = (f32[224,128]{1,0:T(8,128)S(1)}, f32[224,128]{1,0:T(8,128)S(1)}, u32[]{:S(2)}, u32[]{:S(2)}) collective-permute-start(f32[224,128]{1,0:T(8,128)S(1)} %get-tuple-element.55), channel_id=1, source_target_pairs={{0,3},{1,0},{2,1},{3,2},{4,7},{5,4},{6,5},{7,6},{8,11},{9,8},{10,9... | collective-permute-start | bytes 344072 | tf_op jit(solution)/shard_map/ppermute | solution.py:481
  39.7 10.9 %collective-permute-start.8 = (f32[224,128]{1,0:T(8,128)S(1)}, f32[224,128]{1,0:T(8,128)S(1)}, u32[]{:S(2)}, u32[]{:S(2)}) collective-permute-start(f32[224,128]{1,0:T(8,128)S(1)} %get-tuple-element.51), channel_id=1, source_target_pairs={{0,1},{1,2},{2,3},{3,0},{4,5},{5,6},{6,7},{7,4},{8,9},{9,10},{10,1... | collective-permute-start | bytes 344072 | tf_op jit(solution)/shard_map/ppermute | solution.py:481
  41.2 3.9 %copy-start.3 = (f32[1,2048]{1,0:T(1,128)S(1)}, f32[1,2048]{1,0:T(1,128)}, u32[]{:S(2)}) copy-start(f32[1,2048]{1,0:T(1,128)} %param.12) | copy-start | bytes 24580
  46.3 7.2 %collective-permute-start.15 = (f32[224,128]{1,0:T(8,128)S(1)}, f32[224,128]{1,0:T(8,128)S(1)}, u32[]{:S(2)}, u32[]{:S(2)}) collective-permute-start(f32[224,128]{1,0:T(8,128)S(1)} %get-tuple-element.66), channel_id=1, source_target_pairs={{0,2},{1,3},{2,0},{3,1},{4,6},{5,7},{6,4},{7,5},{8,10},{9,11},{10,... | collective-permute-start | bytes 344072 | tf_op jit(solution)/shard_map/ppermute | solution.py:481
  49.1 7.2 %collective-permute-start.16 = (f32[224,128]{1,0:T(8,128)S(1)}, f32[224,128]{1,0:T(8,128)S(1)}, u32[]{:S(2)}, u32[]{:S(2)}) collective-permute-start(f32[224,128]{1,0:T(8,128)S(1)} %get-tuple-element.67), channel_id=1, source_target_pairs={{0,1},{1,2},{2,3},{3,0},{4,5},{5,6},{6,7},{7,4},{8,9},{9,10},{10,1... | collective-permute-start | bytes 344072 | tf_op jit(solution)/shard_map/ppermute | solution.py:481
  49.1 7.6 %collective-permute-start.17 = (f32[224,128]{1,0:T(8,128)S(1)}, f32[224,128]{1,0:T(8,128)S(1)}, u32[]{:S(2)}, u32[]{:S(2)}) collective-permute-start(f32[224,128]{1,0:T(8,128)S(1)} %get-tuple-element.68), channel_id=1, source_target_pairs={{0,3},{1,0},{2,1},{3,2},{4,7},{5,4},{6,5},{7,6},{8,11},{9,8},{10,9... | collective-permute-start | bytes 344072 | tf_op jit(solution)/shard_map/ppermute | solution.py:481
  (3 other events, 5.0 us)
